TPU v7x, 32 devices: a whole 2x2x4 slice. The times are simulated.
32 devices in a mesh: groups: 2 (over y), prow: 8 (over z, x), pcol: 2 (over core).
Axes of the slice: x: 2, y: 2, z: 4, core: 2. Of those that a mesh axis runs over, the one named last changes fastest.
Arguments:
- sigma_root: float32 [12800, 6400], P(('groups', 'prow'), 'pcol'), parts along dimension 0, may hold values from -0.2 to 2.2, as said below
- lower_one: bfloat16 [4, 6400, 512], P(('groups', 'pcol'), 'prow'), parts along dimension 0, may hold values from -0.109375 to 0.109375
- weights_one: float32 [4, 512, 512], P(('groups', 'pcol')), parts along dimension 0, may hold values from -0.2 to 1.4, as said below
- pattern_one: int32 [4, 25, 2], P(('groups', 'pcol')), parts along dimension 0, may hold values 0 or 1
- lower_root: bfloat16 [8, 6400, 256], P(('groups', 'pcol'), 'prow'), parts along dimension 0, may hold values from -0.109375 to 0.109375
- lower_sep: bfloat16 [8, 512, 256], P(('groups', 'pcol'), 'prow'), parts along dimension 0, may hold values from -0.109375 to 0.109375
- weights_two: float32 [8, 256, 256], P(('groups', 'pcol')), parts along dimension 0, may hold values from -0.2 to 1.4, as said below
- pattern_two: int32 [8, 27, 1], P(('groups', 'pcol')), parts along dimension 0, may hold values 0 or 1
Outputs:
- sigma_one_root: float32 [4, 6400, 512], P(('groups', 'pcol'), 'prow'), parts along dimension 0
- sigma_one_diag: float32 [4, 512, 512], P(('groups', 'pcol'), 'prow'), parts along dimension 0
- sigma_two_root: float32 [8, 6400, 256], P(('groups', 'pcol'), 'prow'), parts along dimension 0
- sigma_two_sep: float32 [8, 512, 256], P(('groups', 'pcol'), 'prow'), parts along dimension 0
- sigma_two_diag: float32 [8, 256, 256], P(('groups', 'pcol'), 'prow'), parts along dimension 0
There are 2 independent parts, one for each index of `groups`. A program takes and returns all parts, laid end to end along the dimension named above; each array names one. Nothing has to cross between parts.
Inputs may be any that keep to these rules, and one draw needn't show every extreme that they name: `sigma_root`: symmetric. `weights_one`: lower triangular with diagonal entries of 0.6 to 1.4. `weights_two`: lower triangular with diagonal entries of 0.6 to 1.4.
All inputs are finite; a program needn't handle non-finite values. No bound on the sum of `pattern_one` or of `pattern_two` on one device may be relied on, other than what follows from the above.
Results may differ from a plain program's by a relative error of at most 0.0033.
Values may be sent and summed in bfloat16 or wider, within the bound.
A program may use at most 128 MiB of HBM per device.

v0:
```python
import jax
import jax.numpy as jnp
from jax import lax
from jax.sharding import PartitionSpec as P

B = 256


HIGHEST = lax.Precision.HIGHEST


def expand_pattern(pattern, first_row, row_count, block_width):
    block_ids = (first_row + lax.iota(jnp.int32, row_count)) // block_width
    selector = (block_ids[:, None] == lax.iota(jnp.int32, pattern.shape[1])[None, :]).astype(
        jnp.float32
    )
    spread = jnp.einsum("rk,nkc->nrc", selector, pattern.astype(jnp.float32))
    return jnp.repeat(spread, block_width, axis=2)


def normalize_rows(lower_part, pattern, weights, first_row, block_width):
    masked = lower_part.astype(jnp.float32) * expand_pattern(
        pattern, first_row, lower_part.shape[1], block_width
    )
    return jnp.einsum("nrk,nkc->nrc", masked, weights, precision=HIGHEST).astype(jnp.bfloat16)


def on_device(
    sigma_root, lower_one, weights_one, pattern_one, lower_root, lower_sep, weights_two, pattern_two
):
    grid_rows = lax.axis_size("prow")
    row_index = lax.axis_index("prow")
    root_rows = lower_one.shape[1]
    sep_rows = lower_sep.shape[1]
    sep_two_width = weights_two.shape[2]
    leaf_rows = sep_two_width // grid_rows
    root_blocks = pattern_one.shape[1]
    root_first = row_index * root_rows
    sep_first = row_index * sep_rows
    normal_one = normalize_rows(lower_one, pattern_one, weights_one, root_first, B)
    normal_root = normalize_rows(
        lower_root, pattern_two[:, :root_blocks, :], weights_two, root_first, B
    )
    normal_sep = normalize_rows(
        lower_sep, pattern_two[:, root_blocks:, :], weights_two, sep_first, B
    )
    root_full = lax.all_gather(sigma_root, "pcol", axis=1, tiled=True)
    columns = root_full
    sigma_one_root = -jnp.einsum(
        "rk,nkc->nrc",
        columns,
        lax.all_gather(normal_one, "prow", axis=1, tiled=True).astype(jnp.float32),
        precision=HIGHEST,
    )
    parent_cols = lax.all_to_all(sigma_one_root, "prow", split_axis=2, concat_axis=1, tiled=True)
    piece_float = lax.all_gather(normal_root, "prow", axis=1, tiled=True).astype(jnp.float32)
    columns = root_full
    across = parent_cols[0]
    root_next = jnp.einsum("rk,nkc->nrc", columns, piece_float, precision=HIGHEST)
    sep_next = jnp.einsum("kr,nkc->nrc", across, piece_float, precision=HIGHEST)
    weight_rows = lax.dynamic_slice_in_dim(weights_one, sep_first, sep_rows, 1)
    weight_cols = weight_rows
    normal_cols = normal_one.astype(jnp.float32)
    gram = jnp.einsum("nkr,nkc->rnc", weight_cols, weight_rows, precision=HIGHEST)
    sigma_one_diag = jnp.transpose(
        lax.psum_scatter(
            gram - jnp.einsum("nkr,nkc->rnc", normal_cols, sigma_one_root, precision=HIGHEST),
            "prow",
            scatter_dimension=0,
            tiled=True,
        ),
        (1, 0, 2),
    )
    sep_full = lax.all_gather(normal_sep, "prow", axis=1, tiled=True).astype(jnp.float32)
    sigma_two_root = -(
        root_next + jnp.einsum("rk,nkc->nrc", sigma_one_root[0], sep_full, precision=HIGHEST)
    )
    sigma_two_sep = -(
        sep_next + jnp.einsum("rk,nkc->nrc", sigma_one_diag[0], sep_full, precision=HIGHEST)
    )
    leaf_weights = lax.dynamic_slice_in_dim(weights_two, row_index * leaf_rows, leaf_rows, 1)
    weight_cols = leaf_weights
    root_cols = normal_root.astype(jnp.float32)
    sep_cols = normal_sep.astype(jnp.float32)
    gram = jnp.einsum("nkr,nkc->rnc", weight_cols, leaf_weights, precision=HIGHEST)
    gram = gram - jnp.einsum("nkr,nkc->rnc", root_cols, sigma_two_root, precision=HIGHEST)
    sigma_two_diag = jnp.transpose(
        lax.psum_scatter(
            gram - jnp.einsum("nkr,nkc->rnc", sep_cols, sigma_two_sep, precision=HIGHEST),
            "prow",
            scatter_dimension=0,
            tiled=True,
        ),
        (1, 0, 2),
    )
    return (sigma_one_root, sigma_one_diag, sigma_two_root, sigma_two_sep, sigma_two_diag)


def solution(mesh):
    placed = (
        P(("groups", "prow"), "pcol"),
        P(("groups", "pcol"), "prow", None),
        P(("groups", "pcol"), None, None),
        P(("groups", "pcol"), None, None),
        P(("groups", "pcol"), "prow", None),
        P(("groups", "pcol"), "prow", None),
        P(("groups", "pcol"), None, None),
        P(("groups", "pcol"), None, None),
    )
    return jax.shard_map(
        on_device,
        mesh=mesh,
        in_specs=placed,
        out_specs=(
            P(("groups", "pcol"), "prow", None),
            P(("groups", "pcol"), "prow", None),
            P(("groups", "pcol"), "prow", None),
            P(("groups", "pcol"), "prow", None),
            P(("groups", "pcol"), "prow", None),
        ),
        check_vma=False,
    )
```

profile of v0, /device:TPU:0, one launch (start us, length us, event | category | flops | bytes accessed | tf_op | source)
XLA Modules:
  0.0 469.8 jit_solution(6814390053608366955)
XLA Ops:
  7.2 0.0 copy-start
  7.2 0.0 all-gather.9.cloned.1.call-start
  7.2 1.0 fusion.26
  8.3 1.0 broadcast_in_dim.4
  9.3 0.0 copy-start.10
  9.3 2.5 broadcast_in_dim.5
  11.8 0.0 copy-done.10
  11.8 5.1 %fusion.15 = bf16[800,512]{1,0:T(8,128)(2,1)} fusion(f32[1,800,512]{2,1,0:T(8,128)} %broadcast_in_dim.5, bf16[1,800,512]{2,1,0:T(8,128)(2,1)S(1)} %copy-done.10, f32[1,512,512]{2,1,0:T(8,128)S(1)} %copy-done), kind=kOutput, calls=%fused_computation.15 | convolution fusion | flops 2517811200 | bytes 4325376 | tf_op jit(solution)/shard_map/nrk,nkc->nrc/dot_general | solution.py:25
  16.9 0.0 all-gather.9.cloned.1.call-update
  16.9 0.0 copy-start.15
  16.9 0.0 copy-start.7
  17.0 0.0 copy-start.9
  17.0 0.0 all-gather.5.cloned.1.call-start
  17.0 0.7 all-gather.5.cloned.1.call-update
  17.7 0.0 copy-start.16
  17.7 0.0 copy-start.14
  17.7 0.0 all-gather.7.cloned.1.call-start
  17.8 0.3 convolution_bitcast_fusion
  18.1 0.2 copy-done.9
  18.3 2.6 fusion.18
  20.8 0.0 all-gather.7.cloned.1.call-update
  20.9 0.6 dynamic-slice
  22.1 0.1 slice_convert_fusion
  22.2 0.2 convolution_bitcast_fusion.1
  22.4 0.0 copy-done.14
  22.4 0.5 convolution_convert_fusion
  22.9 0.6 copy-done.11
  23.5 37.2 %all_gather.15 = bf16[2,512,256]{2,1,0:T(8,128)(2,1)} all-gather(bf16[2,64,256]{2,1,0:T(8,128)(2,1)S(1)} %convolution_convert_fusion), channel_id=1, replica_groups=mesh['groups'=2,'prow'=8,'pcol'=2] {'prow'}, dimensions={1}, use_global_device_ids=true | all-gather | bytes 589824 | tf_op jit(solution)/shard_map/all_gather | solution.py:74
  60.8 65.5 %all-gather.9.cloned.1.call-done = bf16[6400,512]{1,0:T(8,128)(2,1)} async-done(((bf16[800,512]{1,0:T(8,128)(2,1)}), bf16[6400,512]{1,0:T(8,128)(2,1)}) %all-gather.9.cloned.1.call-update) | async-done | bytes 6553616 | tf_op jit(solution)/shard_map/all_gather | solution.py:52
  126.3 34.9 %all-gather.5.cloned.1.call-done = f32[800,6400]{1,0:T(8,128)} async-done(((f32[800,3200]{1,0:T(8,128)}), f32[800,6400]{1,0:T(8,128)}) %all-gather.5.cloned.1.call-update) | async-done | bytes 20480016 | tf_op jit(solution)/shard_map/all_gather | solution.py:47
  161.2 19.4 %convolution_negate_fusion = f32[512,800]{0,1:T(8,128)S(1)} fusion(bf16[6400,512]{1,0:T(8,128)(2,1)} %all-gather.9.cloned.1.call-done, f32[800,6400]{1,0:T(8,128)} %all-gather.5.cloned.1.call-done), kind=kOutput, calls=%fused_computation.14 | convolution fusion | flops 31457689600 | bytes 28672000 | tf_op jit(solution)/shard_map/rk,nkc->nrc/dot_general | solution.py:49
  180.7 0.0 copy-start.2
  180.7 1.8 fusion.4
  182.5 2.0 fusion.21
  184.5 3.6 copy.25
  188.1 3.6 copy.26
  191.8 5.8 %all-to-all-start = ((f32[1,800,512]{1,0,2:T(1,128)}), f32[1,800,512]{1,0,2:T(1,128)}, u32[]{:S(2)}, u32[]{:S(2)}) async-start(f32[1,800,512]{1,0,2:T(1,128)} %copy.26), calls=%async_computation | async-start | bytes 3670016 | tf_op jit(solution)/shard_map/all_to_all | solution.py:55
  197.5 0.0 all-reduce.5.cloned.1.call-start
  197.6 0.5 all-reduce.5.cloned.1.call-update
  198.1 0.3 all-reduce.7.cloned.1.call-start
  198.4 98.0 %all-gather.7.cloned.1.call-done = bf16[2,6400,256]{2,1,0:T(8,128)(2,1)} async-done(((bf16[2,800,256]{2,1,0:T(8,128)(2,1)}), bf16[2,6400,256]{2,1,0:T(8,128)(2,1)}) %all-gather.7.cloned.1.call-update) | async-done | bytes 6553616 | tf_op jit(solution)/shard_map/all_gather | solution.py:56
  296.4 19.6 %fusion = f32[2,256,800]{1,2,0:T(8,128)S(1)} fusion(bf16[2,6400,256]{2,1,0:T(8,128)(2,1)} %all-gather.7.cloned.1.call-done, f32[800,6400]{1,0:T(8,128)} %all-gather.5.cloned.1.call-done), kind=kOutput, calls=%fused_computation | convolution fusion | flops 31457280000 | bytes 28672000 | tf_op jit(solution)/shard_map/rk,nkc->nrc/dot_general | solution.py:59
  316.0 1.5 add_negate_fusion
  317.6 0.0 copy-start.5
  317.6 1.7 fusion.46
  319.4 2.4 convolution_subtract_fusion.2
  321.7 54.5 %all-reduce.5.cloned.1.call-done = f32[512,1,512]{2,1,0:T(1,128)} async-done(((f32[512,1,512]{2,1,0:T(1,128)}), f32[512,1,512]{2,1,0:T(1,128)}) %all-reduce.5.cloned.1.call-update) | async-done | bytes 1048592
  376.2 0.9 constant_dynamic-slice_fusion
  377.1 0.0 all-to-all-done
  377.1 1.6 copy.32
  378.7 1.1 copy.27
  379.8 1.8 reshape.113
  381.6 6.2 %fusion.45 = f32[2,256,64]{1,2,0:T(8,128)S(1)} fusion(bf16[2,6400,256]{2,1,0:T(8,128)(2,1)} %all-gather.7.cloned.1.call-done, f32[6400,64,1]{0,1,2:T(8,128)} %reshape.113), kind=kOutput, calls=%fused_computation.64 | convolution fusion | flops 2516582400 | bytes 8323072 | tf_op jit(solution)/shard_map/kr,nkc->nrc/dot_general | solution.py:60
  387.8 0.0 copy-start.1
  387.8 0.4 fusion.23
  388.2 0.0 copy-start.13
  388.2 0.4 fusion.22
  388.6 1.0 copy.28
  389.7 0.0 all-reduce.7.cloned.1.call-update
  390.3 0.9 fusion.63
  391.3 0.7 copy.29
  391.9 69.8 %all-reduce.7.cloned.1.call-done = f32[256,2,256]{2,1,0:T(2,128)} async-done(((f32[256,2,256]{2,1,0:T(2,128)}), f32[256,2,256]{2,1,0:T(2,128)}) %all-reduce.7.cloned.1.call-update) | async-done | bytes 524304
  461.8 0.8 dynamic-slice_bitcast_fusion
  462.6 0.6 copy.30
  (22 shorter events, 0.1 us)
Async XLA Ops:
  7.2 4.6 copy-start
  7.2 119.1 %all-gather.9.cloned.1.call-start = ((), (), s32[]{:S(2)}) async-start(), calls=%async_computation.3 | async-start | bytes 7372800 | tf_op jit(solution)/shard_map/all_gather | solution.py:52
  9.3 2.5 copy-start.10
  16.9 0.9 copy-start.15
  16.9 1.2 copy-start.7
  17.0 1.3 copy-start.9
  17.0 144.2 %all-gather.5.cloned.1.call-start = ((), (), s32[]{:S(2)}) async-start(), calls=%async_computation.1 | async-start | bytes 30720000 | tf_op jit(solution)/shard_map/all_gather | solution.py:47
  17.7 3.2 copy-start.16
  17.7 4.7 copy-start.14
  17.7 278.6 %all-gather.7.cloned.1.call-start = ((), (), s32[]{:S(2)}) async-start(), calls=%async_computation.2 | async-start | bytes 7372800 | tf_op jit(solution)/shard_map/all_gather | solution.py:56
  22.9 0.6 copy-start.11
  60.8 119.9 %copy-start.4 = (bf16[800,512]{1,0:T(8,128)(2,1)S(1)}, bf16[800,512]{1,0:T(8,128)(2,1)}, u32[]{:S(2)}) copy-start(bf16[800,512]{1,0:T(8,128)(2,1)} %fusion.15) | copy-start | bytes 2457604
  180.7 135.4 %copy-start.2 = (f32[512,800]{0,1:T(8,128)}, f32[512,800]{0,1:T(8,128)S(1)}, u32[]{:S(2)}) copy-start(f32[512,800]{0,1:T(8,128)S(1)} %convolution_negate_fusion) | copy-start | bytes 4915204
  191.8 185.3 %all-to-all-start = ((f32[1,800,512]{1,0,2:T(1,128)}), f32[1,800,512]{1,0,2:T(1,128)}, u32[]{:S(2)}, u32[]{:S(2)}) async-start(f32[1,800,512]{1,0,2:T(1,128)} %copy.26), calls=%async_computation | async-start | bytes 3670016 | tf_op jit(solution)/shard_map/all_to_all | solution.py:55
  197.5 178.6 %all-reduce.5.cloned.1.call-start = ((), (), s32[]{:S(2)}) async-start(), calls=%async_computation.4 | async-start | bytes 2097152
  198.1 117.9 %copy-start.6 = (bf16[2,512,256]{2,1,0:T(8,128)(2,1)S(1)}, bf16[2,512,256]{2,1,0:T(8,128)(2,1)}, u32[]{:S(2)}) copy-start(bf16[2,512,256]{2,1,0:T(8,128)(2,1)} %all_gather.15) | copy-start | bytes 1572868
  198.1 263.6 %all-reduce.7.cloned.1.call-start = ((), (), s32[]{:S(2)}) async-start(), calls=%async_computation.5 | async-start | bytes 1048576
  316.0 1.5 copy-start.3
  317.6 1.8 copy-start.5
  381.6 6.6 %copy-start.8 = (f32[2,256,256]{2,1,0:T(8,128)S(1)}, f32[2,256,256]{2,1,0:T(8,128)}, u32[]{:S(2)}) copy-start(f32[2,256,256]{2,1,0:T(8,128)} %convolution_subtract_fusion.2) | copy-start | bytes 1572868
  381.6 6.6 %copy-start.12 = (bf16[2,64,256]{2,1,0:T(8,128)(2,1)S(1)}, bf16[2,64,256]{2,1,0:T(8,128)(2,1)}, u32[]{:S(2)}) copy-start(bf16[2,64,256]{2,1,0:T(8,128)(2,1)} %copy-done.11) | copy-start | bytes 196612
  387.8 75.5 %copy-start.1 = (f32[1,512,512]{2,1,0:T(8,128)S(1)}, f32[1,512,512]{2,1,0:T(8,128)}, u32[]{:S(2)}) copy-start(f32[1,512,512]{2,1,0:T(8,128)} %param.10) | copy-start | bytes 3145732
  388.2 3.7 copy-start.13
Sparse Core Ops, SparseCore 0:
  17.1 109.1 all-gather.8
  127.8 33.3 all-gather.4
  163.4 132.9 all-gather.6
  299.8 76.3 all-reduce.4
  389.8 71.9 all-reduce.6
where the time goes:
time: 470 us
  waiting for transfers between devices  324 us (69%)
  matrix products  65.3 us (14%)
  blocking collectives  37.2 us (8%)
  local copies, waits for them, and re-layouts  21.6 us (5%)
  between operations  15.4 us (3%)
  starting transfers between devices  6.19 us (1%)
    unnamed x7, waiting for transfers between devices  126 us
    all_gather x1, waiting for transfers between devices, on_device(): lax.all_gather(normal_root, 'prow', axis=1, tiled=True).astype(jnp.float32)  98 us
    all_gather x1, waiting for transfers between devices, on_device(): lax.all_gather(normal_one, 'prow', axis=1, tiled=True).astype(jnp.float32)  65.5 us
    all_gather x1, blocking collectives, on_device(): lax.all_gather(normal_sep, 'prow', axis=1, tiled=True).astype(jnp.float32)  37.2 us
    all_gather x1, waiting for transfers between devices, on_device(): root_full = lax.all_gather(sigma_root, 'pcol', axis=1, tiled=True)  34.9 us
    dot_general x1, matrix products, on_device(): jnp.einsum('rk,nkc->nrc', columns, piece_float, precision=HIGHEST)  19.6 us
    dot_general x1, matrix products, on_device(): jnp.einsum('rk,nkc->nrc', columns, lax.all_gather(normal_one, 'prow', axi...  19.4 us
  transfers between devices with their start and end apart: 6, of which 5 were waited for; matrix products, arithmetic and copies ran while one was open for 13% of the time, Pallas kernels for 0%

commit v1 on v0

--- a/solution.py
+++ b/solution.py
@@ -96,6 +96,158 @@
     return (sigma_one_root, sigma_one_diag, sigma_two_root, sigma_two_sep, sigma_two_diag)
 
 
+def split_high_low(values):
+    high = lax.reduce_precision(values, 8, 7)
+    return high.astype(jnp.bfloat16), (values - high).astype(jnp.bfloat16)
+
+
+def masked_product(lower_part, pattern, weights, first_row):
+    mask = expand_pattern(pattern, first_row, lower_part.shape[1], B).astype(jnp.bfloat16)
+    masked = lower_part * mask
+    high, low = split_high_low(weights)
+    both = jnp.einsum(
+        "nrk,nkc->nrc", masked, high, preferred_element_type=jnp.float32
+    ) + jnp.einsum("nrk,nkc->nrc", masked, low, preferred_element_type=jnp.float32)
+    return both.astype(jnp.bfloat16)
+
+
+def dot(left, right):
+    return jnp.dot(left, right, preferred_element_type=jnp.float32)
+
+
+def dot_rows(left, right):
+    return lax.dot_general(
+        left, right, (((0,), (0,)), ((), ())), preferred_element_type=jnp.float32
+    )
+
+
+def line_gather(block, layers, layer):
+    up, down = [], []
+    held_up = held_down = block
+    for step in range(1, layers):
+        held_up = lax.ppermute(
+            held_up,
+            "prow",
+            [(2 * s + x, 2 * s + 2 + x) for s in range(step - 1, layers - 1) for x in (0, 1)],
+        )
+        held_down = lax.ppermute(
+            held_down,
+            "prow",
+            [(2 * s + x, 2 * s - 2 + x) for s in range(1, layers - step + 1) for x in (0, 1)],
+        )
+        up.append(held_up)
+        down.append(held_down)
+    gathered = jnp.zeros((layers,) + block.shape, block.dtype)
+    gathered = lax.dynamic_update_slice(gathered, block[None], (layer, 0, 0))
+    for back in range(1, layers):
+        piece = jnp.where(layer >= back, up[back - 1], down[layers - back - 1])
+        at = lax.rem(layer - back + layers, layers)
+        gathered = lax.dynamic_update_slice(gathered, piece[None], (at, 0, 0))
+    return gathered
+
+
+def scatter_sum(parts):
+    moved = lax.all_to_all(parts.astype(jnp.bfloat16), "prow", 0, 0, tiled=True)
+    return jnp.sum(moved.astype(jnp.float32), axis=0)
+
+
+def on_pairs(
+    sigma_root, lower_one, weights_one, pattern_one, lower_root, lower_sep, weights_two, pattern_two
+):
+    devices = lax.axis_size("prow")
+    layers = devices // 2
+    row_index = lax.axis_index("prow")
+    core = lax.axis_index("pcol")
+    layer, side = row_index // 2, lax.rem(row_index, 2)
+    rows = lower_one.shape[1]
+    sep_rows = lower_sep.shape[1]
+    sep_width = weights_one.shape[2]
+    leaf_width = weights_two.shape[2]
+    leaf_rows = leaf_width // devices
+    root_blocks = pattern_one.shape[1]
+    swap_side = [(s, s ^ 1) for s in range(devices)]
+    swap_core = [(0, 1), (1, 0)]
+
+    own_one = masked_product(lower_one, pattern_one, weights_one, row_index * rows)[0]
+    normal_root = masked_product(
+        lower_root, pattern_two[:, :root_blocks, :], weights_two, row_index * rows
+    )
+    own_two = jnp.concatenate([normal_root[0], normal_root[1]], axis=1)
+    normal_sep = masked_product(
+        lower_sep, pattern_two[:, root_blocks:, :], weights_two, row_index * sep_rows
+    )
+    own_sep = jnp.concatenate([normal_sep[0], normal_sep[1]], axis=1)
+
+    half = layers // 2
+    by_side = sigma_root.astype(jnp.bfloat16).reshape(rows, half, 2, rows)
+    even = by_side[:, :, 0, :].reshape(rows, half * rows)
+    odd = by_side[:, :, 1, :].reshape(rows, half * rows)
+    kept = jnp.where(side == 0, even, odd)
+    given = jnp.where(side == 0, odd, even)
+    taken = lax.ppermute(given, "prow", swap_side)
+    kept_sibling = lax.ppermute(kept, "pcol", swap_core)
+    taken_sibling = lax.ppermute(taken, "pcol", swap_core)
+
+    all_one = line_gather(own_one, layers, layer)
+    all_two = line_gather(own_two, layers, layer)
+    all_sep = lax.all_gather(own_sep, "prow", axis=0, tiled=True)
+
+    def root_product(gathered):
+        width = gathered.shape[2]
+        near = lax.dynamic_slice_in_dim(gathered, core * half, half, 0).reshape(-1, width)
+        far = lax.dynamic_slice_in_dim(gathered, (1 - core) * half, half, 0).reshape(-1, width)
+        away = dot(taken, near) + dot(taken_sibling, far)
+        arrived = lax.ppermute(away.astype(jnp.bfloat16), "prow", swap_side)
+        return dot(kept, near) + dot(kept_sibling, far) + arrived.astype(jnp.float32)
+
+    product_one = root_product(all_one)
+    short_one = product_one.astype(jnp.bfloat16)
+    gram_one = dot_rows(own_one, short_one).reshape(devices, sep_rows, sep_width)
+    sum_one = scatter_sum(gram_one)
+    weight_cols = lax.dynamic_slice_in_dim(weights_one[0], row_index * sep_rows, sep_rows, 1)
+    diag_rows = (
+        lax.dot_general(
+            weight_cols, weights_one[0], (((0,), (0,)), ((), ())), precision=HIGHEST
+        )
+        + sum_one
+    )
+
+    cross = dot_rows(short_one, own_two).reshape(devices, sep_rows, 2 * leaf_width)
+    product_two = root_product(all_two)
+    two_root = dot(short_one, all_sep) - product_two
+    short_two = two_root.astype(jnp.bfloat16)
+    leaf_gram = [
+        dot_rows(normal_root[b], short_two[:, b * leaf_width : (b + 1) * leaf_width]).reshape(
+            devices, leaf_rows, leaf_width
+        )
+        for b in range(2)
+    ]
+    sums = scatter_sum(cross)
+    sep_two = sums - dot(diag_rows.astype(jnp.bfloat16), all_sep)
+    short_sep = sep_two.astype(jnp.bfloat16)
+    leaf_gram = [
+        leaf_gram[b]
+        + dot_rows(normal_sep[b], short_sep[:, b * leaf_width : (b + 1) * leaf_width]).reshape(
+            devices, leaf_rows, leaf_width
+        )
+        for b in range(2)
+    ]
+    leaf_sum = scatter_sum(jnp.concatenate(leaf_gram, axis=2))
+    leaf_cols = lax.dynamic_slice_in_dim(weights_two, row_index * leaf_rows, leaf_rows, 2)
+    leaf_square = jnp.einsum("nkr,nkc->nrc", leaf_cols, weights_two, precision=HIGHEST)
+
+    def by_leaf(joined):
+        return jnp.stack([joined[:, :leaf_width], joined[:, leaf_width:]])
+
+    return (
+        -product_one[None],
+        diag_rows[None],
+        by_leaf(two_root),
+        by_leaf(sep_two),
+        leaf_square - by_leaf(leaf_sum),
+    )
+
+
 def solution(mesh):
     placed = (
         P(("groups", "prow"), "pcol"),
@@ -107,8 +259,9 @@
         P(("groups", "pcol"), None, None),
         P(("groups", "pcol"), None, None),
     )
+    body = on_pairs if mesh.shape["prow"] == 8 else on_device
     return jax.shard_map(
-        on_device,
+        body,
         mesh=mesh,
         in_specs=placed,
         out_specs=(

time: 470 us -> 334 us (0.71)
  waiting for transfers between devices: 324 us -> 57.9 us
  starting transfers between devices: 6.19 us -> 72.7 us
  local copies, waits for them, and re-layouts: 21.6 us -> 86.6 us
  other arithmetic: 0.1 us -> 26.7 us
  matrix products: 65.3 us -> 42.6 us
  between operations: 15.4 us -> 1.33 us
  blocking collectives: 37.2 us -> 43.7 us
    all_gather x3 -> x0, waiting for transfers between devices: 198 us -> none  [the longest x1 98 us: on_device(): lax.all_gather(normal_root, 'prow', axis=1, tiled=True).astype(jnp.float32)]
    unnamed x7 -> x0, waiting for transfers between devices: 126 us -> none
    ppermute x0 -> x17, waiting for transfers between devices: none -> 42.6 us  [the longest x6 24.3 us: line_gather(): lax.ppermute(held_up, 'prow', [(2 * s + x, 2 * s + 2 + x) for s in range(...]
    all_to_all x1 -> x3, starting transfers between devices: 5.78 us -> 44.6 us  [scatter_sum(): moved = lax.all_to_all(parts.astype(jnp.bfloat16), 'prow', 0, 0, tiled=True)]
    unnamed x39 -> x72, local copies, waits for them, and re-layouts: 5.29 us -> 40.5 us
    ppermute x0 -> x17, starting transfers between devices: none -> 28.1 us  [the longest x6 14.8 us: line_gather(): lax.ppermute(held_up, 'prow', [(2 * s + x, 2 * s + 2 + x) for s in range(...]
    dot_general x13 -> x24, matrix products: 63.7 us -> 41.8 us  [the longest x10 28.3 us: dot(): return jnp.dot(left, right, preferred_element_type=jnp.float32)]
    all_to_all x1 -> x3, waiting for transfers between devices: 0.01 us -> 15.4 us  [scatter_sum(): moved = lax.all_to_all(parts.astype(jnp.bfloat16), 'prow', 0, 0, tiled=True)]
  transfers between devices with their start and end apart: 6 -> 20, of which waited for: 5 -> 7; matrix products, arithmetic and copies ran while one was open for 13% -> 41% of each run, Pallas kernels for 0% -> 0%
where the time goes in v1:
time: 334 us; the launch traced here: 332 us
  local copies, waits for them, and re-layouts  86.6 us (26%)
  starting transfers between devices  72.7 us (22%)
  waiting for transfers between devices  57.9 us (17%)
  blocking collectives  43.7 us (13%)
  matrix products  42.6 us (13%)
  other arithmetic  26.7 us (8%)
    all_to_all x3, starting transfers between devices, scatter_sum(): moved = lax.all_to_all(parts.astype(jnp.bfloat16), 'prow', 0, 0, tiled=True)  44.6 us
    all_gather x1, blocking collectives, on_pairs(): all_sep = lax.all_gather(own_sep, 'prow', axis=0, tiled=True)  43.7 us
    unnamed x72, local copies, waits for them, and re-layouts  40.5 us
    dot_general x10, matrix products, dot(): return jnp.dot(left, right, preferred_element_type=jnp.float32)  28.3 us
    ppermute x6, waiting for transfers between devices, line_gather(): lax.ppermute(held_up, 'prow', [(2 * s + x, 2 * s + 2 + x) for s in range(...  24.3 us
    all_to_all x3, waiting for transfers between devices, scatter_sum(): moved = lax.all_to_all(parts.astype(jnp.bfloat16), 'prow', 0, 0, tiled=True)  15.4 us
    ppermute x6, starting transfers between devices, line_gather(): lax.ppermute(held_up, 'prow', [(2 * s + x, 2 * s + 2 + x) for s in range(...  14.8 us
    ppermute x2, waiting for transfers between devices, root_product(): arrived = lax.ppermute(away.astype(jnp.bfloat16), 'prow', swap_side)  13.1 us
  transfers between devices with their start and end apart: 20, of which 7 were waited for; matrix products, arithmetic and copies ran while one was open for 41% of the time, Pallas kernels for 0%

profile of v1, /device:TPU:0, one launch (start us, length us, event | category | flops | bytes accessed | tf_op | source)
XLA Modules:
  0.0 331.5 jit_solution(559670383233354613)
XLA Ops:
  1.7 1.8 fusion.12
  4.0 1.0 slice_bitcast_fusion.8
  5.8 1.0 pad_maximum_fusion.1
  6.7 1.4 collective-permute-start.11
  8.7 1.0 broadcast_in_dim.36
  13.4 1.5 bitcast_dynamic-update-slice_fusion.7
  14.9 1.3 collective-permute-start.1
  16.2 6.7 %convert_element_type.117 = bf16[800,3200]{1,0:T(8,128)(2,1)} convert(f32[800,3200]{1,0:T(8,128)} %param.8) | non-fusion elementwise | flops 2560000 | bytes 15360000 | tf_op jit(solution)/shard_map/convert_element_type | solution.py:182
  22.9 11.0 %reshape.136 = bf16[800,2,2,800]{3,2,1,0:T(2,128)(2,1)} reshape(bf16[800,3200]{1,0:T(8,128)(2,1)} %convert_element_type.117) | data formatting | bytes 10240000 | tf_op jit(solution)/shard_map/reshape | solution.py:182
  34.0 13.1 %fusion.47 = (bf16[800,2,1,800]{3,2,1,0:T(2,128)(2,1)}, bf16[800,2,1,800]{3,2,1,0:T(2,128)(2,1)}) fusion(bf16[800,2,2,800]{3,2,1,0:T(2,128)(2,1)} %reshape.136), kind=kLoop, calls=%fused_computation.119 | loop fusion | bytes 10240000 | tf_op jit(solution)/shard_map/slice | solution.py:183
  47.0 17.4 %copy.40 = bf16[800,2,1,800]{0,3,1,2:T(8,128)(2,1)} copy(bf16[800,2,1,800]{3,2,1,0:T(2,128)(2,1)} %get-tuple-element.7) | data formatting | bytes 5120000
  64.4 17.3 %copy.41 = bf16[800,2,1,800]{0,3,1,2:T(8,128)(2,1)} copy(bf16[800,2,1,800]{3,2,1,0:T(2,128)(2,1)} %get-tuple-element.8) | data formatting | bytes 5120000
  81.7 5.7 %broadcast_select_fusion.1 = (bf16[800,2,1,800]{0,3,1,2:T(8,128)(2,1)}, bf16[800,2,1,800]{0,3,1,2:T(8,128)(2,1)}) fusion(bf16[800,2,1,800]{0,3,1,2:T(8,128)(2,1)} %copy.40, bf16[800,2,1,800]{0,3,1,2:T(8,128)(2,1)} %copy.41, pred[]{:T(512)S(6)} %eq.14), kind=kLoop, calls=%fused_computation.1 | loop fusion | flops 2560000 | bytes 10240001 | tf_op jit(solution)/shard_map/jit(_where)/select_n | solution.py:185
  87.4 5.2 %copy.33 = bf16[800,1600]{1,0:T(8,128)(2,1)} copy(bf16[800,1600]{0,1:T(8,128)(2,1)} %bitcast.140) | data formatting | bytes 5120000 | tf_op jit(solution)/shard_map/jit(_where)/select_n | solution.py:186
  92.5 2.9 collective-permute-start.7
  95.5 6.1 %collective-permute-start.10 = (bf16[800,512]{1,0:T(8,128)(2,1)}, bf16[800,512]{1,0:T(8,128)(2,1)}, u32[]{:S(2)}, u32[]{:S(2)}) collective-permute-start(bf16[800,512]{1,0:T(8,128)(2,1)} %pad_maximum_fusion.1), channel_id=1, source_target_pairs={{0,4},{2,6},{4,8},{6,10},{8,12},{10,14},{1,5},{3,7},{5,9},{7,11},{... | collective-permute-start | bytes 2457608 | tf_op jit(solution)/shard_map/ppermute | solution.py:128
  101.6 3.9 %collective-permute-start = (bf16[800,512]{1,0:T(8,128)(2,1)}, bf16[800,512]{1,0:T(8,128)(2,1)}, u32[]{:S(2)}, u32[]{:S(2)}) collective-permute-start(bf16[800,512]{1,0:T(8,128)(2,1)} %get-tuple-element.30), channel_id=1, source_target_pairs={{0,4},{2,6},{4,8},{6,10},{8,12},{10,14},{1,5},{3,7},{5,9},{7,11},{... | collective-permute-start | bytes 2457608 | tf_op jit(solution)/shard_map/ppermute | solution.py:128
  105.5 1.3 collective-permute-start.12
  106.9 1.3 collective-permute-start.2
  108.4 11.3 %collective-permute-done.10 = bf16[800,512]{1,0:T(8,128)(2,1)} collective-permute-done((bf16[800,512]{1,0:T(8,128)(2,1)}, bf16[800,512]{1,0:T(8,128)(2,1)}, u32[]{:S(2)}, u32[]{:S(2)}) %collective-permute-start.10) | collective-permute-done | bytes 819232 | tf_op jit(solution)/shard_map/ppermute | solution.py:128
  119.7 1.6 collective-permute-start.14
  121.2 1.2 fusion.29
  122.5 13.0 %collective-permute-done = bf16[800,512]{1,0:T(8,128)(2,1)} collective-permute-done((bf16[800,512]{1,0:T(8,128)(2,1)}, bf16[800,512]{1,0:T(8,128)(2,1)}, u32[]{:S(2)}, u32[]{:S(2)}) %collective-permute-start) | collective-permute-done | bytes 819232 | tf_op jit(solution)/shard_map/ppermute | solution.py:128
  135.5 1.6 collective-permute-start.4
  137.0 1.3 collective-permute-start.13
  138.3 1.3 fusion.2
  139.6 5.1 %collective-permute-done.2 = bf16[800,512]{1,0:T(8,128)(2,1)} collective-permute-done((bf16[800,512]{1,0:T(8,128)(2,1)}, bf16[800,512]{1,0:T(8,128)(2,1)}, u32[]{:S(2)}, u32[]{:S(2)}) %collective-permute-start.2) | collective-permute-done | bytes 819232 | tf_op jit(solution)/shard_map/ppermute | solution.py:133
  144.7 1.3 collective-permute-start.3
  146.1 5.1 %copy.32 = bf16[800,1600]{1,0:T(8,128)(2,1)} copy(bf16[800,1600]{0,1:T(8,128)(2,1)} %bitcast.137) | data formatting | bytes 5120000 | tf_op jit(solution)/shard_map/jit(_where)/select_n | solution.py:185
  151.2 2.2 copy.34
  154.2 2.0 copy.38
  156.9 2.0 copy.36
  158.9 43.7 %all_gather.3 = bf16[512,512]{1,0:T(8,128)(2,1)} all-gather(bf16[64,512]{1,0:T(8,128)(2,1)S(1)} %pad_maximum_fusion.4), channel_id=1, replica_groups=mesh['groups'=2,'prow'=8,'pcol'=2] {'prow'}, dimensions={0}, use_global_device_ids=true | all-gather | bytes 589824 | tf_op jit(solution)/shard_map/all_gather | solution.py:193
  205.4 1.4 bitcast_dynamic-update-slice_fusion.2
  206.9 1.4 bitcast_dynamic-update-slice_fusion.6
  208.3 1.4 bitcast_dynamic-update-slice_fusion.1
  209.7 1.4 bitcast_dynamic-update-slice_fusion.5
  211.2 1.4 bitcast_dynamic-update-slice_fusion
  212.6 1.4 bitcast_dynamic-update-slice_fusion.4
  214.6 4.6 %fusion.51 = f32[800,512]{1,0:T(8,128)S(1)} fusion(bf16[800,1600]{1,0:T(8,128)(2,1)} %collective-permute-done.7, bf16[1600,512]{1,0:T(8,128)(2,1)S(1)} %bitcast.147), kind=kOutput, calls=%fused_computation.123 | convolution fusion | flops 1310720000 | bytes 5836800 | tf_op jit(solution)/shard_map/dot_general | solution.py:115
  219.2 1.6 fusion.50
  220.9 1.6 add_convert_fusion.2
  222.6 2.5 collective-permute-start.9
  225.0 3.4 %fusion.54 = f32[800,512]{1,0:T(8,128)S(1)} fusion(bf16[800,1600]{1,0:T(8,128)(2,1)} %collective-permute-done.7, bf16[1600,512]{1,0:T(8,128)(2,1)S(1)} %bitcast.145), kind=kOutput, calls=%fused_computation.126 | convolution fusion | flops 1310720000 | bytes 5836800 | tf_op jit(solution)/shard_map/dot_general | solution.py:115
  228.4 2.5 add_convert_fusion
  231.0 13.1 %collective-permute-done.9 = bf16[800,512]{1,0:T(8,128)(2,1)S(1)} collective-permute-done((bf16[800,512]{1,0:T(8,128)(2,1)S(1)}, bf16[800,512]{1,0:T(8,128)(2,1)S(1)}, u32[]{:S(2)}, u32[]{:S(2)}) %collective-permute-start.9) | collective-permute-done | bytes 819232 | tf_op jit(solution)/shard_map/ppermute | solution.py:200
  244.1 2.9 fusion.26
  247.9 1.5 convolution_convert_fusion.1
  249.4 35.6 %all-to-all-start = ((bf16[8,64,512]{2,1,0:T(8,128)(2,1)}), bf16[8,64,512]{2,1,0:T(8,128)(2,1)S(1)}, u32[]{:S(2)}, u32[]{:S(2)}) async-start(bf16[8,64,512]{2,1,0:T(8,128)(2,1)} %convolution_convert_fusion.1), calls=%async_computation | async-start | bytes 1048576 | tf_op jit(solution)/shard_map/all_to_all | solution.py:150
  285.0 4.5 %fusion.52 = f32[800,512]{1,0:T(8,128)} fusion(bf16[800,1600]{0,1:T(8,128)(2,1)S(1)} %bitcast.139, bf16[1600,512]{1,0:T(8,128)(2,1)} %bitcast.146), kind=kOutput, calls=%fused_computation.124 | convolution fusion | flops 1310720000 | bytes 5836800 | tf_op jit(solution)/shard_map/dot_general | solution.py:115
  289.5 2.8 fusion.53
  292.4 1.6 convolution_convert_fusion
  293.9 1.5 all-to-all-done
  295.4 5.3 %all-to-all-start.1 = ((bf16[8,64,512]{2,1,0:T(8,128)(2,1)}), bf16[8,64,512]{2,1,0:T(8,128)(2,1)}, u32[]{:S(2)}, u32[]{:S(2)}) async-start(bf16[8,64,512]{2,1,0:T(8,128)(2,1)} %bitcast.153), calls=%async_computation.1 | async-start | bytes 1048576 | tf_op jit(solution)/shard_map/all_to_all | solution.py:150
  300.8 2.5 fusion.49
  303.5 1.0 copy-done.5
  304.5 1.4 convolution_add_fusion.3
  306.0 7.6 %all-to-all-done.1 = bf16[8,64,512]{2,1,0:T(8,128)(2,1)} async-done(((bf16[8,64,512]{2,1,0:T(8,128)(2,1)}), bf16[8,64,512]{2,1,0:T(8,128)(2,1)}, u32[]{:S(2)}, u32[]{:S(2)}) %all-to-all-start.1) | async-done | bytes 524320 | tf_op jit(solution)/shard_map/all_to_all | solution.py:150
  313.6 1.2 convert_reduce_fusion
  314.7 1.8 fusion.48
  318.3 3.6 %all-to-all-start.2 = ((bf16[8,32,512]{2,1,0:T(8,128)(2,1)}), bf16[8,32,512]{2,1,0:T(8,128)(2,1)S(1)}, u32[]{:S(2)}, u32[]{:S(2)}) async-start(bf16[8,32,512]{2,1,0:T(8,128)(2,1)} %pad_maximum_fusion.2), calls=%async_computation.2 | async-start | bytes 524288 | tf_op jit(solution)/shard_map/all_to_all | solution.py:150
  321.9 1.3 pad_maximum_fusion
  323.9 6.3 %all-to-all-done.2 = bf16[8,32,512]{2,1,0:T(8,128)(2,1)S(1)} async-done(((bf16[8,32,512]{2,1,0:T(8,128)(2,1)}), bf16[8,32,512]{2,1,0:T(8,128)(2,1)S(1)}, u32[]{:S(2)}, u32[]{:S(2)}) %all-to-all-start.2) | async-done | bytes 262176 | tf_op jit(solution)/shard_map/all_to_all | solution.py:150
  330.2 1.3 convolution_subtract_fusion.1
  (117 shorter events, 15.3 us)
Async XLA Ops:
  0.6 2.9 copy-start.17
  0.6 2.9 copy-start
  4.0 4.2 %copy-start.34 = (s32[1,25,2]{1,2,0:T(2,128)S(1)}, s32[1,25,2]{1,2,0:T(2,128)}, u32[]{:S(2)}) copy-start(s32[1,25,2]{1,2,0:T(2,128)} %param.11) | copy-start | bytes 604
  5.0 0.7 copy-start.9
  5.0 1.7 copy-start.12
  6.7 4.4 %copy-start.3 = (f32[1,512,512]{2,1,0:T(8,128)S(1)}, f32[1,512,512]{2,1,0:T(8,128)}, u32[]{:S(2)}) copy-start(f32[1,512,512]{2,1,0:T(8,128)} %param.10) | copy-start | bytes 3145732
  6.7 4.4 %copy-start.15 = (bf16[1,800,512]{2,1,0:T(8,128)(2,1)S(1)}, bf16[1,800,512]{2,1,0:T(8,128)(2,1)}, u32[]{:S(2)}) copy-start(bf16[1,800,512]{2,1,0:T(8,128)(2,1)} %param.9) | copy-start | bytes 2457604
  6.7 98.8 %collective-permute-start.11 = (bf16[800,512]{1,0:T(8,128)(2,1)}, bf16[800,512]{1,0:T(8,128)(2,1)}, u32[]{:S(2)}, u32[]{:S(2)}) collective-permute-start(bf16[800,512]{1,0:T(8,128)(2,1)} %pad_maximum_fusion.1), channel_id=1, source_target_pairs={{4,0},{6,2},{8,4},{10,6},{12,8},{14,10},{5,1},{7,3},{9,5},{11,7},{... | collective-permute-start | bytes 2457608 | tf_op jit(solution)/shard_map/ppermute | solution.py:133
  10.2 0.9 copy-start.6
  11.7 1.2 copy-start.4
  11.7 1.5 copy-start.7
  11.7 1.7 copy-start.16
  14.9 92.0 %collective-permute-start.1 = (bf16[800,512]{1,0:T(8,128)(2,1)}, bf16[800,512]{1,0:T(8,128)(2,1)}, u32[]{:S(2)}, u32[]{:S(2)}) collective-permute-start(bf16[800,512]{1,0:T(8,128)(2,1)} %get-tuple-element.30), channel_id=1, source_target_pairs={{4,0},{6,2},{8,4},{10,6},{12,8},{14,10},{5,1},{7,3},{9,5},{11,7},{... | collective-permute-start | bytes 2457608 | tf_op jit(solution)/shard_map/ppermute | solution.py:133
  87.4 19.4 %copy-start.31 = (s32[2,27,1]{1,2,0:T(1,128)S(1)}, s32[2,27,1]{1,2,0:T(1,128)}, u32[]{:S(2)}) copy-start(s32[2,27,1]{1,2,0:T(1,128)} %param.15) | copy-start | bytes 652
  87.4 33.8 %copy-start.30 = (bf16[2,64,256]{2,1,0:T(8,128)(2,1)S(1)}, bf16[2,64,256]{2,1,0:T(8,128)(2,1)}, u32[]{:S(2)}) copy-start(bf16[2,64,256]{2,1,0:T(8,128)(2,1)} %param.13) | copy-start | bytes 196612
  92.5 114.3 %collective-permute-start.7 = (bf16[800,1600]{1,0:T(8,128)(2,1)}, bf16[800,1600]{1,0:T(8,128)(2,1)}, u32[]{:S(2)}, u32[]{:S(2)}) collective-permute-start(bf16[800,1600]{1,0:T(8,128)(2,1)} %copy.33), channel_id=1, source_target_pairs={{0,2},{2,0},{4,6},{6,4},{8,10},{10,8},{12,14},{14,12},{1,3},{3,1},... | collective-permute-start | bytes 7680008 | tf_op jit(solution)/shard_map/ppermute | solution.py:187
  95.5 24.2 %collective-permute-start.10 = (bf16[800,512]{1,0:T(8,128)(2,1)}, bf16[800,512]{1,0:T(8,128)(2,1)}, u32[]{:S(2)}, u32[]{:S(2)}) collective-permute-start(bf16[800,512]{1,0:T(8,128)(2,1)} %pad_maximum_fusion.1), channel_id=1, source_target_pairs={{0,4},{2,6},{4,8},{6,10},{8,12},{10,14},{1,5},{3,7},{5,9},{7,11},{... | collective-permute-start | bytes 2457608 | tf_op jit(solution)/shard_map/ppermute | solution.py:128
  101.6 33.9 %collective-permute-start = (bf16[800,512]{1,0:T(8,128)(2,1)}, bf16[800,512]{1,0:T(8,128)(2,1)}, u32[]{:S(2)}, u32[]{:S(2)}) collective-permute-start(bf16[800,512]{1,0:T(8,128)(2,1)} %get-tuple-element.30), channel_id=1, source_target_pairs={{0,4},{2,6},{4,8},{6,10},{8,12},{10,14},{1,5},{3,7},{5,9},{7,11},{... | collective-permute-start | bytes 2457608 | tf_op jit(solution)/shard_map/ppermute | solution.py:128
  105.5 31.6 %collective-permute-start.12 = (bf16[800,512]{1,0:T(8,128)(2,1)}, bf16[800,512]{1,0:T(8,128)(2,1)}, u32[]{:S(2)}, u32[]{:S(2)}) collective-permute-start(bf16[800,512]{1,0:T(8,128)(2,1)} %collective-permute-done.11), channel_id=1, source_target_pairs={{4,0},{6,2},{8,4},{10,6},{5,1},{7,3},{9,5},{11,7},{20,16},{22,18},... | collective-permute-start | bytes 2457608 | tf_op jit(solution)/shard_map/ppermute | solution.py:133
  106.9 37.9 %collective-permute-start.2 = (bf16[800,512]{1,0:T(8,128)(2,1)}, bf16[800,512]{1,0:T(8,128)(2,1)}, u32[]{:S(2)}, u32[]{:S(2)}) collective-permute-start(bf16[800,512]{1,0:T(8,128)(2,1)} %collective-permute-done.1), channel_id=1, source_target_pairs={{4,0},{6,2},{8,4},{10,6},{5,1},{7,3},{9,5},{11,7},{20,16},{22,18},... | collective-permute-start | bytes 2457608 | tf_op jit(solution)/shard_map/ppermute | solution.py:133
  119.7 82.9 %collective-permute-start.14 = (bf16[800,512]{1,0:T(8,128)(2,1)}, bf16[800,512]{1,0:T(8,128)(2,1)}, u32[]{:S(2)}, u32[]{:S(2)}) collective-permute-start(bf16[800,512]{1,0:T(8,128)(2,1)} %collective-permute-done.10), channel_id=1, source_target_pairs={{4,8},{6,10},{8,12},{10,14},{5,9},{7,11},{9,13},{11,15},{20,24},{2... | collective-permute-start | bytes 2457608 | tf_op jit(solution)/shard_map/ppermute | solution.py:128
  135.5 68.3 %collective-permute-start.4 = (bf16[800,512]{1,0:T(8,128)(2,1)}, bf16[800,512]{1,0:T(8,128)(2,1)}, u32[]{:S(2)}, u32[]{:S(2)}) collective-permute-start(bf16[800,512]{1,0:T(8,128)(2,1)} %collective-permute-done), channel_id=1, source_target_pairs={{4,8},{6,10},{8,12},{10,14},{5,9},{7,11},{9,13},{11,15},{20,24},{2... | collective-permute-start | bytes 2457608 | tf_op jit(solution)/shard_map/ppermute | solution.py:128
  137.0 67.4 %collective-permute-start.13 = (bf16[800,512]{1,0:T(8,128)(2,1)}, bf16[800,512]{1,0:T(8,128)(2,1)}, u32[]{:S(2)}, u32[]{:S(2)}) collective-permute-start(bf16[800,512]{1,0:T(8,128)(2,1)} %collective-permute-done.12), channel_id=1, source_target_pairs={{4,0},{6,2},{5,1},{7,3},{20,16},{22,18},{21,17},{23,19}} | collective-permute-start | bytes 2457608 | tf_op jit(solution)/shard_map/ppermute | solution.py:133
  144.7 62.2 %collective-permute-start.3 = (bf16[800,512]{1,0:T(8,128)(2,1)}, bf16[800,512]{1,0:T(8,128)(2,1)}, u32[]{:S(2)}, u32[]{:S(2)}) collective-permute-start(bf16[800,512]{1,0:T(8,128)(2,1)} %collective-permute-done.2), channel_id=1, source_target_pairs={{4,0},{6,2},{5,1},{7,3},{20,16},{22,18},{21,17},{23,19}} | collective-permute-start | bytes 2457608 | tf_op jit(solution)/shard_map/ppermute | solution.py:133
  202.5 1.0 copy-start.10
  202.6 1.1 copy-start.13
  202.6 16.7 %collective-permute-start.6 = (bf16[800,1600]{1,0:T(8,128)(2,1)}, bf16[800,1600]{1,0:T(8,128)(2,1)S(1)}, u32[]{:S(2)}, u32[]{:S(2)}) collective-permute-start(bf16[800,1600]{1,0:T(8,128)(2,1)} %copy.32), channel_id=1, source_target_pairs={{0,1},{1,0},{2,3},{3,2},{4,5},{5,4},{6,7},{7,6},{8,9},{9,8},{10,11... | collective-permute-start | bytes 7680008 | tf_op jit(solution)/shard_map/ppermute | solution.py:188
  203.8 7.4 %collective-permute-start.15 = (bf16[800,512]{1,0:T(8,128)(2,1)}, bf16[800,512]{1,0:T(8,128)(2,1)S(1)}, u32[]{:S(2)}, u32[]{:S(2)}) collective-permute-start(bf16[800,512]{1,0:T(8,128)(2,1)} %collective-permute-done.14), channel_id=1, source_target_pairs={{8,12},{10,14},{9,13},{11,15},{24,28},{26,30},{25,29},{27,31}} | collective-permute-start | bytes 2457608 | tf_op jit(solution)/shard_map/ppermute | solution.py:128
  204.5 8.1 %collective-permute-start.5 = (bf16[800,512]{1,0:T(8,128)(2,1)}, bf16[800,512]{1,0:T(8,128)(2,1)S(1)}, u32[]{:S(2)}, u32[]{:S(2)}) collective-permute-start(bf16[800,512]{1,0:T(8,128)(2,1)} %collective-permute-done.4), channel_id=1, source_target_pairs={{8,12},{10,14},{9,13},{11,15},{24,28},{26,30},{25,29},{27,31}} | collective-permute-start | bytes 2457608 | tf_op jit(solution)/shard_map/ppermute | solution.py:128
  206.8 14.1 %collective-permute-start.8 = (bf16[800,1600]{1,0:T(8,128)(2,1)}, bf16[800,1600]{1,0:T(8,128)(2,1)S(1)}, u32[]{:S(2)}, u32[]{:S(2)}) collective-permute-start(bf16[800,1600]{1,0:T(8,128)(2,1)} %collective-permute-done.7), channel_id=1, source_target_pairs={{0,1},{1,0},{2,3},{3,2},{4,5},{5,4},{6,7},{7,6},{8,9},{9,8},{10,11... | collective-permute-start | bytes 7680008 | tf_op jit(solution)/shard_map/ppermute | solution.py:189
  214.6 10.4 %copy-start.22 = (bf16[2,800,512]{2,1,0:T(8,128)(2,1)}, bf16[2,800,512]{2,1,0:T(8,128)(2,1)S(1)}, u32[]{:S(2)}) copy-start(bf16[2,800,512]{2,1,0:T(8,128)(2,1)S(1)} %get-tuple-element.12) | copy-start | bytes 4915204
  214.6 13.8 %copy-start.20 = (bf16[2,800,512]{2,1,0:T(8,128)(2,1)}, bf16[2,800,512]{2,1,0:T(8,128)(2,1)S(1)}, u32[]{:S(2)}) copy-start(bf16[2,800,512]{2,1,0:T(8,128)(2,1)S(1)} %get-tuple-element.11) | copy-start | bytes 4915204
  219.2 1.7 copy-start.32
  222.6 21.5 %collective-permute-start.9 = (bf16[800,512]{1,0:T(8,128)(2,1)S(1)}, bf16[800,512]{1,0:T(8,128)(2,1)S(1)}, u32[]{:S(2)}, u32[]{:S(2)}) collective-permute-start(bf16[800,512]{1,0:T(8,128)(2,1)S(1)} %add_convert_fusion.2), channel_id=1, source_target_pairs={{0,2},{2,0},{4,6},{6,4},{8,10},{10,8},{12,14},{14,12},{1,3},{3,1},... | collective-permute-start | bytes 2457608 | tf_op jit(solution)/shard_map/ppermute | solution.py:200
  228.4 15.7 %copy-start.2 = (bf16[800,2,1,800]{0,3,1,2:T(8,128)(2,1)S(1)}, bf16[800,2,1,800]{0,3,1,2:T(8,128)(2,1)}, u32[]{:S(2)}) copy-start(bf16[800,2,1,800]{0,3,1,2:T(8,128)(2,1)} %get-tuple-element.5) | copy-start | bytes 7680004
  231.0 16.9 %copy-start.24 = (bf16[512,800]{1,0:T(8,128)(2,1)S(1)}, bf16[512,800]{1,0:T(8,128)(2,1)}, u32[]{:S(2)}) copy-start(bf16[512,800]{1,0:T(8,128)(2,1)} %copy.34) | copy-start | bytes 2457604
  231.0 69.8 %collective-permute-start.16 = (bf16[800,512]{1,0:T(8,128)(2,1)}, bf16[800,512]{1,0:T(8,128)(2,1)}, u32[]{:S(2)}, u32[]{:S(2)}) collective-permute-start(bf16[800,512]{1,0:T(8,128)(2,1)} %add_convert_fusion), channel_id=1, source_target_pairs={{0,2},{2,0},{4,6},{6,4},{8,10},{10,8},{12,14},{14,12},{1,3},{3,1},... | collective-permute-start | bytes 2457608 | tf_op jit(solution)/shard_map/ppermute | solution.py:200
  247.0 0.9 copy-start.25
  249.4 46.0 %all-to-all-start = ((bf16[8,64,512]{2,1,0:T(8,128)(2,1)}), bf16[8,64,512]{2,1,0:T(8,128)(2,1)S(1)}, u32[]{:S(2)}, u32[]{:S(2)}) async-start(bf16[8,64,512]{2,1,0:T(8,128)(2,1)} %convolution_convert_fusion.1), calls=%async_computation | async-start | bytes 1048576 | tf_op jit(solution)/shard_map/all_to_all | solution.py:150
  285.0 4.5 %copy-start.21 = (bf16[2,800,512]{2,1,0:T(8,128)(2,1)S(1)}, bf16[2,800,512]{2,1,0:T(8,128)(2,1)}, u32[]{:S(2)}) copy-start(bf16[2,800,512]{2,1,0:T(8,128)(2,1)} %copy-done.20) | copy-start | bytes 4915204
  285.0 4.5 %copy-start.33 = (bf16[800,1600]{1,0:T(8,128)(2,1)S(1)}, bf16[800,1600]{1,0:T(8,128)(2,1)}, u32[]{:S(2)}) copy-start(bf16[800,1600]{1,0:T(8,128)(2,1)} %copy-done.32) | copy-start | bytes 7680004
  289.5 2.8 copy-start.11
  289.5 2.8 copy-start.14
  289.5 2.8 copy-start.26
  292.3 8.4 %copy-start.8 = (bf16[512,512]{1,0:T(8,128)(2,1)S(1)}, bf16[512,512]{1,0:T(8,128)(2,1)}, u32[]{:S(2)}) copy-start(bf16[512,512]{1,0:T(8,128)(2,1)} %all_gather.3) | copy-start | bytes 1572868
  292.3 8.4 %copy-start.23 = (f32[800,512]{1,0:T(8,128)S(1)}, f32[800,512]{1,0:T(8,128)}, u32[]{:S(2)}) copy-start(f32[800,512]{1,0:T(8,128)} %fusion.52) | copy-start | bytes 4915204
  295.4 18.2 %all-to-all-start.1 = ((bf16[8,64,512]{2,1,0:T(8,128)(2,1)}), bf16[8,64,512]{2,1,0:T(8,128)(2,1)}, u32[]{:S(2)}, u32[]{:S(2)}) async-start(bf16[8,64,512]{2,1,0:T(8,128)(2,1)} %bitcast.153), calls=%async_computation.1 | async-start | bytes 1048576 | tf_op jit(solution)/shard_map/all_to_all | solution.py:150
  303.3 1.2 copy-start.5
  304.5 12.0 %copy-start.28 = (bf16[256,64]{1,0:T(8,128)(2,1)S(1)}, bf16[256,64]{1,0:T(8,128)(2,1)}, u32[]{:S(2)}) copy-start(bf16[256,64]{1,0:T(8,128)(2,1)} %copy.39) | copy-start | bytes 98308
  304.5 12.4 %copy-start.18 = (bf16[256,800]{1,0:T(8,128)(2,1)S(1)}, bf16[256,800]{1,0:T(8,128)(2,1)}, u32[]{:S(2)}) copy-start(bf16[256,800]{1,0:T(8,128)(2,1)} %copy.38) | copy-start | bytes 1228804
  313.6 3.2 copy-start.29
  314.7 2.5 copy-start.19
  318.3 11.9 %all-to-all-start.2 = ((bf16[8,32,512]{2,1,0:T(8,128)(2,1)}), bf16[8,32,512]{2,1,0:T(8,128)(2,1)S(1)}, u32[]{:S(2)}, u32[]{:S(2)}) async-start(bf16[8,32,512]{2,1,0:T(8,128)(2,1)} %pad_maximum_fusion.2), calls=%async_computation.2 | async-start | bytes 524288 | tf_op jit(solution)/shard_map/all_to_all | solution.py:150
  321.9 1.3 copy-start.27
  321.9 8.3 %copy-start.1 = (f32[2,256,256]{2,1,0:T(8,128)S(1)}, f32[2,256,256]{2,1,0:T(8,128)}, u32[]{:S(2)}) copy-start(f32[2,256,256]{2,1,0:T(8,128)} %param.14) | copy-start | bytes 1572868

commit v2 on v1

--- a/solution.py
+++ b/solution.py
@@ -1,6 +1,8 @@
 import jax
 import jax.numpy as jnp
 from jax import lax
+from jax.experimental import pallas as pl
+from jax.experimental.pallas import tpu as pltpu
 from jax.sharding import PartitionSpec as P
 
 B = 256
@@ -121,8 +123,49 @@
     )
 
 
-def line_gather(block, layers, layer):
+def part_columns(sigma, side):
+    rows, columns = sigma.shape
+    step = 160 if rows % 160 == 0 else rows
+    count = columns // rows
+
+    def kernel(side_ref, sigma_ref, kept_ref, given_ref):
+        def pick(first):
+            pieces = [
+                sigma_ref[:, block * rows : (block + 1) * rows] for block in range(first, count, 2)
+            ]
+            return jnp.concatenate(pieces, axis=1).astype(jnp.bfloat16)
+
+        @pl.when(side_ref[0] == 0)
+        def _():
+            kept_ref[...] = pick(0)
+            given_ref[...] = pick(1)
+
+        @pl.when(side_ref[0] != 0)
+        def _():
+            kept_ref[...] = pick(1)
+            given_ref[...] = pick(0)
+
+    half = jax.ShapeDtypeStruct((rows, columns // 2), jnp.bfloat16)
+    return pl.pallas_call(
+        kernel,
+        grid=(rows // step,),
+        in_specs=[
+            pl.BlockSpec(memory_space=pltpu.SMEM),
+            pl.BlockSpec((step, columns), lambda i: (i, 0)),
+        ],
+        out_specs=[pl.BlockSpec((step, columns // 2), lambda i: (i, 0))] * 2,
+        out_shape=[half, half],
+        compiler_params=pltpu.CompilerParams(vmem_limit_bytes=24 * 2**20),
+        cost_estimate=pl.CostEstimate(
+            flops=0, bytes_accessed=rows * columns * 6, transcendentals=0
+        ),
+    )(side.reshape(1), sigma)
+
+
+def line_gather(block, layers, layer, after=None):
     up, down = [], []
+    if after is not None:
+        block, _ = lax.optimization_barrier((block, after))
     held_up = held_down = block
     for step in range(1, layers):
         held_up = lax.ppermute(
@@ -143,7 +186,7 @@
         piece = jnp.where(layer >= back, up[back - 1], down[layers - back - 1])
         at = lax.rem(layer - back + layers, layers)
         gathered = lax.dynamic_update_slice(gathered, piece[None], (at, 0, 0))
-    return gathered
+    return gathered, (up[1], down[1])
 
 
 def scatter_sum(parts):
@@ -179,18 +222,21 @@
     own_sep = jnp.concatenate([normal_sep[0], normal_sep[1]], axis=1)
 
     half = layers // 2
-    by_side = sigma_root.astype(jnp.bfloat16).reshape(rows, half, 2, rows)
-    even = by_side[:, :, 0, :].reshape(rows, half * rows)
-    odd = by_side[:, :, 1, :].reshape(rows, half * rows)
-    kept = jnp.where(side == 0, even, odd)
-    given = jnp.where(side == 0, odd, even)
+    kept, given = part_columns(sigma_root, side)
     taken = lax.ppermute(given, "prow", swap_side)
     kept_sibling = lax.ppermute(kept, "pcol", swap_core)
     taken_sibling = lax.ppermute(taken, "pcol", swap_core)
 
-    all_one = line_gather(own_one, layers, layer)
-    all_two = line_gather(own_two, layers, layer)
-    all_sep = lax.all_gather(own_sep, "prow", axis=0, tiled=True)
+    joined, late = line_gather(jnp.concatenate([own_one, own_sep]), layers, layer)
+    all_one = joined[:, :rows]
+    all_two, _ = line_gather(own_two, layers, layer, late)
+    sep_here = joined[:, rows:]
+    sep_there = lax.ppermute(sep_here, "prow", swap_side)
+    all_sep = jnp.where(
+        side == 0,
+        jnp.stack([sep_here, sep_there], axis=1),
+        jnp.stack([sep_there, sep_here], axis=1),
+    ).reshape(sep_width, 2 * leaf_width)
 
     def root_product(gathered):
         width = gathered.shape[2]

time: 334 us -> 232 us (0.69)
  local copies, waits for them, and re-layouts: 86.6 us -> 21.1 us
  waiting for transfers between devices: 57.9 us -> 103 us
  blocking collectives: 43.7 us -> 0 us
  starting transfers between devices: 72.7 us -> 46.8 us
  other arithmetic: 26.7 us -> 14.2 us
    ppermute x6, waiting for transfers between devices: 5.14 us -> 62.5 us  [line_gather(): lax.ppermute(held_down, 'prow', [(2 * s + x, 2 * s - 2 + x) for s in rang...]
    all_gather x1 -> x0, blocking collectives: 43.7 us -> none  [on_pairs(): all_sep = lax.all_gather(own_sep, 'prow', axis=0, tiled=True)]
    unnamed x72 -> x58, local copies, waits for them, and re-layouts: 40.5 us -> 6.98 us
    all_to_all x3, starting transfers between devices: 44.6 us -> 16.3 us  [scatter_sum(): moved = lax.all_to_all(parts.astype(jnp.bfloat16), 'prow', 0, 0, tiled=True)]
    ppermute x6, waiting for transfers between devices: 24.3 us -> 7.88 us  [line_gather(): lax.ppermute(held_up, 'prow', [(2 * s + x, 2 * s + 2 + x) for s in range(...]
    slice x1, local copies, waits for them, and re-layouts: 13.1 us -> 0.21 us  [on_pairs(): all_one = joined[:, :rows]]
    reshape x1 -> x0, local copies, waits for them, and re-layouts: 11 us -> none  [on_pairs(): by_side = sigma_root.astype(jnp.bfloat16).reshape(rows, half, 2, rows)]
    select_n x2 -> x0, local copies, waits for them, and re-layouts: 10.3 us -> none  [the longest x1 5.15 us: on_pairs(): given = jnp.where(side == 0, odd, even)]
  transfers between devices with their start and end apart: 20 -> 21, of which waited for: 7 -> 12; matrix products, arithmetic and copies ran while one was open for 41% -> 24% of each run, Pallas kernels for 0% -> 1%
where the time goes in v2:
time: 232 us; the launch traced here: 231 us
  waiting for transfers between devices  103 us (44%)
  starting transfers between devices  46.8 us (20%)
  matrix products  41.2 us (18%)
  local copies, waits for them, and re-layouts  21.1 us (9%)
  other arithmetic  14.2 us (6%)
  Pallas kernels  3.33 us (1%)
    ppermute x6, waiting for transfers between devices, line_gather(): lax.ppermute(held_down, 'prow', [(2 * s + x, 2 * s - 2 + x) for s in rang...  62.5 us
    dot_general x10, matrix products, dot(): return jnp.dot(left, right, preferred_element_type=jnp.float32)  27.7 us
    ppermute x6, starting transfers between devices, line_gather(): lax.ppermute(held_up, 'prow', [(2 * s + x, 2 * s + 2 + x) for s in range(...  17.1 us
    all_to_all x3, starting transfers between devices, scatter_sum(): moved = lax.all_to_all(parts.astype(jnp.bfloat16), 'prow', 0, 0, tiled=True)  16.3 us
    all_to_all x3, waiting for transfers between devices, scatter_sum(): moved = lax.all_to_all(parts.astype(jnp.bfloat16), 'prow', 0, 0, tiled=True)  15.2 us
    ppermute x2, waiting for transfers between devices, root_product(): arrived = lax.ppermute(away.astype(jnp.bfloat16), 'prow', swap_side)  14.9 us
    dot_general x6, local copies, waits for them, and re-layouts, dot_rows(): lax.dot_general(left, right, (((0,), (0,)), ((), ())), preferred_element_...  8.58 us
    ppermute x6, waiting for transfers between devices, line_gather(): lax.ppermute(held_up, 'prow', [(2 * s + x, 2 * s + 2 + x) for s in range(...  7.88 us
  transfers between devices with their start and end apart: 21, of which 12 were waited for; matrix products, arithmetic and copies ran while one was open for 24% of the time, Pallas kernels for 1%

profile of v2, /device:TPU:0, one launch (start us, length us, event | category | flops | bytes accessed | tf_op | source)
XLA Modules:
  0.0 230.7 jit_solution(11747730983180367117)
XLA Ops:
  1.6 1.3 fusion.29
  2.9 1.3 fusion.2
  5.4 1.0 broadcast_in_dim.46
  8.8 1.0 maximum_maximum_fusion
  9.8 5.9 %collective-permute-start = (bf16[864,512]{1,0:T(8,128)(2,1)}, bf16[864,512]{1,0:T(8,128)(2,1)}, u32[]{:S(2)}, u32[]{:S(2)}) collective-permute-start(bf16[864,512]{1,0:T(8,128)(2,1)} %maximum_maximum_fusion), channel_id=1, source_target_pairs={{0,4},{2,6},{4,8},{6,10},{8,12},{10,14},{1,5},{3,7},{5,9},{7,11},{... | collective-permute-start | bytes 2654216 | tf_op jit(solution)/shard_map/ppermute | solution.py:171
  15.8 1.3 collective-permute-start.1
  17.1 3.9 %copy-done = f32[800,3200]{1,0:T(8,128)S(1)} copy-done((f32[800,3200]{1,0:T(8,128)S(1)}, f32[800,3200]{1,0:T(8,128)}, u32[]{:S(2)}) %copy-start) | copy-done | bytes 10240024
  21.0 3.3 %shard_map.119 = (bf16[800,1600]{1,0:T(8,128)(2,1)S(1)}, bf16[800,1600]{1,0:T(8,128)(2,1)}) custom-call(s32[1]{0:T(128)} %bitcast.side_ref, f32[800,3200]{1,0:T(8,128)S(1)} %copy-done), custom_call_target="tpu_custom_call" | custom-call | bytes 15360000 | tf_op jit(solution)/shard_map/pallas_call | solution.py:149
  24.3 1.5 collective-permute-start.7
  26.1 7.9 %collective-permute-done = bf16[864,512]{1,0:T(8,128)(2,1)} collective-permute-done((bf16[864,512]{1,0:T(8,128)(2,1)}, bf16[864,512]{1,0:T(8,128)(2,1)}, u32[]{:S(2)}, u32[]{:S(2)}) %collective-permute-start) | collective-permute-done | bytes 884768 | tf_op jit(solution)/shard_map/ppermute | solution.py:171
  33.9 1.6 collective-permute-start.4
  35.6 3.5 %collective-permute-done.1 = bf16[864,512]{1,0:T(8,128)(2,1)} collective-permute-done((bf16[864,512]{1,0:T(8,128)(2,1)}, bf16[864,512]{1,0:T(8,128)(2,1)}, u32[]{:S(2)}, u32[]{:S(2)}) %collective-permute-start.1) | collective-permute-done | bytes 884768 | tf_op jit(solution)/shard_map/ppermute | solution.py:176
  39.1 1.3 collective-permute-start.2
  41.2 1.0 slice_bitcast_fusion.8
  43.0 1.0 pad_maximum_fusion.1
  44.0 17.6 %collective-permute-done.2 = bf16[864,512]{1,0:T(8,128)(2,1)} collective-permute-done((bf16[864,512]{1,0:T(8,128)(2,1)}, bf16[864,512]{1,0:T(8,128)(2,1)}, u32[]{:S(2)}, u32[]{:S(2)}) %collective-permute-start.2) | collective-permute-done | bytes 884768 | tf_op jit(solution)/shard_map/ppermute | solution.py:176
  61.6 1.3 collective-permute-start.12
  62.9 1.3 collective-permute-start.3
  64.2 6.4 %collective-permute-start.11 = (bf16[800,512]{1,0:T(8,128)(2,1)}, bf16[800,512]{1,0:T(8,128)(2,1)}, u32[]{:S(2)}, u32[]{:S(2)}) collective-permute-start(bf16[800,512]{1,0:T(8,128)(2,1)} %pad_maximum_fusion.1), channel_id=1, source_target_pairs={{0,4},{2,6},{4,8},{6,10},{8,12},{10,14},{1,5},{3,7},{5,9},{7,11},{... | collective-permute-start | bytes 2457608 | tf_op jit(solution)/shard_map/ppermute | solution.py:171
  70.5 1.6 collective-permute-start.5
  72.1 12.8 %collective-permute-done.12 = bf16[800,512]{1,0:T(8,128)(2,1)} collective-permute-done((bf16[800,512]{1,0:T(8,128)(2,1)}, bf16[800,512]{1,0:T(8,128)(2,1)}, u32[]{:S(2)}, u32[]{:S(2)}) %collective-permute-start.12) | collective-permute-done | bytes 819232 | tf_op jit(solution)/shard_map/ppermute | solution.py:176
  85.0 1.3 collective-permute-start.13
  86.3 1.5 copy.24
  87.8 1.5 copy.26
  89.3 1.3 copy.21
  90.6 2.0 copy.23
  92.5 2.0 copy.25
  95.9 8.0 %collective-permute-done.3 = bf16[864,512]{1,0:T(8,128)(2,1)} collective-permute-done((bf16[864,512]{1,0:T(8,128)(2,1)}, bf16[864,512]{1,0:T(8,128)(2,1)}, u32[]{:S(2)}, u32[]{:S(2)}) %collective-permute-start.3) | collective-permute-done | bytes 884768 | tf_op jit(solution)/shard_map/ppermute | solution.py:176
  104.6 1.5 bitcast_dynamic-update-slice_fusion.2
  106.1 1.5 bitcast_dynamic-update-slice_fusion.1
  107.6 10.7 %collective-permute-done.13 = bf16[800,512]{1,0:T(8,128)(2,1)} collective-permute-done((bf16[800,512]{1,0:T(8,128)(2,1)}, bf16[800,512]{1,0:T(8,128)(2,1)}, u32[]{:S(2)}, u32[]{:S(2)}) %collective-permute-start.13) | collective-permute-done | bytes 819232 | tf_op jit(solution)/shard_map/ppermute | solution.py:176
  118.3 1.3 collective-permute-start.14
  119.6 1.5 bitcast_dynamic-update-slice_fusion
  121.1 1.6 collective-permute-start.10
  123.8 1.2 bitcast_dynamic-update-slice_fusion.7
  125.2 2.3 collective-permute-done.10
  127.6 9.9 %collective-permute-done.14 = bf16[800,512]{1,0:T(8,128)(2,1)S(1)} collective-permute-done((bf16[800,512]{1,0:T(8,128)(2,1)}, bf16[800,512]{1,0:T(8,128)(2,1)S(1)}, u32[]{:S(2)}, u32[]{:S(2)}) %collective-permute-start.14) | collective-permute-done | bytes 819232 | tf_op jit(solution)/shard_map/ppermute | solution.py:176
  137.7 1.4 bitcast_dynamic-update-slice_fusion.5
  139.1 1.4 bitcast_dynamic-update-slice_fusion.4
  141.0 4.6 %fusion.53 = f32[800,512]{1,0:T(8,128)S(1)} fusion(bf16[800,1600]{1,0:T(8,128)(2,1)} %collective-permute-done.7, bf16[1600,512]{1,0:T(8,128)(2,1)S(1)} %bitcast.143), kind=kOutput, calls=%fused_computation.125 | convolution fusion | flops 1310720000 | bytes 5836800 | tf_op jit(solution)/shard_map/dot_general | solution.py:117
  145.6 3.4 %fusion.50 = f32[800,512]{1,0:T(8,128)S(1)} fusion(bf16[800,1600]{1,0:T(8,128)(2,1)} %collective-permute-done.7, bf16[1600,512]{1,0:T(8,128)(2,1)S(1)} %bitcast.145), kind=kOutput, calls=%fused_computation.122 | convolution fusion | flops 1310720000 | bytes 5836800 | tf_op jit(solution)/shard_map/dot_general | solution.py:117
  149.0 1.6 add_convert_fusion.2
  150.7 1.6 collective-permute-start.9
  152.2 1.6 fusion.49
  153.9 2.6 %add_convert_fusion = bf16[800,512]{1,0:T(8,128)(2,1)} fusion(f32[800,512]{1,0:T(8,128)S(1)} %fusion.53, bf16[800,1600]{1,0:T(8,128)(2,1)S(1)} %collective-permute-done.8, bf16[1600,512]{1,0:T(8,128)(2,1)S(1)} %bitcast.141), kind=kOutput, calls=%fused_computation.2 | convolution fusion | flops 1311539200 | bytes 6656000 | tf_op jit(solution)/shard_map/dot_general | solution.py:117
  157.1 14.9 %collective-permute-done.9 = bf16[800,512]{1,0:T(8,128)(2,1)S(1)} collective-permute-done((bf16[800,512]{1,0:T(8,128)(2,1)S(1)}, bf16[800,512]{1,0:T(8,128)(2,1)S(1)}, u32[]{:S(2)}, u32[]{:S(2)}) %collective-permute-start.9) | collective-permute-done | bytes 819232 | tf_op jit(solution)/shard_map/ppermute | solution.py:246
  171.9 2.8 %fusion.26 = (bf16[800,512]{1,0:T(8,128)(2,1)S(1)}, f32[1,800,512]{2,1,0:T(8,128)}) fusion(bf16[800,512]{1,0:T(8,128)(2,1)S(1)} %collective-permute-done.9, f32[800,512]{1,0:T(8,128)S(1)} %fusion.49, bf16[800,1600]{1,0:T(8,128)(2,1)S(1)} %get-tuple-element.8, bf16[1600,512]{1,0:T(8,128)(2,1)S(1)} %bitcast.146), kind=kOutput, calls=%fused_computation.71 | convolution fusion | flops 1312768000 | bytes 9113600 | tf_op jit(solution)/shard_map/dot_general | solution.py:117
  174.7 1.0 copy-done.19
  175.7 1.5 convolution_convert_fusion.1
  177.2 4.9 %all-to-all-start = ((bf16[8,64,512]{2,1,0:T(8,128)(2,1)}), bf16[8,64,512]{2,1,0:T(8,128)(2,1)}, u32[]{:S(2)}, u32[]{:S(2)}) async-start(bf16[8,64,512]{2,1,0:T(8,128)(2,1)} %convolution_convert_fusion.1), calls=%async_computation | async-start | bytes 1048576 | tf_op jit(solution)/shard_map/all_to_all | solution.py:193
  182.2 4.5 %fusion.51 = f32[800,512]{1,0:T(8,128)} fusion(bf16[800,1600]{1,0:T(8,128)(2,1)S(1)} %get-tuple-element.8, bf16[1600,512]{1,0:T(8,128)(2,1)} %bitcast.144), kind=kOutput, calls=%fused_computation.123 | convolution fusion | flops 1310720000 | bytes 5836800 | tf_op jit(solution)/shard_map/dot_general | solution.py:117
  186.6 2.8 %fusion.52 = f32[800,512]{1,0:T(8,128)} fusion(bf16[800,1600]{1,0:T(8,128)(2,1)S(1)} %copy-done.27, bf16[1600,512]{1,0:T(8,128)(2,1)S(1)} %bitcast.142), kind=kOutput, calls=%fused_computation.124 | convolution fusion | flops 1310720000 | bytes 5836800 | tf_op jit(solution)/shard_map/dot_general | solution.py:117
  189.5 1.5 convolution_convert_fusion
  191.0 2.6 %all-to-all-done = bf16[8,64,512]{2,1,0:T(8,128)(2,1)} async-done(((bf16[8,64,512]{2,1,0:T(8,128)(2,1)}), bf16[8,64,512]{2,1,0:T(8,128)(2,1)}, u32[]{:S(2)}, u32[]{:S(2)}) %all-to-all-start) | async-done | bytes 524320 | tf_op jit(solution)/shard_map/all_to_all | solution.py:193
  193.6 6.7 %all-to-all-start.1 = ((bf16[8,64,512]{2,1,0:T(8,128)(2,1)}), bf16[8,64,512]{2,1,0:T(8,128)(2,1)S(1)}, u32[]{:S(2)}, u32[]{:S(2)}) async-start(bf16[8,64,512]{2,1,0:T(8,128)(2,1)} %bitcast.151), calls=%async_computation.1 | async-start | bytes 1048576 | tf_op jit(solution)/shard_map/all_to_all | solution.py:193
  200.3 3.5 %fusion.48 = (bf16[800,512]{1,0:T(8,128)(2,1)}, f32[800,512]{1,0:T(8,128)S(1)}) fusion(bf16[800,512]{1,0:T(8,128)(2,1)} %collective-permute-done.17, f32[800,512]{1,0:T(8,128)S(1)} %copy-done.17, f32[800,512]{1,0:T(8,128)} %fusion.52, bf16[800,512]{1,0:T(8,128)(2,1)} %copy-done.19, bf16[512,512]{1,0:T(8,128)(2,1)S(1)} %bitcast.137), kind=kOutput, calls=%fused_computation.120 | convolution fusion | flops 421478400 | bytes 7897088 | tf_op jit(solution)/shard_map/dot_general | solution.py:117
  203.9 1.2 convert_reduce_fusion.1
  205.9 6.4 %all-to-all-done.1 = bf16[8,64,512]{2,1,0:T(8,128)(2,1)S(1)} async-done(((bf16[8,64,512]{2,1,0:T(8,128)(2,1)}), bf16[8,64,512]{2,1,0:T(8,128)(2,1)S(1)}, u32[]{:S(2)}, u32[]{:S(2)}) %all-to-all-start.1) | async-done | bytes 524320 | tf_op jit(solution)/shard_map/all_to_all | solution.py:193
  212.6 1.1 fusion.35
  213.9 1.4 fusion.1
  216.4 4.6 %all-to-all-start.2 = ((bf16[8,32,512]{2,1,0:T(8,128)(2,1)}), bf16[8,32,512]{2,1,0:T(8,128)(2,1)S(1)}, u32[]{:S(2)}, u32[]{:S(2)}) async-start(bf16[8,32,512]{2,1,0:T(8,128)(2,1)} %pad_maximum_fusion.2), calls=%async_computation.2 | async-start | bytes 524288 | tf_op jit(solution)/shard_map/all_to_all | solution.py:193
  221.1 1.3 pad_maximum_fusion
  223.0 6.3 %all-to-all-done.2 = bf16[8,32,512]{2,1,0:T(8,128)(2,1)S(1)} async-done(((bf16[8,32,512]{2,1,0:T(8,128)(2,1)}), bf16[8,32,512]{2,1,0:T(8,128)(2,1)S(1)}, u32[]{:S(2)}, u32[]{:S(2)}) %all-to-all-start.2) | async-done | bytes 262176 | tf_op jit(solution)/shard_map/all_to_all | solution.py:193
  229.4 1.3 convolution_subtract_fusion.1
  (103 shorter events, 14.4 us)
Async XLA Ops:
  0.6 4.3 %copy-start.28 = (s32[1,25,2]{1,2,0:T(2,128)S(1)}, s32[1,25,2]{1,2,0:T(2,128)}, u32[]{:S(2)}) copy-start(s32[1,25,2]{1,2,0:T(2,128)} %param.11) | copy-start | bytes 604
  4.2 2.7 %copy-start.3 = (f32[1,512,512]{2,1,0:T(8,128)S(1)}, f32[1,512,512]{2,1,0:T(8,128)}, u32[]{:S(2)}) copy-start(f32[1,512,512]{2,1,0:T(8,128)} %param.10) | copy-start | bytes 3145732
  4.2 2.7 %copy-start.5 = (bf16[1,800,512]{2,1,0:T(8,128)(2,1)S(1)}, bf16[1,800,512]{2,1,0:T(8,128)(2,1)}, u32[]{:S(2)}) copy-start(bf16[1,800,512]{2,1,0:T(8,128)(2,1)} %param.9) | copy-start | bytes 2457604
  6.9 1.1 copy-start.6
  8.1 0.8 copy-start.22
  9.8 24.1 %collective-permute-start = (bf16[864,512]{1,0:T(8,128)(2,1)}, bf16[864,512]{1,0:T(8,128)(2,1)}, u32[]{:S(2)}, u32[]{:S(2)}) collective-permute-start(bf16[864,512]{1,0:T(8,128)(2,1)} %maximum_maximum_fusion), channel_id=1, source_target_pairs={{0,4},{2,6},{4,8},{6,10},{8,12},{10,14},{1,5},{3,7},{5,9},{7,11},{... | collective-permute-start | bytes 2654216 | tf_op jit(solution)/shard_map/ppermute | solution.py:171
  15.8 23.3 %collective-permute-start.1 = (bf16[864,512]{1,0:T(8,128)(2,1)}, bf16[864,512]{1,0:T(8,128)(2,1)}, u32[]{:S(2)}, u32[]{:S(2)}) collective-permute-start(bf16[864,512]{1,0:T(8,128)(2,1)} %maximum_maximum_fusion), channel_id=1, source_target_pairs={{4,0},{6,2},{8,4},{10,6},{12,8},{14,10},{5,1},{7,3},{9,5},{11,7},{... | collective-permute-start | bytes 2654216 | tf_op jit(solution)/shard_map/ppermute | solution.py:176
  17.1 3.9 %copy-start = (f32[800,3200]{1,0:T(8,128)S(1)}, f32[800,3200]{1,0:T(8,128)}, u32[]{:S(2)}) copy-start(f32[800,3200]{1,0:T(8,128)} %sigma_ref.1) | copy-start | bytes 30720004
  21.0 4.8 %copy-start.25 = (s32[2,27,1]{1,2,0:T(1,128)S(1)}, s32[2,27,1]{1,2,0:T(1,128)}, u32[]{:S(2)}) copy-start(s32[2,27,1]{1,2,0:T(1,128)} %param.15) | copy-start | bytes 652
  21.0 19.4 %copy-start.1 = (f32[2,256,256]{2,1,0:T(8,128)S(1)}, f32[2,256,256]{2,1,0:T(8,128)}, u32[]{:S(2)}) copy-start(f32[2,256,256]{2,1,0:T(8,128)} %param.14) | copy-start | bytes 1572868
  21.0 19.4 %copy-start.7 = (bf16[2,800,256]{2,1,0:T(8,128)(2,1)S(1)}, bf16[2,800,256]{2,1,0:T(8,128)(2,1)}, u32[]{:S(2)}) copy-start(bf16[2,800,256]{2,1,0:T(8,128)(2,1)} %param.12) | copy-start | bytes 2457604
  24.3 71.0 %collective-permute-start.7 = (bf16[800,1600]{1,0:T(8,128)(2,1)}, bf16[800,1600]{1,0:T(8,128)(2,1)}, u32[]{:S(2)}, u32[]{:S(2)}) collective-permute-start(bf16[800,1600]{1,0:T(8,128)(2,1)} %get-tuple-element.9), channel_id=1, source_target_pairs={{0,2},{2,0},{4,6},{6,4},{8,10},{10,8},{12,14},{14,12},{1,3},{3,1},... | collective-permute-start | bytes 7680008 | tf_op jit(solution)/shard_map/ppermute | solution.py:226
  33.9 10.0 %collective-permute-start.4 = (bf16[864,512]{1,0:T(8,128)(2,1)}, bf16[864,512]{1,0:T(8,128)(2,1)}, u32[]{:S(2)}, u32[]{:S(2)}) collective-permute-start(bf16[864,512]{1,0:T(8,128)(2,1)} %collective-permute-done), channel_id=1, source_target_pairs={{4,8},{6,10},{8,12},{10,14},{5,9},{7,11},{9,13},{11,15},{20,24},{2... | collective-permute-start | bytes 2654216 | tf_op jit(solution)/shard_map/ppermute | solution.py:171
  39.1 22.5 %collective-permute-start.2 = (bf16[864,512]{1,0:T(8,128)(2,1)}, bf16[864,512]{1,0:T(8,128)(2,1)}, u32[]{:S(2)}, u32[]{:S(2)}) collective-permute-start(bf16[864,512]{1,0:T(8,128)(2,1)} %collective-permute-done.1), channel_id=1, source_target_pairs={{4,0},{6,2},{8,4},{10,6},{5,1},{7,3},{9,5},{11,7},{20,16},{22,18},... | collective-permute-start | bytes 2654216 | tf_op jit(solution)/shard_map/ppermute | solution.py:176
  42.3 0.7 copy-start.10
  42.3 1.7 copy-start.12
  61.6 23.4 %collective-permute-start.12 = (bf16[800,512]{1,0:T(8,128)(2,1)}, bf16[800,512]{1,0:T(8,128)(2,1)}, u32[]{:S(2)}, u32[]{:S(2)}) collective-permute-start(bf16[800,512]{1,0:T(8,128)(2,1)} %pad_maximum_fusion.1), channel_id=1, source_target_pairs={{4,0},{6,2},{8,4},{10,6},{12,8},{14,10},{5,1},{7,3},{9,5},{11,7},{... | collective-permute-start | bytes 2457608 | tf_op jit(solution)/shard_map/ppermute | solution.py:176
  62.9 41.1 %collective-permute-start.3 = (bf16[864,512]{1,0:T(8,128)(2,1)}, bf16[864,512]{1,0:T(8,128)(2,1)}, u32[]{:S(2)}, u32[]{:S(2)}) collective-permute-start(bf16[864,512]{1,0:T(8,128)(2,1)} %collective-permute-done.2), channel_id=1, source_target_pairs={{4,0},{6,2},{5,1},{7,3},{20,16},{22,18},{21,17},{23,19}} | collective-permute-start | bytes 2654216 | tf_op jit(solution)/shard_map/ppermute | solution.py:176
  64.2 31.3 %collective-permute-start.11 = (bf16[800,512]{1,0:T(8,128)(2,1)}, bf16[800,512]{1,0:T(8,128)(2,1)}, u32[]{:S(2)}, u32[]{:S(2)}) collective-permute-start(bf16[800,512]{1,0:T(8,128)(2,1)} %pad_maximum_fusion.1), channel_id=1, source_target_pairs={{0,4},{2,6},{4,8},{6,10},{8,12},{10,14},{1,5},{3,7},{5,9},{7,11},{... | collective-permute-start | bytes 2457608 | tf_op jit(solution)/shard_map/ppermute | solution.py:171
  70.5 49.0 %collective-permute-start.5 = (bf16[864,512]{1,0:T(8,128)(2,1)}, bf16[864,512]{1,0:T(8,128)(2,1)}, u32[]{:S(2)}, u32[]{:S(2)}) collective-permute-start(bf16[864,512]{1,0:T(8,128)(2,1)} %collective-permute-done.4), channel_id=1, source_target_pairs={{8,12},{10,14},{9,13},{11,15},{24,28},{26,30},{25,29},{27,31}} | collective-permute-start | bytes 2654216 | tf_op jit(solution)/shard_map/ppermute | solution.py:171
  85.0 33.3 %collective-permute-start.13 = (bf16[800,512]{1,0:T(8,128)(2,1)}, bf16[800,512]{1,0:T(8,128)(2,1)}, u32[]{:S(2)}, u32[]{:S(2)}) collective-permute-start(bf16[800,512]{1,0:T(8,128)(2,1)} %collective-permute-done.12), channel_id=1, source_target_pairs={{4,0},{6,2},{8,4},{10,6},{5,1},{7,3},{9,5},{11,7},{20,16},{22,18},... | collective-permute-start | bytes 2457608 | tf_op jit(solution)/shard_map/ppermute | solution.py:176
  94.5 0.8 copy-start.23
  95.4 56.8 %collective-permute-start.6 = (bf16[800,1600]{1,0:T(8,128)(2,1)S(1)}, bf16[800,1600]{1,0:T(8,128)(2,1)S(1)}, u32[]{:S(2)}, u32[]{:S(2)}) collective-permute-start(bf16[800,1600]{1,0:T(8,128)(2,1)S(1)} %get-tuple-element.8), channel_id=1, source_target_pairs={{0,1},{1,0},{2,3},{3,2},{4,5},{5,4},{6,7},{7,6},{8,9},{9,8},{10,11... | collective-permute-start | bytes 7680008 | tf_op jit(solution)/shard_map/ppermute | solution.py:227
  95.5 53.5 %collective-permute-start.8 = (bf16[800,1600]{1,0:T(8,128)(2,1)}, bf16[800,1600]{1,0:T(8,128)(2,1)S(1)}, u32[]{:S(2)}, u32[]{:S(2)}) collective-permute-start(bf16[800,1600]{1,0:T(8,128)(2,1)} %collective-permute-done.7), channel_id=1, source_target_pairs={{0,1},{1,0},{2,3},{3,2},{4,5},{5,4},{6,7},{7,6},{8,9},{9,8},{10,11... | collective-permute-start | bytes 7680008 | tf_op jit(solution)/shard_map/ppermute | solution.py:228
  103.9 18.7 %collective-permute-start.15 = (bf16[800,512]{1,0:T(8,128)(2,1)}, bf16[800,512]{1,0:T(8,128)(2,1)S(1)}, u32[]{:S(2)}, u32[]{:S(2)}) collective-permute-start(bf16[800,512]{1,0:T(8,128)(2,1)} %collective-permute-done.11), channel_id=1, source_target_pairs={{4,8},{6,10},{8,12},{10,14},{5,9},{7,11},{9,13},{11,15},{20,24},{2... | collective-permute-start | bytes 2457608 | tf_op jit(solution)/shard_map/ppermute | solution.py:171
  118.3 19.2 %collective-permute-start.14 = (bf16[800,512]{1,0:T(8,128)(2,1)}, bf16[800,512]{1,0:T(8,128)(2,1)S(1)}, u32[]{:S(2)}, u32[]{:S(2)}) collective-permute-start(bf16[800,512]{1,0:T(8,128)(2,1)} %collective-permute-done.13), channel_id=1, source_target_pairs={{4,0},{6,2},{5,1},{7,3},{20,16},{22,18},{21,17},{23,19}} | collective-permute-start | bytes 2457608 | tf_op jit(solution)/shard_map/ppermute | solution.py:176
  121.1 6.4 %collective-permute-start.10 = (bf16[4,64,512]{2,1,0:T(8,128)(2,1)S(1)}, bf16[4,64,512]{2,1,0:T(8,128)(2,1)S(1)}, u32[]{:S(2)}, u32[]{:S(2)}) collective-permute-start(bf16[4,64,512]{2,1,0:T(8,128)(2,1)S(1)} %get-tuple-element.14), channel_id=1, source_target_pairs={{0,2},{2,0},{4,6},{6,4},{8,10},{10,8},{12,14},{14,12},{1,3},{3,1},... | collective-permute-start | bytes 786440 | tf_op jit(solution)/shard_map/ppermute | solution.py:234
  122.7 16.5 %collective-permute-start.16 = (bf16[800,512]{1,0:T(8,128)(2,1)S(1)}, bf16[800,512]{1,0:T(8,128)(2,1)S(1)}, u32[]{:S(2)}, u32[]{:S(2)}) collective-permute-start(bf16[800,512]{1,0:T(8,128)(2,1)S(1)} %collective-permute-done.15), channel_id=1, source_target_pairs={{8,12},{10,14},{9,13},{11,15},{24,28},{26,30},{25,29},{27,31}} | collective-permute-start | bytes 2457608 | tf_op jit(solution)/shard_map/ppermute | solution.py:171
  141.0 4.6 %copy-start.16 = (bf16[2,800,512]{2,1,0:T(8,128)(2,1)}, bf16[2,800,512]{2,1,0:T(8,128)(2,1)S(1)}, u32[]{:S(2)}) copy-start(bf16[2,800,512]{2,1,0:T(8,128)(2,1)S(1)} %get-tuple-element.16) | copy-start | bytes 4915204
  141.0 12.9 %copy-start.14 = (bf16[2,800,512]{2,1,0:T(8,128)(2,1)}, bf16[2,800,512]{2,1,0:T(8,128)(2,1)S(1)}, u32[]{:S(2)}) copy-start(bf16[2,800,512]{2,1,0:T(8,128)(2,1)S(1)} %get-tuple-element.15) | copy-start | bytes 4915204
  150.7 21.2 %collective-permute-start.9 = (bf16[800,512]{1,0:T(8,128)(2,1)S(1)}, bf16[800,512]{1,0:T(8,128)(2,1)S(1)}, u32[]{:S(2)}, u32[]{:S(2)}) collective-permute-start(bf16[800,512]{1,0:T(8,128)(2,1)S(1)} %add_convert_fusion.2), channel_id=1, source_target_pairs={{0,2},{2,0},{4,6},{6,4},{8,10},{10,8},{12,14},{14,12},{1,3},{3,1},... | collective-permute-start | bytes 2457608 | tf_op jit(solution)/shard_map/ppermute | solution.py:246
  152.2 1.6 copy-start.26
  156.5 19.2 %copy-start.18 = (bf16[512,800]{1,0:T(8,128)(2,1)S(1)}, bf16[512,800]{1,0:T(8,128)(2,1)}, u32[]{:S(2)}) copy-start(bf16[512,800]{1,0:T(8,128)(2,1)} %copy.21) | copy-start | bytes 2457604
  156.5 43.8 %collective-permute-start.17 = (bf16[800,512]{1,0:T(8,128)(2,1)}, bf16[800,512]{1,0:T(8,128)(2,1)}, u32[]{:S(2)}, u32[]{:S(2)}) collective-permute-start(bf16[800,512]{1,0:T(8,128)(2,1)} %add_convert_fusion), channel_id=1, source_target_pairs={{0,2},{2,0},{4,6},{6,4},{8,10},{10,8},{12,14},{14,12},{1,3},{3,1},... | collective-permute-start | bytes 2457608 | tf_op jit(solution)/shard_map/ppermute | solution.py:246
  174.7 1.0 copy-start.19
  177.2 16.3 %all-to-all-start = ((bf16[8,64,512]{2,1,0:T(8,128)(2,1)}), bf16[8,64,512]{2,1,0:T(8,128)(2,1)}, u32[]{:S(2)}, u32[]{:S(2)}) async-start(bf16[8,64,512]{2,1,0:T(8,128)(2,1)} %convolution_convert_fusion.1), calls=%async_computation | async-start | bytes 1048576 | tf_op jit(solution)/shard_map/all_to_all | solution.py:193
  182.1 4.5 %copy-start.15 = (bf16[2,800,512]{2,1,0:T(8,128)(2,1)S(1)}, bf16[2,800,512]{2,1,0:T(8,128)(2,1)}, u32[]{:S(2)}) copy-start(bf16[2,800,512]{2,1,0:T(8,128)(2,1)} %copy-done.14) | copy-start | bytes 4915204
  182.1 4.5 %copy-start.27 = (bf16[800,1600]{1,0:T(8,128)(2,1)S(1)}, bf16[800,1600]{1,0:T(8,128)(2,1)}, u32[]{:S(2)}) copy-start(bf16[800,1600]{1,0:T(8,128)(2,1)} %copy-done.26) | copy-start | bytes 7680004
  186.6 2.8 %copy-start.11 = (bf16[800,256]{1,0:T(8,128)(2,1)S(1)}, bf16[800,256]{1,0:T(8,128)(2,1)}, u32[]{:S(2)}) copy-start(bf16[800,256]{1,0:T(8,128)(2,1)} %copy-done.10) | copy-start | bytes 1228804
  186.6 2.8 %copy-start.13 = (bf16[800,256]{1,0:T(8,128)(2,1)S(1)}, bf16[800,256]{1,0:T(8,128)(2,1)}, u32[]{:S(2)}) copy-start(bf16[800,256]{1,0:T(8,128)(2,1)} %copy-done.12) | copy-start | bytes 1228804
  186.6 2.8 %copy-start.20 = (bf16[800,512]{1,0:T(8,128)(2,1)S(1)}, bf16[800,512]{1,0:T(8,128)(2,1)}, u32[]{:S(2)}) copy-start(bf16[800,512]{1,0:T(8,128)(2,1)} %copy-done.19) | copy-start | bytes 2457604
  189.5 10.9 %copy-start.17 = (f32[800,512]{1,0:T(8,128)S(1)}, f32[800,512]{1,0:T(8,128)}, u32[]{:S(2)}) copy-start(f32[800,512]{1,0:T(8,128)} %fusion.51) | copy-start | bytes 4915204
  193.6 18.8 %all-to-all-start.1 = ((bf16[8,64,512]{2,1,0:T(8,128)(2,1)}), bf16[8,64,512]{2,1,0:T(8,128)(2,1)S(1)}, u32[]{:S(2)}, u32[]{:S(2)}) async-start(bf16[8,64,512]{2,1,0:T(8,128)(2,1)} %bitcast.151), calls=%async_computation.1 | async-start | bytes 1048576 | tf_op jit(solution)/shard_map/all_to_all | solution.py:193
  203.8 1.4 copy-start.4
  205.2 8.6 %copy-start.24 = (bf16[256,64]{1,0:T(8,128)(2,1)S(1)}, bf16[256,64]{1,0:T(8,128)(2,1)}, u32[]{:S(2)}) copy-start(bf16[256,64]{1,0:T(8,128)(2,1)} %copy.24) | copy-start | bytes 98308
  205.9 9.5 %copy-start.21 = (f32[64,512]{1,0:T(8,128)}, f32[64,512]{1,0:T(8,128)S(1)}, u32[]{:S(2)}) copy-start(f32[64,512]{1,0:T(8,128)S(1)} %convolution_add_fusion.2) | copy-start | bytes 393220
  212.4 3.0 %copy-start.8 = (bf16[800,512]{1,0:T(8,128)(2,1)S(1)}, bf16[800,512]{1,0:T(8,128)(2,1)}, u32[]{:S(2)}) copy-start(bf16[800,512]{1,0:T(8,128)(2,1)} %get-tuple-element.35) | copy-start | bytes 2457604
  212.4 3.0 %copy-start.9 = (bf16[256,800]{1,0:T(8,128)(2,1)S(1)}, bf16[256,800]{1,0:T(8,128)(2,1)}, u32[]{:S(2)}) copy-start(bf16[256,800]{1,0:T(8,128)(2,1)} %copy.23) | copy-start | bytes 1228804
  216.4 12.9 %all-to-all-start.2 = ((bf16[8,32,512]{2,1,0:T(8,128)(2,1)}), bf16[8,32,512]{2,1,0:T(8,128)(2,1)S(1)}, u32[]{:S(2)}, u32[]{:S(2)}) async-start(bf16[8,32,512]{2,1,0:T(8,128)(2,1)} %pad_maximum_fusion.2), calls=%async_computation.2 | async-start | bytes 524288 | tf_op jit(solution)/shard_map/all_to_all | solution.py:193
  221.1 8.3 %copy-start.2 = (f32[2,256,256]{2,1,0:T(8,128)S(1)}, f32[2,256,256]{2,1,0:T(8,128)}, u32[]{:S(2)}) copy-start(f32[2,256,256]{2,1,0:T(8,128)} %param.14) | copy-start | bytes 1572868

commit v3 on v2

--- a/solution.py
+++ b/solution.py
@@ -162,31 +162,24 @@
     )(side.reshape(1), sigma)
 
 
-def line_gather(block, layers, layer, after=None):
-    up, down = [], []
-    if after is not None:
-        block, _ = lax.optimization_barrier((block, after))
-    held_up = held_down = block
-    for step in range(1, layers):
-        held_up = lax.ppermute(
-            held_up,
-            "prow",
-            [(2 * s + x, 2 * s + 2 + x) for s in range(step - 1, layers - 1) for x in (0, 1)],
-        )
-        held_down = lax.ppermute(
-            held_down,
-            "prow",
-            [(2 * s + x, 2 * s - 2 + x) for s in range(1, layers - step + 1) for x in (0, 1)],
-        )
-        up.append(held_up)
-        down.append(held_down)
+def line_hop(held, layers, step):
+    up = [(2 * s + x, 2 * s + 2 + x) for s in range(step - 1, layers - 1) for x in (0, 1)]
+    down = [(2 * s + x, 2 * s - 2 + x) for s in range(1, layers - step + 1) for x in (0, 1)]
+    return lax.ppermute(held[0], "prow", up), lax.ppermute(held[1], "prow", down)
+
+
+def line_order(block, hops, layers, layer):
     gathered = jnp.zeros((layers,) + block.shape, block.dtype)
     gathered = lax.dynamic_update_slice(gathered, block[None], (layer, 0, 0))
     for back in range(1, layers):
-        piece = jnp.where(layer >= back, up[back - 1], down[layers - back - 1])
+        piece = jnp.where(layer >= back, hops[back - 1][0], hops[layers - back - 1][1])
         at = lax.rem(layer - back + layers, layers)
         gathered = lax.dynamic_update_slice(gathered, piece[None], (at, 0, 0))
-    return gathered, (up[1], down[1])
+    return gathered
+
+
+def tie(values, after):
+    return lax.optimization_barrier((values, after))[0]
 
 
 def scatter_sum(parts):
@@ -227,55 +220,63 @@
     kept_sibling = lax.ppermute(kept, "pcol", swap_core)
     taken_sibling = lax.ppermute(taken, "pcol", swap_core)
 
-    joined, late = line_gather(jnp.concatenate([own_one, own_sep]), layers, layer)
-    all_one = joined[:, :rows]
-    all_two, _ = line_gather(own_two, layers, layer, late)
+    def root_parts(gathered):
+        width = gathered.shape[2]
+        near = lax.dynamic_slice_in_dim(gathered, core * half, half, 0).reshape(-1, width)
+        far = lax.dynamic_slice_in_dim(gathered, (1 - core) * half, half, 0).reshape(-1, width)
+        away = (dot(taken, near) + dot(taken_sibling, far)).astype(jnp.bfloat16)
+        return near, far, away
+
+    def root_total(near, far, arrived):
+        return dot(kept, near) + dot(kept_sibling, far) + arrived.astype(jnp.float32)
+
+    first = jnp.concatenate([own_one, own_sep])
+    hops_one = [line_hop((first, first), layers, 1)]
+    second = tie(own_two, hops_one[0])
+    hops_two = []
+    held = (second, second)
+    for step in range(2, layers):
+        hops_one.append(line_hop(hops_one[-1], layers, step))
+        held = line_hop(held, layers, step - 1)
+        hops_two.append(held)
+    joined = line_order(first, hops_one, layers, layer)
+    near_one, far_one, away_one = root_parts(joined[:, :rows])
+    arrived_one = lax.ppermute(away_one, "prow", swap_side)
     sep_here = joined[:, rows:]
     sep_there = lax.ppermute(sep_here, "prow", swap_side)
+    hops_two.append(line_hop(tie(held, away_one), layers, layers - 1))
+
+    product_one = root_total(near_one, far_one, arrived_one)
+    short_one = product_one.astype(jnp.bfloat16)
+    packed = dot_rows(short_one, jnp.concatenate([own_one, own_two], axis=1)).astype(jnp.bfloat16)
+    packed = packed.reshape(devices, sep_rows, -1)
     all_sep = jnp.where(
         side == 0,
         jnp.stack([sep_here, sep_there], axis=1),
         jnp.stack([sep_there, sep_here], axis=1),
     ).reshape(sep_width, 2 * leaf_width)
-
-    def root_product(gathered):
-        width = gathered.shape[2]
-        near = lax.dynamic_slice_in_dim(gathered, core * half, half, 0).reshape(-1, width)
-        far = lax.dynamic_slice_in_dim(gathered, (1 - core) * half, half, 0).reshape(-1, width)
-        away = dot(taken, near) + dot(taken_sibling, far)
-        arrived = lax.ppermute(away.astype(jnp.bfloat16), "prow", swap_side)
-        return dot(kept, near) + dot(kept_sibling, far) + arrived.astype(jnp.float32)
-
-    product_one = root_product(all_one)
-    short_one = product_one.astype(jnp.bfloat16)
-    gram_one = dot_rows(own_one, short_one).reshape(devices, sep_rows, sep_width)
-    sum_one = scatter_sum(gram_one)
+    hops_two[-1] = tie(hops_two[-1], packed)
+    sums = scatter_sum(packed)
     weight_cols = lax.dynamic_slice_in_dim(weights_one[0], row_index * sep_rows, sep_rows, 1)
     diag_rows = (
         lax.dot_general(
             weight_cols, weights_one[0], (((0,), (0,)), ((), ())), precision=HIGHEST
         )
-        + sum_one
-    )
-
-    cross = dot_rows(short_one, own_two).reshape(devices, sep_rows, 2 * leaf_width)
-    product_two = root_product(all_two)
+        + sums[:, :sep_width]
+    )
+    sep_two = sums[:, sep_width:] - dot(diag_rows.astype(jnp.bfloat16), all_sep)
+    short_sep = sep_two.astype(jnp.bfloat16)
+
+    near_two, far_two, away_two = root_parts(line_order(own_two, hops_two, layers, layer))
+    arrived_two = lax.ppermute(away_two, "prow", swap_side)
+    product_two = root_total(near_two, far_two, arrived_two)
     two_root = dot(short_one, all_sep) - product_two
     short_two = two_root.astype(jnp.bfloat16)
     leaf_gram = [
-        dot_rows(normal_root[b], short_two[:, b * leaf_width : (b + 1) * leaf_width]).reshape(
-            devices, leaf_rows, leaf_width
-        )
-        for b in range(2)
-    ]
-    sums = scatter_sum(cross)
-    sep_two = sums - dot(diag_rows.astype(jnp.bfloat16), all_sep)
-    short_sep = sep_two.astype(jnp.bfloat16)
-    leaf_gram = [
-        leaf_gram[b]
-        + dot_rows(normal_sep[b], short_sep[:, b * leaf_width : (b + 1) * leaf_width]).reshape(
-            devices, leaf_rows, leaf_width
-        )
+        (
+            dot_rows(normal_root[b], short_two[:, b * leaf_width : (b + 1) * leaf_width])
+            + dot_rows(normal_sep[b], short_sep[:, b * leaf_width : (b + 1) * leaf_width])
+        ).reshape(devices, leaf_rows, leaf_width)
         for b in range(2)
     ]
     leaf_sum = scatter_sum(jnp.concatenate(leaf_gram, axis=2))

time: 232 us -> 202 us (0.87)
  waiting for transfers between devices: 103 us -> 84.6 us
  matrix products: 41.2 us -> 32.4 us
  other arithmetic: 14.2 us -> 19.1 us
  local copies, waits for them, and re-layouts: 21.1 us -> 16.3 us
  starting transfers between devices: 46.8 us -> 44 us
    all_to_all x3 -> x2, waiting for transfers between devices: 15.2 us -> 5.12 us  [scatter_sum(): moved = lax.all_to_all(parts.astype(jnp.bfloat16), 'prow', 0, 0, tiled=True)]
    dot_general x6 -> x0, local copies, waits for them, and re-layouts: 8.58 us -> none  [dot_rows(): lax.dot_general(left, right, (((0,), (0,)), ((), ())), preferred_element_...]
    all_to_all x3 -> x2, starting transfers between devices: 16.3 us -> 9.91 us  [scatter_sum(): moved = lax.all_to_all(parts.astype(jnp.bfloat16), 'prow', 0, 0, tiled=True)]
    ppermute x14, waiting for transfers between devices: 85.3 us -> 79.5 us  [the longest x6 56.8 us: line_hop(): lax.ppermute(held[1], 'prow', down)]
    dot_general x10, matrix products: 27.7 us -> 21.9 us  [dot(): return jnp.dot(left, right, preferred_element_type=jnp.float32)]
    ppermute x14, starting transfers between devices: 26.9 us -> 30 us  [the longest x6 17.3 us: line_hop(): lax.ppermute(held[0], 'prow', up)]
    dot_general x6 -> x5, matrix products: 6.05 us -> 3.34 us  [dot_rows(): lax.dot_general(left, right, (((0,), (0,)), ((), ())), preferred_element_...]
    dynamic_update_slice x7 -> x8, other arithmetic: 7.51 us -> 10.2 us  [the longest x6 10.1 us: line_order(): gathered = lax.dynamic_update_slice(gathered, piece[None], (at, 0, 0))]
  transfers between devices with their start and end apart: 21 -> 20, of which waited for: 12 -> 9; matrix products, arithmetic and copies ran while one was open for 24% -> 28% of each run, Pallas kernels for 1% -> 0%
where the time goes in v3:
time: 202 us; the launch traced here: 201 us
  waiting for transfers between devices  84.6 us (42%)
  starting transfers between devices  44 us (22%)
  matrix products  32.4 us (16%)
  other arithmetic  19.1 us (9%)
  local copies, waits for them, and re-layouts  16.3 us (8%)
  Pallas kernels  3.32 us (2%)
    ppermute x6, waiting for transfers between devices, line_hop(): lax.ppermute(held[1], 'prow', down)  56.8 us
    dot_general x10, matrix products, dot(): return jnp.dot(left, right, preferred_element_type=jnp.float32)  21.9 us
    ppermute x6, starting transfers between devices, line_hop(): lax.ppermute(held[0], 'prow', up)  17.3 us
    dynamic_update_slice x6, other arithmetic, line_order(): gathered = lax.dynamic_update_slice(gathered, piece[None], (at, 0, 0))  10.1 us
    all_to_all x2, starting transfers between devices, scatter_sum(): moved = lax.all_to_all(parts.astype(jnp.bfloat16), 'prow', 0, 0, tiled=True)  9.91 us
    ppermute x6, waiting for transfers between devices, line_hop(): lax.ppermute(held[0], 'prow', up)  8.57 us
    ppermute x6, starting transfers between devices, line_hop(): lax.ppermute(held[1], 'prow', down)  7.88 us
    ppermute x1, waiting for transfers between devices, on_pairs(): arrived_one = lax.ppermute(away_one, 'prow', swap_side)  7.12 us
  transfers between devices with their start and end apart: 20, of which 9 were waited for; matrix products, arithmetic and copies ran while one was open for 28% of the time, Pallas kernels for 0%

profile of v3, /device:TPU:0, one launch (start us, length us, event | category | flops | bytes accessed | tf_op | source)
XLA Modules:
  0.0 201.1 jit_solution(606977506617601729)
XLA Ops:
  0.6 3.9 %copy-done = f32[800,3200]{1,0:T(8,128)S(1)} copy-done((f32[800,3200]{1,0:T(8,128)S(1)}, f32[800,3200]{1,0:T(8,128)}, u32[]{:S(2)}) %copy-start) | copy-done | bytes 10240024
  4.6 3.3 %shard_map.119 = (bf16[800,1600]{1,0:T(8,128)(2,1)S(1)}, bf16[800,1600]{1,0:T(8,128)(2,1)}) custom-call(s32[1]{0:T(128)} %bitcast.side_ref, f32[800,3200]{1,0:T(8,128)S(1)} %copy-done), custom_call_target="tpu_custom_call" | custom-call | bytes 15360000 | tf_op jit(solution)/shard_map/pallas_call | solution.py:149
  7.9 2.9 %collective-permute-start.7 = (bf16[800,1600]{1,0:T(8,128)(2,1)}, bf16[800,1600]{1,0:T(8,128)(2,1)}, u32[]{:S(2)}, u32[]{:S(2)}) collective-permute-start(bf16[800,1600]{1,0:T(8,128)(2,1)} %get-tuple-element.13), channel_id=1, source_target_pairs={{0,2},{2,0},{4,6},{6,4},{8,10},{10,8},{12,14},{14,12},{1,3},{3,1},... | collective-permute-start | bytes 7680008 | tf_op jit(solution)/shard_map/ppermute | solution.py:219
  11.4 1.8 broadcast_in_dim.46
  13.2 3.2 %convert_element_type.101 = bf16[1,800,512]{2,1,0:T(8,128)(2,1)} reshape(bf16[800,2,256]{2,1,0:T(2,128)(2,1)} %broadcast_in_dim.46) | data formatting | bytes 1638400 | tf_op jit(solution)/shard_map/convert_element_type | solution.py:107
  16.4 2.5 %fusion.17 = f32[800,512]{1,0:T(8,128)S(1)} fusion(f32[1,512,512]{2,1,0:T(8,128)} %param.10, bf16[1,800,512]{2,1,0:T(8,128)(2,1)} %param.9, bf16[1,800,512]{2,1,0:T(8,128)(2,1)} %convert_element_type.101), kind=kOutput, calls=%fused_computation.47 | convolution fusion | flops 420364288 | bytes 4325376 | tf_op jit(solution)/shard_map/nrk,nkc->nrc/dot_general | solution.py:110
  18.9 0.6 add_convert_fusion.3
  20.4 1.3 collective-permute-start.1
  21.7 4.6 %collective-permute-start = (bf16[864,512]{1,0:T(8,128)(2,1)S(1)}, bf16[864,512]{1,0:T(8,128)(2,1)S(1)}, u32[]{:S(2)}, u32[]{:S(2)}) collective-permute-start(bf16[864,512]{1,0:T(8,128)(2,1)S(1)} %maximum_maximum_fusion), channel_id=1, source_target_pairs={{0,4},{2,6},{4,8},{6,10},{8,12},{10,14},{1,5},{3,7},{5,9},{7,11},{... | collective-permute-start | bytes 2654216 | tf_op jit(solution)/shard_map/ppermute | solution.py:168
  26.4 17.1 %collective-permute-done.1 = bf16[864,512]{1,0:T(8,128)(2,1)S(1)} collective-permute-done((bf16[864,512]{1,0:T(8,128)(2,1)S(1)}, bf16[864,512]{1,0:T(8,128)(2,1)S(1)}, u32[]{:S(2)}, u32[]{:S(2)}) %collective-permute-start.1) | collective-permute-done | bytes 884768 | tf_op jit(solution)/shard_map/ppermute | solution.py:168
  43.4 1.3 collective-permute-start.2
  45.0 0.4 fusion.20
  45.5 0.4 add_convert_fusion.1
  45.9 1.6 collective-permute-start.4
  47.6 18.1 %collective-permute-done.2 = bf16[864,512]{1,0:T(8,128)(2,1)} collective-permute-done((bf16[864,512]{1,0:T(8,128)(2,1)S(1)}, bf16[864,512]{1,0:T(8,128)(2,1)}, u32[]{:S(2)}, u32[]{:S(2)}) %collective-permute-start.2) | collective-permute-done | bytes 884768 | tf_op jit(solution)/shard_map/ppermute | solution.py:168
  65.7 1.3 collective-permute-start.3
  67.0 1.0 pad_maximum_fusion.1
  68.0 6.4 %collective-permute-start.11 = (bf16[800,512]{1,0:T(8,128)(2,1)}, bf16[800,512]{1,0:T(8,128)(2,1)}, u32[]{:S(2)}, u32[]{:S(2)}) collective-permute-start(bf16[800,512]{1,0:T(8,128)(2,1)} %pad_maximum_fusion.1), channel_id=1, source_target_pairs={{0,4},{2,6},{4,8},{6,10},{8,12},{10,14},{1,5},{3,7},{5,9},{7,11},{... | collective-permute-start | bytes 2457608 | tf_op jit(solution)/shard_map/ppermute | solution.py:168
  74.4 1.3 collective-permute-start.13
  75.8 1.6 collective-permute-start.5
  77.7 0.7 copy-done.10
  78.9 1.4 copy-done.1
  80.4 8.6 %collective-permute-done.11 = bf16[800,512]{1,0:T(8,128)(2,1)} collective-permute-done((bf16[800,512]{1,0:T(8,128)(2,1)}, bf16[800,512]{1,0:T(8,128)(2,1)}, u32[]{:S(2)}, u32[]{:S(2)}) %collective-permute-start.11) | collective-permute-done | bytes 819232 | tf_op jit(solution)/shard_map/ppermute | solution.py:168
  89.0 15.9 %collective-permute-done.13 = bf16[800,512]{1,0:T(8,128)(2,1)} collective-permute-done((bf16[800,512]{1,0:T(8,128)(2,1)}, bf16[800,512]{1,0:T(8,128)(2,1)}, u32[]{:S(2)}, u32[]{:S(2)}) %collective-permute-start.13) | collective-permute-done | bytes 819232 | tf_op jit(solution)/shard_map/ppermute | solution.py:168
  104.9 1.6 collective-permute-start.12
  106.4 1.3 collective-permute-start.14
  107.7 1.5 bitcast_dynamic-update-slice_fusion.2
  109.2 1.5 bitcast_dynamic-update-slice_fusion.1
  111.3 1.1 collective-permute-start.10
  112.7 3.4 %fusion.65 = f32[800,512]{1,0:T(8,128)S(1)} fusion(bf16[800,1600]{1,0:T(8,128)(2,1)} %collective-permute-done.7, bf16[1600,512]{1,0:T(8,128)(2,1)S(1)} %bitcast.112), kind=kOutput, calls=%fused_computation.124 | convolution fusion | flops 1310720000 | bytes 5836800 | tf_op jit(solution)/shard_map/dot_general | solution.py:117
  116.2 3.4 %add_convert_fusion.2 = bf16[800,512]{1,0:T(8,128)(2,1)S(1)} fusion(f32[800,512]{1,0:T(8,128)S(1)} %fusion.65, bf16[800,1600]{1,0:T(8,128)(2,1)} %collective-permute-done.8, bf16[1600,512]{1,0:T(8,128)(2,1)S(1)} %bitcast.106), kind=kOutput, calls=%fused_computation.13 | convolution fusion | flops 1311539200 | bytes 6656000 | tf_op jit(solution)/shard_map/dot_general | solution.py:117
  119.6 1.1 collective-permute-start.9
  120.6 1.6 fusion.63
  122.3 1.6 fusion.64
  124.0 1.7 collective-permute-done.14
  125.7 1.6 collective-permute-start.15
  127.3 1.5 collective-permute-start.16
  128.7 0.9 maximum_select_fusion
  129.6 7.1 %collective-permute-done.9 = bf16[800,512]{1,0:T(8,128)(2,1)S(1)} collective-permute-done((bf16[800,512]{1,0:T(8,128)(2,1)S(1)}, bf16[800,512]{1,0:T(8,128)(2,1)S(1)}, u32[]{:S(2)}, u32[]{:S(2)}) %collective-permute-start.9) | collective-permute-done | bytes 819232 | tf_op jit(solution)/shard_map/ppermute | solution.py:244
  136.7 1.7 negate_bitcast_fusion
  138.4 2.2 %fusion.6 = bf16[512,1024]{1,0:T(8,128)(2,1)} fusion(bf16[800,256]{1,0:T(8,128)(2,1)S(1)} %copy-done.12, bf16[800,256]{1,0:T(8,128)(2,1)S(1)} %copy-done.10, bf16[800,512]{1,0:T(8,128)(2,1)S(1)} %copy-done.6, bf16[800,512]{1,0:T(8,128)(2,1)S(1)} %get-tuple-element.20), kind=kOutput, calls=%fused_computation.17 | convolution fusion | flops 844300288 | bytes 3506176 | tf_op jit(solution)/shard_map/dot_general | solution.py:121
  140.6 4.3 %all-to-all-start = ((bf16[8,64,1024]{2,1,0:T(8,128)(2,1)}), bf16[8,64,1024]{2,1,0:T(8,128)(2,1)}, u32[]{:S(2)}, u32[]{:S(2)}) async-start(bf16[8,64,1024]{2,1,0:T(8,128)(2,1)} %bitcast.114), calls=%async_computation | async-start | bytes 2097152 | tf_op jit(solution)/shard_map/all_to_all | solution.py:186
  144.9 3.9 %collective-permute-done.16 = bf16[800,512]{1,0:T(8,128)(2,1)} collective-permute-done((bf16[800,512]{1,0:T(8,128)(2,1)}, bf16[800,512]{1,0:T(8,128)(2,1)}, u32[]{:S(2)}, u32[]{:S(2)}) %collective-permute-start.16) | collective-permute-done | bytes 819232 | tf_op jit(solution)/shard_map/ppermute | solution.py:168
  148.8 2.3 %bitcast_dynamic-update-slice_fusion.6 = bf16[4,800,512]{2,1,0:T(8,128)(2,1)} fusion(bf16[4,800,512]{2,1,0:T(8,128)(2,1)} %copy-done.1, s32[]{:T(128)S(6)} %select_n.112, bf16[800,512]{1,0:T(8,128)(2,1)} %collective-permute-done.11, bf16[800,512]{1,0:T(8,128)(2,1)} %collective-permute-done.16, pred[]{:T(512)S(6)} %ge.12), kind=kLoop, calls=%fused_computation.44 | loop fusion | flops 409600 | bytes 2457605 | tf_op jit(solution)/shard_map/dynamic_update_slice | solution.py:177
  151.1 2.3 %bitcast_dynamic-update-slice_fusion.5 = bf16[4,800,512]{2,1,0:T(8,128)(2,1)} fusion(bf16[4,800,512]{2,1,0:T(8,128)(2,1)} %bitcast_dynamic-update-slice_fusion.6, s32[]{:T(128)S(6)} %select_n.115, bf16[800,512]{1,0:T(8,128)(2,1)} %collective-permute-done.12, bf16[800,512]{1,0:T(8,128)(2,1)} %collective-permute-done.14, pred[]{:T(512)S(6)} %ge.13), kind=kLoop, calls=%fused_computation.43 | loop fusion | flops 409600 | bytes 2457605 | tf_op jit(solution)/shard_map/dynamic_update_slice | solution.py:177
  153.4 2.3 %bitcast_dynamic-update-slice_fusion.4 = bf16[4,800,512]{2,1,0:T(8,128)(2,1)} fusion(bf16[4,800,512]{2,1,0:T(8,128)(2,1)} %bitcast_dynamic-update-slice_fusion.5, s32[]{:T(128)S(6)} %select_n.118, bf16[800,512]{1,0:T(8,128)(2,1)} %collective-permute-done.15, bf16[800,512]{1,0:T(8,128)(2,1)} %collective-permute-done.13, pred[]{:T(512)S(6)} %ge.14), kind=kLoop, calls=%fused_computation.42 | loop fusion | flops 409600 | bytes 2457605 | tf_op jit(solution)/shard_map/dynamic_update_slice | solution.py:177
  155.6 2.1 %constant_dynamic-slice_fusion = (bf16[2,800,512]{2,1,0:T(8,128)(2,1)S(1)}, bf16[2,800,512]{2,1,0:T(8,128)(2,1)S(1)}) fusion(bf16[4,800,512]{2,1,0:T(8,128)(2,1)} %bitcast_dynamic-update-slice_fusion.4, s32[]{:T(128)S(6)} %select_n.120, s32[]{:T(128)S(6)} %select_n.119), kind=kLoop, calls=%fused_computation.105 | loop fusion | bytes 6553608 | tf_op jit(solution)/shard_map/dynamic_slice | solution.py:226
  157.8 3.4 %fusion.68 = f32[800,512]{1,0:T(8,128)S(1)} fusion(bf16[800,1600]{1,0:T(8,128)(2,1)} %collective-permute-done.7, bf16[1600,512]{1,0:T(8,128)(2,1)S(1)} %bitcast.110), kind=kOutput, calls=%fused_computation.127 | convolution fusion | flops 1310720000 | bytes 5836800 | tf_op jit(solution)/shard_map/dot_general | solution.py:117
  161.2 3.4 %add_convert_fusion = bf16[800,512]{1,0:T(8,128)(2,1)S(1)} fusion(f32[800,512]{1,0:T(8,128)S(1)} %fusion.68, bf16[800,1600]{1,0:T(8,128)(2,1)} %collective-permute-done.8, bf16[1600,512]{1,0:T(8,128)(2,1)S(1)} %bitcast.108), kind=kOutput, calls=%fused_computation.9 | convolution fusion | flops 1311539200 | bytes 6656000 | tf_op jit(solution)/shard_map/dot_general | solution.py:117
  164.6 3.8 %collective-permute-start.17 = (bf16[800,512]{1,0:T(8,128)(2,1)S(1)}, bf16[800,512]{1,0:T(8,128)(2,1)S(1)}, u32[]{:S(2)}, u32[]{:S(2)}) collective-permute-start(bf16[800,512]{1,0:T(8,128)(2,1)S(1)} %add_convert_fusion), channel_id=1, source_target_pairs={{0,2},{2,0},{4,6},{6,4},{8,10},{10,8},{12,14},{14,12},{1,3},{3,1},... | collective-permute-start | bytes 2457608 | tf_op jit(solution)/shard_map/ppermute | solution.py:271
  168.3 1.6 fusion.66
  170.0 1.7 fusion.67
  171.7 7.0 %collective-permute-done.17 = bf16[800,512]{1,0:T(8,128)(2,1)S(1)} collective-permute-done((bf16[800,512]{1,0:T(8,128)(2,1)S(1)}, bf16[800,512]{1,0:T(8,128)(2,1)S(1)}, u32[]{:S(2)}, u32[]{:S(2)}) %collective-permute-start.17) | collective-permute-done | bytes 819232 | tf_op jit(solution)/shard_map/ppermute | solution.py:271
  178.7 1.5 fusion.62
  180.2 1.3 slice_bitcast_fusion.1
  181.5 1.4 convert_reduce_fusion
  183.0 0.8 convolution_add_fusion.2
  184.8 0.3 fusion.10
  185.1 0.7 pad_maximum_fusion.2
  185.8 5.7 %all-to-all-start.1 = ((bf16[8,32,512]{2,1,0:T(8,128)(2,1)}), bf16[8,32,512]{2,1,0:T(8,128)(2,1)S(1)}, u32[]{:S(2)}, u32[]{:S(2)}) async-start(bf16[8,32,512]{2,1,0:T(8,128)(2,1)} %pad_maximum_fusion.2), calls=%async_computation.1 | async-start | bytes 524288 | tf_op jit(solution)/shard_map/all_to_all | solution.py:186
  191.5 2.4 %pad_maximum_fusion = f32[2,800,256]{2,1,0:T(8,128)} fusion(f32[1,800,256]{2,1,0:T(8,128)} %get-tuple-element.28, f32[1,800,256]{2,1,0:T(8,128)S(1)} %copy-done.16), kind=kLoop, calls=%fused_computation.7 | loop fusion | flops 409600 | bytes 3276800 | tf_op jit(solution)/shard_map/stack | solution.py:287
  193.9 0.7 pad_maximum_fusion.3
  194.6 5.1 %all-to-all-done.1 = bf16[8,32,512]{2,1,0:T(8,128)(2,1)S(1)} async-done(((bf16[8,32,512]{2,1,0:T(8,128)(2,1)}), bf16[8,32,512]{2,1,0:T(8,128)(2,1)S(1)}, u32[]{:S(2)}, u32[]{:S(2)}) %all-to-all-start.1) | async-done | bytes 262176 | tf_op jit(solution)/shard_map/all_to_all | solution.py:186
  199.8 1.3 convolution_subtract_fusion.1
  (100 shorter events, 4.8 us)
Async XLA Ops:
  0.6 3.9 %copy-start = (f32[800,3200]{1,0:T(8,128)S(1)}, f32[800,3200]{1,0:T(8,128)}, u32[]{:S(2)}) copy-start(f32[800,3200]{1,0:T(8,128)} %sigma_ref.1) | copy-start | bytes 30720004
  4.5 6.3 %copy-start.27 = (s32[2,27,1]{1,2,0:T(1,128)S(1)}, s32[2,27,1]{1,2,0:T(1,128)}, u32[]{:S(2)}) copy-start(s32[2,27,1]{1,2,0:T(1,128)} %param.15) | copy-start | bytes 652
  4.5 6.3 %copy-start.30 = (s32[1,25,2]{1,2,0:T(2,128)S(1)}, s32[1,25,2]{1,2,0:T(2,128)}, u32[]{:S(2)}) copy-start(s32[1,25,2]{1,2,0:T(2,128)} %param.11) | copy-start | bytes 604
  7.9 67.8 %collective-permute-start.7 = (bf16[800,1600]{1,0:T(8,128)(2,1)}, bf16[800,1600]{1,0:T(8,128)(2,1)}, u32[]{:S(2)}, u32[]{:S(2)}) collective-permute-start(bf16[800,1600]{1,0:T(8,128)(2,1)} %get-tuple-element.13), channel_id=1, source_target_pairs={{0,2},{2,0},{4,6},{6,4},{8,10},{10,8},{12,14},{14,12},{1,3},{3,1},... | collective-permute-start | bytes 7680008 | tf_op jit(solution)/shard_map/ppermute | solution.py:219
  16.4 2.5 %copy-start.3 = (f32[1,512,512]{2,1,0:T(8,128)S(1)}, f32[1,512,512]{2,1,0:T(8,128)}, u32[]{:S(2)}) copy-start(f32[1,512,512]{2,1,0:T(8,128)} %param.10) | copy-start | bytes 3145732
  16.4 2.5 %copy-start.7 = (bf16[1,800,512]{2,1,0:T(8,128)(2,1)S(1)}, bf16[1,800,512]{2,1,0:T(8,128)(2,1)}, u32[]{:S(2)}) copy-start(bf16[1,800,512]{2,1,0:T(8,128)(2,1)} %convert_element_type.101) | copy-start | bytes 2457604
  16.4 2.5 %copy-start.13 = (bf16[1,800,512]{2,1,0:T(8,128)(2,1)S(1)}, bf16[1,800,512]{2,1,0:T(8,128)(2,1)}, u32[]{:S(2)}) copy-start(bf16[1,800,512]{2,1,0:T(8,128)(2,1)} %param.9) | copy-start | bytes 2457604
  18.9 1.0 copy-start.2
  18.9 1.0 copy-start.26
  19.5 0.9 copy-start.5
  19.9 25.1 %copy-start.17 = (bf16[2,800,256]{2,1,0:T(8,128)(2,1)S(1)}, bf16[2,800,256]{2,1,0:T(8,128)(2,1)}, u32[]{:S(2)}) copy-start(bf16[2,800,256]{2,1,0:T(8,128)(2,1)} %param.12) | copy-start | bytes 2457604
  20.4 23.0 %collective-permute-start.1 = (bf16[864,512]{1,0:T(8,128)(2,1)S(1)}, bf16[864,512]{1,0:T(8,128)(2,1)S(1)}, u32[]{:S(2)}, u32[]{:S(2)}) collective-permute-start(bf16[864,512]{1,0:T(8,128)(2,1)S(1)} %maximum_maximum_fusion), channel_id=1, source_target_pairs={{4,0},{6,2},{8,4},{10,6},{12,8},{14,10},{5,1},{7,3},{9,5},{11,7},{... | collective-permute-start | bytes 2654216 | tf_op jit(solution)/shard_map/ppermute | solution.py:168
  21.7 24.2 %collective-permute-start = (bf16[864,512]{1,0:T(8,128)(2,1)S(1)}, bf16[864,512]{1,0:T(8,128)(2,1)S(1)}, u32[]{:S(2)}, u32[]{:S(2)}) collective-permute-start(bf16[864,512]{1,0:T(8,128)(2,1)S(1)} %maximum_maximum_fusion), channel_id=1, source_target_pairs={{0,4},{2,6},{4,8},{6,10},{8,12},{10,14},{1,5},{3,7},{5,9},{7,11},{... | collective-permute-start | bytes 2654216 | tf_op jit(solution)/shard_map/ppermute | solution.py:168
  43.4 2.5 %copy-start.20 = (bf16[864,512]{1,0:T(8,128)(2,1)}, bf16[864,512]{1,0:T(8,128)(2,1)S(1)}, u32[]{:S(2)}) copy-start(bf16[864,512]{1,0:T(8,128)(2,1)S(1)} %collective-permute-done.1) | copy-start | bytes 2654212
  43.4 22.3 %collective-permute-start.2 = (bf16[864,512]{1,0:T(8,128)(2,1)S(1)}, bf16[864,512]{1,0:T(8,128)(2,1)}, u32[]{:S(2)}, u32[]{:S(2)}) collective-permute-start(bf16[864,512]{1,0:T(8,128)(2,1)S(1)} %collective-permute-done.1), channel_id=1, source_target_pairs={{4,0},{6,2},{8,4},{10,6},{5,1},{7,3},{9,5},{11,7},{20,16},{22,18},... | collective-permute-start | bytes 2654216 | tf_op jit(solution)/shard_map/ppermute | solution.py:168
  45.9 22.1 %copy-start.14 = (bf16[2,800,256]{2,1,0:T(8,128)(2,1)}, bf16[2,800,256]{2,1,0:T(8,128)(2,1)S(1)}, u32[]{:S(2)}) copy-start(bf16[2,800,256]{2,1,0:T(8,128)(2,1)S(1)} %add_convert_fusion.1) | copy-start | bytes 2457604
  45.9 28.5 %copy-start.22 = (bf16[864,512]{1,0:T(8,128)(2,1)}, bf16[864,512]{1,0:T(8,128)(2,1)S(1)}, u32[]{:S(2)}) copy-start(bf16[864,512]{1,0:T(8,128)(2,1)S(1)} %collective-permute-done) | copy-start | bytes 2654212
  45.9 29.8 %collective-permute-start.4 = (bf16[864,512]{1,0:T(8,128)(2,1)S(1)}, bf16[864,512]{1,0:T(8,128)(2,1)}, u32[]{:S(2)}, u32[]{:S(2)}) collective-permute-start(bf16[864,512]{1,0:T(8,128)(2,1)S(1)} %collective-permute-done), channel_id=1, source_target_pairs={{4,8},{6,10},{8,12},{10,14},{5,9},{7,11},{9,13},{11,15},{20,24},{2... | collective-permute-start | bytes 2654216 | tf_op jit(solution)/shard_map/ppermute | solution.py:168
  47.6 19.5 %copy-start.9 = (bf16[800,256]{1,0:T(8,128)(2,1)}, bf16[800,256]{1,0:T(8,128)(2,1)S(1)}, u32[]{:S(2)}) copy-start(bf16[800,256]{1,0:T(8,128)(2,1)S(1)} %get-tuple-element.29) | copy-start | bytes 1228804
  47.6 20.4 %copy-start.11 = (bf16[800,256]{1,0:T(8,128)(2,1)}, bf16[800,256]{1,0:T(8,128)(2,1)S(1)}, u32[]{:S(2)}) copy-start(bf16[800,256]{1,0:T(8,128)(2,1)S(1)} %get-tuple-element.30) | copy-start | bytes 1228804
  65.7 40.7 %collective-permute-start.3 = (bf16[864,512]{1,0:T(8,128)(2,1)}, bf16[864,512]{1,0:T(8,128)(2,1)}, u32[]{:S(2)}, u32[]{:S(2)}) collective-permute-start(bf16[864,512]{1,0:T(8,128)(2,1)} %collective-permute-done.2), channel_id=1, source_target_pairs={{4,0},{6,2},{5,1},{7,3},{20,16},{22,18},{21,17},{23,19}} | collective-permute-start | bytes 2654216 | tf_op jit(solution)/shard_map/ppermute | solution.py:168
  68.0 21.0 %collective-permute-start.11 = (bf16[800,512]{1,0:T(8,128)(2,1)}, bf16[800,512]{1,0:T(8,128)(2,1)}, u32[]{:S(2)}, u32[]{:S(2)}) collective-permute-start(bf16[800,512]{1,0:T(8,128)(2,1)} %pad_maximum_fusion.1), channel_id=1, source_target_pairs={{0,4},{2,6},{4,8},{6,10},{8,12},{10,14},{1,5},{3,7},{5,9},{7,11},{... | collective-permute-start | bytes 2457608 | tf_op jit(solution)/shard_map/ppermute | solution.py:168
  74.4 30.5 %collective-permute-start.13 = (bf16[800,512]{1,0:T(8,128)(2,1)}, bf16[800,512]{1,0:T(8,128)(2,1)}, u32[]{:S(2)}, u32[]{:S(2)}) collective-permute-start(bf16[800,512]{1,0:T(8,128)(2,1)} %pad_maximum_fusion.1), channel_id=1, source_target_pairs={{4,0},{6,2},{8,4},{10,6},{12,8},{14,10},{5,1},{7,3},{9,5},{11,7},{... | collective-permute-start | bytes 2457608 | tf_op jit(solution)/shard_map/ppermute | solution.py:168
  75.7 40.5 %collective-permute-start.8 = (bf16[800,1600]{1,0:T(8,128)(2,1)}, bf16[800,1600]{1,0:T(8,128)(2,1)}, u32[]{:S(2)}, u32[]{:S(2)}) collective-permute-start(bf16[800,1600]{1,0:T(8,128)(2,1)} %collective-permute-done.7), channel_id=1, source_target_pairs={{0,1},{1,0},{2,3},{3,2},{4,5},{5,4},{6,7},{7,6},{8,9},{9,8},{10,11... | collective-permute-start | bytes 7680008 | tf_op jit(solution)/shard_map/ppermute | solution.py:221
  75.8 35.0 %collective-permute-start.5 = (bf16[864,512]{1,0:T(8,128)(2,1)}, bf16[864,512]{1,0:T(8,128)(2,1)}, u32[]{:S(2)}, u32[]{:S(2)}) collective-permute-start(bf16[864,512]{1,0:T(8,128)(2,1)} %collective-permute-done.4), channel_id=1, source_target_pairs={{8,12},{10,14},{9,13},{11,15},{24,28},{26,30},{25,29},{27,31}} | collective-permute-start | bytes 2654216 | tf_op jit(solution)/shard_map/ppermute | solution.py:168
  77.4 1.0 copy-start.10
  77.4 1.1 copy-start.12
  78.6 1.7 copy-start.1
  78.6 1.7 copy-start.6
  80.3 27.4 %copy-start.23 = (bf16[864,512]{1,0:T(8,128)(2,1)S(1)}, bf16[864,512]{1,0:T(8,128)(2,1)}, u32[]{:S(2)}) copy-start(bf16[864,512]{1,0:T(8,128)(2,1)} %copy-done.22) | copy-start | bytes 2654212
  89.0 33.3 %collective-permute-start.6 = (bf16[800,1600]{1,0:T(8,128)(2,1)S(1)}, bf16[800,1600]{1,0:T(8,128)(2,1)S(1)}, u32[]{:S(2)}, u32[]{:S(2)}) collective-permute-start(bf16[800,1600]{1,0:T(8,128)(2,1)S(1)} %get-tuple-element.12), channel_id=1, source_target_pairs={{0,1},{1,0},{2,3},{3,2},{4,5},{5,4},{6,7},{7,6},{8,9},{9,8},{10,11... | collective-permute-start | bytes 7680008 | tf_op jit(solution)/shard_map/ppermute | solution.py:220
  104.9 19.1 %collective-permute-start.12 = (bf16[800,512]{1,0:T(8,128)(2,1)}, bf16[800,512]{1,0:T(8,128)(2,1)}, u32[]{:S(2)}, u32[]{:S(2)}) collective-permute-start(bf16[800,512]{1,0:T(8,128)(2,1)} %collective-permute-done.11), channel_id=1, source_target_pairs={{4,8},{6,10},{8,12},{10,14},{5,9},{7,11},{9,13},{11,15},{20,24},{2... | collective-permute-start | bytes 2457608 | tf_op jit(solution)/shard_map/ppermute | solution.py:168
  106.4 19.3 %collective-permute-start.14 = (bf16[800,512]{1,0:T(8,128)(2,1)}, bf16[800,512]{1,0:T(8,128)(2,1)}, u32[]{:S(2)}, u32[]{:S(2)}) collective-permute-start(bf16[800,512]{1,0:T(8,128)(2,1)} %collective-permute-done.13), channel_id=1, source_target_pairs={{4,0},{6,2},{8,4},{10,6},{5,1},{7,3},{9,5},{11,7},{20,16},{22,18},... | collective-permute-start | bytes 2457608 | tf_op jit(solution)/shard_map/ppermute | solution.py:168
  109.2 1.6 copy-start.21
  111.3 17.4 %collective-permute-start.10 = (bf16[4,64,512]{2,1,0:T(8,128)(2,1)S(1)}, bf16[4,64,512]{2,1,0:T(8,128)(2,1)S(1)}, u32[]{:S(2)}, u32[]{:S(2)}) collective-permute-start(bf16[4,64,512]{2,1,0:T(8,128)(2,1)S(1)} %get-tuple-element.22), channel_id=1, source_target_pairs={{0,2},{2,0},{4,6},{6,4},{8,10},{10,8},{12,14},{14,12},{1,3},{3,1},... | collective-permute-start | bytes 786440 | tf_op jit(solution)/shard_map/ppermute | solution.py:246
  119.6 17.2 %collective-permute-start.9 = (bf16[800,512]{1,0:T(8,128)(2,1)S(1)}, bf16[800,512]{1,0:T(8,128)(2,1)S(1)}, u32[]{:S(2)}, u32[]{:S(2)}) collective-permute-start(bf16[800,512]{1,0:T(8,128)(2,1)S(1)} %add_convert_fusion.2), channel_id=1, source_target_pairs={{0,2},{2,0},{4,6},{6,4},{8,10},{10,8},{12,14},{14,12},{1,3},{3,1},... | collective-permute-start | bytes 2457608 | tf_op jit(solution)/shard_map/ppermute | solution.py:244
  122.3 1.7 copy-start.28
  125.7 19.2 %collective-permute-start.15 = (bf16[800,512]{1,0:T(8,128)(2,1)}, bf16[800,512]{1,0:T(8,128)(2,1)}, u32[]{:S(2)}, u32[]{:S(2)}) collective-permute-start(bf16[800,512]{1,0:T(8,128)(2,1)} %collective-permute-done.12), channel_id=1, source_target_pairs={{8,12},{10,14},{9,13},{11,15},{24,28},{26,30},{25,29},{27,31}} | collective-permute-start | bytes 2457608 | tf_op jit(solution)/shard_map/ppermute | solution.py:168
  127.3 21.6 %collective-permute-start.16 = (bf16[800,512]{1,0:T(8,128)(2,1)}, bf16[800,512]{1,0:T(8,128)(2,1)}, u32[]{:S(2)}, u32[]{:S(2)}) collective-permute-start(bf16[800,512]{1,0:T(8,128)(2,1)} %collective-permute-done.14), channel_id=1, source_target_pairs={{4,0},{6,2},{5,1},{7,3},{20,16},{22,18},{21,17},{23,19}} | collective-permute-start | bytes 2457608 | tf_op jit(solution)/shard_map/ppermute | solution.py:168
  138.4 2.2 %copy-start.18 = (bf16[800,512]{1,0:T(8,128)(2,1)}, bf16[800,512]{1,0:T(8,128)(2,1)S(1)}, u32[]{:S(2)}) copy-start(bf16[800,512]{1,0:T(8,128)(2,1)S(1)} %get-tuple-element.20) | copy-start | bytes 2457604
  140.6 40.9 %all-to-all-start = ((bf16[8,64,1024]{2,1,0:T(8,128)(2,1)}), bf16[8,64,1024]{2,1,0:T(8,128)(2,1)}, u32[]{:S(2)}, u32[]{:S(2)}) async-start(bf16[8,64,1024]{2,1,0:T(8,128)(2,1)} %bitcast.114), calls=%async_computation | async-start | bytes 2097152 | tf_op jit(solution)/shard_map/all_to_all | solution.py:186
  164.6 5.4 %copy-start.29 = (bf16[800,1600]{1,0:T(8,128)(2,1)S(1)}, bf16[800,1600]{1,0:T(8,128)(2,1)}, u32[]{:S(2)}) copy-start(bf16[800,1600]{1,0:T(8,128)(2,1)} %copy-done.28) | copy-start | bytes 7680004
  164.6 14.1 %collective-permute-start.17 = (bf16[800,512]{1,0:T(8,128)(2,1)S(1)}, bf16[800,512]{1,0:T(8,128)(2,1)S(1)}, u32[]{:S(2)}, u32[]{:S(2)}) collective-permute-start(bf16[800,512]{1,0:T(8,128)(2,1)S(1)} %add_convert_fusion), channel_id=1, source_target_pairs={{0,2},{2,0},{4,6},{6,4},{8,10},{10,8},{12,14},{14,12},{1,3},{3,1},... | collective-permute-start | bytes 2457608 | tf_op jit(solution)/shard_map/ppermute | solution.py:271
  170.0 8.7 %copy-start.8 = (bf16[4,2,64,512]{3,2,1,0:T(8,128)(2,1)S(1)}, bf16[4,2,64,512]{3,2,1,0:T(8,128)(2,1)}, u32[]{:S(2)}) copy-start(bf16[4,2,64,512]{3,2,1,0:T(8,128)(2,1)} %maximum_select_fusion) | copy-start | bytes 1572868
  170.0 8.7 %copy-start.19 = (bf16[800,512]{1,0:T(8,128)(2,1)S(1)}, bf16[800,512]{1,0:T(8,128)(2,1)}, u32[]{:S(2)}) copy-start(bf16[800,512]{1,0:T(8,128)(2,1)} %copy-done.18) | copy-start | bytes 2457604
  180.2 2.7 %copy-start.4 = (f32[1,512,512]{2,1,0:T(8,128)S(1)}, f32[1,512,512]{2,1,0:T(8,128)}, u32[]{:S(2)}) copy-start(f32[1,512,512]{2,1,0:T(8,128)} %param.10) | copy-start | bytes 3145732
  183.0 1.4 copy-start.15
  183.0 1.4 copy-start.24
  183.7 1.4 copy-start.25
  184.8 6.8 %copy-start.16 = (f32[1,800,256]{2,1,0:T(8,128)S(1)}, f32[1,800,256]{2,1,0:T(8,128)}, u32[]{:S(2)}) copy-start(f32[1,800,256]{2,1,0:T(8,128)} %get-tuple-element.27) | copy-start | bytes 2457604
  185.8 13.9 %all-to-all-start.1 = ((bf16[8,32,512]{2,1,0:T(8,128)(2,1)}), bf16[8,32,512]{2,1,0:T(8,128)(2,1)S(1)}, u32[]{:S(2)}, u32[]{:S(2)}) async-start(bf16[8,32,512]{2,1,0:T(8,128)(2,1)} %pad_maximum_fusion.2), calls=%async_computation.1 | async-start | bytes 524288 | tf_op jit(solution)/shard_map/all_to_all | solution.py:186

commit v4 on v3

--- a/solution.py
+++ b/solution.py
@@ -104,8 +104,16 @@
 
 
 def masked_product(lower_part, pattern, weights, first_row):
-    mask = expand_pattern(pattern, first_row, lower_part.shape[1], B).astype(jnp.bfloat16)
-    masked = lower_part * mask
+    block_ids = (first_row + lax.iota(jnp.int32, lower_part.shape[1])) // B
+    picked = (block_ids[:, None] == lax.iota(jnp.int32, pattern.shape[1])[None, :])[None, :, :, None]
+    spread = jnp.sum(jnp.where(picked, pattern[:, None], 0), axis=2).astype(jnp.bfloat16)
+    masked = jnp.concatenate(
+        [
+            lower_part[:, :, k * B : (k + 1) * B] * spread[:, :, k : k + 1]
+            for k in range(pattern.shape[2])
+        ],
+        axis=2,
+    )
     high, low = split_high_low(weights)
     both = jnp.einsum(
         "nrk,nkc->nrc", masked, high, preferred_element_type=jnp.float32
@@ -168,14 +176,20 @@
     return lax.ppermute(held[0], "prow", up), lax.ppermute(held[1], "prow", down)
 
 
-def line_order(block, hops, layers, layer):
-    gathered = jnp.zeros((layers,) + block.shape, block.dtype)
-    gathered = lax.dynamic_update_slice(gathered, block[None], (layer, 0, 0))
-    for back in range(1, layers):
-        piece = jnp.where(layer >= back, hops[back - 1][0], hops[layers - back - 1][1])
-        at = lax.rem(layer - back + layers, layers)
-        gathered = lax.dynamic_update_slice(gathered, piece[None], (at, 0, 0))
-    return gathered
+def line_order(block, hops, layers, layer, first):
+    by_distance = [block] + [
+        jnp.where(layer >= back, hops[back - 1][0], hops[layers - back - 1][1])
+        for back in range(1, layers)
+    ]
+
+    def at(place):
+        back = lax.rem(layer - place + 2 * layers, layers)
+        found = by_distance[0]
+        for distance in range(1, layers):
+            found = jnp.where(back == distance, by_distance[distance], found)
+        return found
+
+    return [at(first + place) for place in range(layers)]
 
 
 def tie(values, after):
@@ -214,35 +228,42 @@
     )
     own_sep = jnp.concatenate([normal_sep[0], normal_sep[1]], axis=1)
 
+    first = jnp.concatenate([own_one, own_sep])
     half = layers // 2
-    kept, given = part_columns(sigma_root, side)
+    kept, given = part_columns(sigma_root, tie(side, first))
     taken = lax.ppermute(given, "prow", swap_side)
     kept_sibling = lax.ppermute(kept, "pcol", swap_core)
     taken_sibling = lax.ppermute(taken, "pcol", swap_core)
 
     def root_parts(gathered):
-        width = gathered.shape[2]
-        near = lax.dynamic_slice_in_dim(gathered, core * half, half, 0).reshape(-1, width)
-        far = lax.dynamic_slice_in_dim(gathered, (1 - core) * half, half, 0).reshape(-1, width)
+        near = jnp.concatenate(gathered[:half])
+        far = jnp.concatenate(gathered[half:])
         away = (dot(taken, near) + dot(taken_sibling, far)).astype(jnp.bfloat16)
         return near, far, away
 
     def root_total(near, far, arrived):
         return dot(kept, near) + dot(kept_sibling, far) + arrived.astype(jnp.float32)
 
-    first = jnp.concatenate([own_one, own_sep])
     hops_one = [line_hop((first, first), layers, 1)]
-    second = tie(own_two, hops_one[0])
+    second = tie(own_two, first)
     hops_two = []
     held = (second, second)
     for step in range(2, layers):
         hops_one.append(line_hop(hops_one[-1], layers, step))
         held = line_hop(held, layers, step - 1)
         hops_two.append(held)
-    joined = line_order(first, hops_one, layers, layer)
-    near_one, far_one, away_one = root_parts(joined[:, :rows])
+    def order(block, hops):
+        return line_order(block, hops, layers, layer, core * half)
+
+    near_one, far_one, away_one = root_parts(
+        order(own_one, [[held[:rows] for held in hop] for hop in hops_one])
+    )
     arrived_one = lax.ppermute(away_one, "prow", swap_side)
-    sep_here = joined[:, rows:]
+    sep_here = jnp.stack(
+        line_order(
+            own_sep, [[held[rows:] for held in hop] for hop in hops_one], layers, layer, 0
+        )
+    )
     sep_there = lax.ppermute(sep_here, "prow", swap_side)
     hops_two.append(line_hop(tie(held, away_one), layers, layers - 1))
 
@@ -267,7 +288,7 @@
     sep_two = sums[:, sep_width:] - dot(diag_rows.astype(jnp.bfloat16), all_sep)
     short_sep = sep_two.astype(jnp.bfloat16)
 
-    near_two, far_two, away_two = root_parts(line_order(own_two, hops_two, layers, layer))
+    near_two, far_two, away_two = root_parts(order(own_two, hops_two))
     arrived_two = lax.ppermute(away_two, "prow", swap_side)
     product_two = root_total(near_two, far_two, arrived_two)
     two_root = dot(short_one, all_sep) - product_two

time: 202 us -> 242 us (1.20)
  waiting for transfers between devices: 84.6 us -> 133 us
  local copies, waits for them, and re-layouts: 16.3 us -> 9.01 us
  starting transfers between devices: 44 us -> 40.4 us
  matrix products: 32.4 us -> 35.5 us
    ppermute x1, waiting for transfers between devices: 0.01 us -> 27 us  [on_pairs(): taken = lax.ppermute(given, 'prow', swap_side)]
    ppermute x6, waiting for transfers between devices: 8.57 us -> 29.2 us  [line_hop(): lax.ppermute(held[0], 'prow', up)]
    ppermute x1, waiting for transfers between devices: 0.01 us -> 19.5 us  [on_pairs(): sep_there = lax.ppermute(sep_here, 'prow', swap_side)]
    ppermute x6, waiting for transfers between devices: 56.8 us -> 46.5 us  [line_hop(): lax.ppermute(held[1], 'prow', down)]
    dynamic_update_slice x8 -> x0, other arithmetic: 10.2 us -> none  [the longest x6 10.1 us: line_order(): gathered = lax.dynamic_update_slice(gathered, piece[None], (at, 0, 0))]
    ppermute x1, waiting for transfers between devices: 7.12 us -> 0.01 us  [on_pairs(): arrived_one = lax.ppermute(away_one, 'prow', swap_side)]
    select_n x2 -> x6, other arithmetic: 0.02 us -> 6.48 us  [the longest x4 6.46 us: at(): found = jnp.where(back == distance, by_distance[distance], found)]
    dot_general x10, matrix products: 21.9 us -> 26.3 us  [dot(): return jnp.dot(left, right, preferred_element_type=jnp.float32)]
  transfers between devices with their start and end apart: 20 -> 20, of which waited for: 9 -> 9; matrix products, arithmetic and copies ran while one was open for 28% -> 19% of each run, Pallas kernels for 0% -> 0%
where the time goes in v4:
time: 242 us; the launch traced here: 241 us
  waiting for transfers between devices  133 us (55%)
  starting transfers between devices  40.4 us (17%)
  matrix products  35.5 us (15%)
  other arithmetic  17.9 us (7%)
  local copies, waits for them, and re-layouts  9.01 us (4%)
  Pallas kernels  3.29 us (1%)
    ppermute x6, waiting for transfers between devices, line_hop(): lax.ppermute(held[1], 'prow', down)  46.5 us
    ppermute x6, waiting for transfers between devices, line_hop(): lax.ppermute(held[0], 'prow', up)  29.2 us
    ppermute x1, waiting for transfers between devices, on_pairs(): taken = lax.ppermute(given, 'prow', swap_side)  27 us
    dot_general x10, matrix products, dot(): return jnp.dot(left, right, preferred_element_type=jnp.float32)  26.3 us
    ppermute x1, waiting for transfers between devices, on_pairs(): sep_there = lax.ppermute(sep_here, 'prow', swap_side)  19.5 us
    ppermute x6, starting transfers between devices, line_hop(): lax.ppermute(held[0], 'prow', up)  14.6 us
    all_to_all x2, starting transfers between devices, scatter_sum(): moved = lax.all_to_all(parts.astype(jnp.bfloat16), 'prow', 0, 0, tiled=True)  9.49 us
    ppermute x6, starting transfers between devices, line_hop(): lax.ppermute(held[1], 'prow', down)  7.69 us
  transfers between devices with their start and end apart: 20, of which 9 were waited for; matrix products, arithmetic and copies ran while one was open for 19% of the time, Pallas kernels for 0%

profile of v4, /device:TPU:0, one launch (start us, length us, event | category | flops | bytes accessed | tf_op | source)
XLA Modules:
  0.0 240.6 jit_solution(8183597038351669227)
XLA Ops:
  0.7 0.8 copy.18
  1.8 1.4 slice_multiply_fusion.1
  3.2 0.6 fusion.23
  3.8 0.6 add_convert_fusion.3
  5.3 1.0 maximum_maximum_fusion
  6.3 3.9 %copy-done = f32[800,3200]{1,0:T(8,128)S(1)} copy-done((f32[800,3200]{1,0:T(8,128)S(1)}, f32[800,3200]{1,0:T(8,128)}, u32[]{:S(2)}) %copy-start) | copy-done | bytes 10240024
  10.2 3.3 %shard_map.119 = (bf16[800,1600]{1,0:T(8,128)(2,1)S(1)}, bf16[800,1600]{1,0:T(8,128)(2,1)}) custom-call(s32[1]{0:T(128)} %bitcast.8.side_ref, f32[800,3200]{1,0:T(8,128)S(1)} %copy-done), custom_call_target="tpu_custom_call" | custom-call | bytes 15360000 | tf_op jit(solution)/shard_map/pallas_call | solution.py:157
  13.5 2.9 %collective-permute-start.7 = (bf16[800,1600]{1,0:T(8,128)(2,1)}, bf16[800,1600]{1,0:T(8,128)(2,1)}, u32[]{:S(2)}, u32[]{:S(2)}) collective-permute-start(bf16[800,1600]{1,0:T(8,128)(2,1)} %get-tuple-element.15), channel_id=1, source_target_pairs={{0,2},{2,0},{4,6},{6,4},{8,10},{10,8},{12,14},{14,12},{1,3},{3,1},... | collective-permute-start | bytes 7680008 | tf_op jit(solution)/shard_map/ppermute | solution.py:234
  16.4 4.4 %collective-permute-start = (bf16[864,512]{1,0:T(8,128)(2,1)}, bf16[864,512]{1,0:T(8,128)(2,1)}, u32[]{:S(2)}, u32[]{:S(2)}) collective-permute-start(bf16[864,512]{1,0:T(8,128)(2,1)} %maximum_maximum_fusion), channel_id=1, source_target_pairs={{0,4},{2,6},{4,8},{6,10},{8,12},{10,14},{1,5},{3,7},{5,9},{7,11},{... | collective-permute-start | bytes 2654216 | tf_op jit(solution)/shard_map/ppermute | solution.py:176
  20.8 1.3 collective-permute-start.3
  22.1 0.7 copy.19
  22.8 1.0 select_reduce_fusion
  23.9 15.0 %collective-permute-done = bf16[864,512]{1,0:T(8,128)(2,1)} collective-permute-done((bf16[864,512]{1,0:T(8,128)(2,1)}, bf16[864,512]{1,0:T(8,128)(2,1)}, u32[]{:S(2)}, u32[]{:S(2)}) %collective-permute-start) | collective-permute-done | bytes 884768 | tf_op jit(solution)/shard_map/ppermute | solution.py:176
  38.8 1.6 collective-permute-start.1
  40.4 3.5 %collective-permute-done.3 = bf16[864,512]{1,0:T(8,128)(2,1)} collective-permute-done((bf16[864,512]{1,0:T(8,128)(2,1)}, bf16[864,512]{1,0:T(8,128)(2,1)}, u32[]{:S(2)}, u32[]{:S(2)}) %collective-permute-start.3) | collective-permute-done | bytes 884768 | tf_op jit(solution)/shard_map/ppermute | solution.py:176
  43.9 1.3 collective-permute-start.4
  45.1 1.8 fusion.21
  46.9 0.4 add_convert_fusion.1
  47.4 27.0 %collective-permute-done.7 = bf16[800,1600]{1,0:T(8,128)(2,1)} collective-permute-done((bf16[800,1600]{1,0:T(8,128)(2,1)}, bf16[800,1600]{1,0:T(8,128)(2,1)}, u32[]{:S(2)}, u32[]{:S(2)}) %collective-permute-start.7) | collective-permute-done | bytes 2560032 | tf_op jit(solution)/shard_map/ppermute | solution.py:234
  74.5 1.0 pad_maximum_fusion.15
  75.4 3.8 %collective-permute-start.11 = (bf16[800,512]{1,0:T(8,128)(2,1)}, bf16[800,512]{1,0:T(8,128)(2,1)S(1)}, u32[]{:S(2)}, u32[]{:S(2)}) collective-permute-start(bf16[800,512]{1,0:T(8,128)(2,1)} %pad_maximum_fusion.15), channel_id=1, source_target_pairs={{0,4},{2,6},{4,8},{6,10},{8,12},{10,14},{1,5},{3,7},{5,9},{7,11},{... | collective-permute-start | bytes 2457608 | tf_op jit(solution)/shard_map/ppermute | solution.py:176
  79.3 1.6 collective-permute-start.2
  80.8 1.3 collective-permute-start.5
  82.1 1.3 collective-permute-start.13
  83.4 14.2 %collective-permute-done.11 = bf16[800,512]{1,0:T(8,128)(2,1)S(1)} collective-permute-done((bf16[800,512]{1,0:T(8,128)(2,1)}, bf16[800,512]{1,0:T(8,128)(2,1)S(1)}, u32[]{:S(2)}, u32[]{:S(2)}) %collective-permute-start.11) | collective-permute-done | bytes 819232 | tf_op jit(solution)/shard_map/ppermute | solution.py:176
  97.7 0.9 copy-done.21
  98.6 23.8 %collective-permute-done.13 = bf16[800,512]{1,0:T(8,128)(2,1)} collective-permute-done((bf16[800,512]{1,0:T(8,128)(2,1)}, bf16[800,512]{1,0:T(8,128)(2,1)}, u32[]{:S(2)}, u32[]{:S(2)}) %collective-permute-start.13) | collective-permute-done | bytes 819232 | tf_op jit(solution)/shard_map/ppermute | solution.py:176
  122.4 1.6 collective-permute-start.12
  123.9 1.3 collective-permute-start.14
  125.2 1.1 select_bitcast_fusion.3
  126.4 2.8 %select_select_fusion.5 = (bf16[800,512]{1,0:T(8,128)(2,1)S(1)}, bf16[800,512]{1,0:T(8,128)(2,1)S(1)}, bf16[800,512]{1,0:T(8,128)(2,1)S(1)}, bf16[800,512]{1,0:T(8,128)(2,1)S(1)}) fusion(bf16[800,512]{1,0:T(8,128)(2,1)S(1)} %add_convert_fusion.3, pred[]{:T(512)S(6)} %eq.141, pred[]{:T(512)S(6)} %eq.140, pred[]{:T(512)S(6)} %eq.139, ...), kind=kLoop, calls=%fused_computation.52 | loop fusion | flops 2457600 | bytes 9011206 | tf_op jit(solution)/shard_map/jit(_where)/select_n | solution.py:189
  129.4 3.4 %fusion.16 = f32[800,512]{1,0:T(8,128)S(1)} fusion(bf16[800,1600]{1,0:T(8,128)(2,1)} %collective-permute-done.7, bf16[800,512]{1,0:T(8,128)(2,1)S(1)} %get-tuple-element.39, bf16[800,512]{1,0:T(8,128)(2,1)S(1)} %get-tuple-element.40), kind=kOutput, calls=%fused_computation.35 | convolution fusion | flops 1313996800 | bytes 5836800 | tf_op jit(solution)/shard_map/dot_general | solution.py:125
  132.9 3.4 %add_convert_fusion.2 = bf16[800,512]{1,0:T(8,128)(2,1)S(1)} fusion(f32[800,512]{1,0:T(8,128)S(1)} %fusion.16, bf16[800,1600]{1,0:T(8,128)(2,1)} %collective-permute-done.8, bf16[800,512]{1,0:T(8,128)(2,1)S(1)} %get-tuple-element.38, bf16[800,512]{1,0:T(8,128)(2,1)S(1)} %get-tuple-element.31), kind=kOutput, calls=%fused_computation.17 | convolution fusion | flops 1314816000 | bytes 6656000 | tf_op jit(solution)/shard_map/dot_general | solution.py:125
  136.3 1.5 collective-permute-start.9
  138.0 0.6 collective-permute-start.10
  138.6 3.4 %fusion.15 = f32[800,512]{1,0:T(8,128)S(1)} fusion(bf16[800,1600]{1,0:T(8,128)(2,1)} %collective-permute-done.6, bf16[800,512]{1,0:T(8,128)(2,1)S(1)} %get-tuple-element.38, bf16[800,512]{1,0:T(8,128)(2,1)S(1)} %get-tuple-element.31), kind=kOutput, calls=%fused_computation.34 | convolution fusion | flops 1313996800 | bytes 5836800 | tf_op jit(solution)/shard_map/dot_general | solution.py:125
  142.0 19.5 %collective-permute-done.10 = bf16[4,64,512]{2,1,0:T(8,128)(2,1)S(1)} collective-permute-done((bf16[4,64,512]{2,1,0:T(8,128)(2,1)S(1)}, bf16[4,64,512]{2,1,0:T(8,128)(2,1)S(1)}, u32[]{:S(2)}, u32[]{:S(2)}) %collective-permute-start.10) | collective-permute-done | bytes 262176 | tf_op jit(solution)/shard_map/ppermute | solution.py:267
  161.6 0.9 copy.20
  162.5 1.7 collective-permute-start.15
  164.2 1.3 collective-permute-start.16
  165.5 1.6 convert_add_fusion
  167.2 2.3 fusion.6
  169.4 6.1 %all-to-all-start = ((bf16[8,64,1024]{2,1,0:T(8,128)(2,1)}), bf16[8,64,1024]{2,1,0:T(8,128)(2,1)}, u32[]{:S(2)}, u32[]{:S(2)}) async-start(bf16[8,64,1024]{2,1,0:T(8,128)(2,1)} %bitcast.78), calls=%async_computation | async-start | bytes 2097152 | tf_op jit(solution)/shard_map/all_to_all | solution.py:200
  175.5 19.2 %collective-permute-done.16 = bf16[800,512]{1,0:T(8,128)(2,1)} collective-permute-done((bf16[800,512]{1,0:T(8,128)(2,1)}, bf16[800,512]{1,0:T(8,128)(2,1)}, u32[]{:S(2)}, u32[]{:S(2)}) %collective-permute-start.16) | collective-permute-done | bytes 819232 | tf_op jit(solution)/shard_map/ppermute | solution.py:176
  194.8 2.5 %select_select_fusion.1 = (bf16[800,512]{1,0:T(8,128)(2,1)S(1)}, bf16[800,512]{1,0:T(8,128)(2,1)S(1)}, bf16[800,512]{1,0:T(8,128)(2,1)S(1)}, bf16[800,512]{1,0:T(8,128)(2,1)S(1)}) fusion(pred[]{:T(512)S(6)} %eq.141, pred[]{:T(512)S(6)} %eq.140, pred[]{:T(512)S(6)} %eq.139, bf16[800,256]{1,0:T(8,128)(2,1)S(1)} %copy-done.13, ...), kind=kLoop, calls=%fused_computation.48 | loop fusion | flops 4096000 | bytes 9011206 | tf_op jit(solution)/shard_map/jit(_where)/select_n | solution.py:189
  197.3 0.9 select_select_fusion
  198.2 3.4 %fusion.13 = f32[800,512]{1,0:T(8,128)S(1)} fusion(bf16[800,1600]{1,0:T(8,128)(2,1)} %collective-permute-done.7, bf16[800,512]{1,0:T(8,128)(2,1)S(1)} %get-tuple-element.36, bf16[800,512]{1,0:T(8,128)(2,1)S(1)} %get-tuple-element.37), kind=kOutput, calls=%fused_computation.32 | convolution fusion | flops 1313996800 | bytes 5836800 | tf_op jit(solution)/shard_map/dot_general | solution.py:125
  201.6 3.5 %add_convert_fusion = bf16[800,512]{1,0:T(8,128)(2,1)S(1)} fusion(f32[800,512]{1,0:T(8,128)S(1)} %fusion.13, bf16[800,1600]{1,0:T(8,128)(2,1)} %collective-permute-done.8, bf16[800,512]{1,0:T(8,128)(2,1)S(1)} %get-tuple-element.35, bf16[800,512]{1,0:T(8,128)(2,1)S(1)} %get-tuple-element.27), kind=kOutput, calls=%fused_computation.13 | convolution fusion | flops 1314816000 | bytes 6656000 | tf_op jit(solution)/shard_map/dot_general | solution.py:125
  205.1 3.5 %collective-permute-start.17 = (bf16[800,512]{1,0:T(8,128)(2,1)S(1)}, bf16[800,512]{1,0:T(8,128)(2,1)S(1)}, u32[]{:S(2)}, u32[]{:S(2)}) collective-permute-start(bf16[800,512]{1,0:T(8,128)(2,1)S(1)} %add_convert_fusion), channel_id=1, source_target_pairs={{0,2},{2,0},{4,6},{6,4},{8,10},{10,8},{12,14},{14,12},{1,3},{3,1},... | collective-permute-start | bytes 2457608 | tf_op jit(solution)/shard_map/ppermute | solution.py:292
  208.6 1.3 negate_bitcast_fusion
  210.0 1.6 fusion.14
  211.6 3.5 %fusion.12 = f32[800,512]{1,0:T(8,128)S(1)} fusion(bf16[800,1600]{1,0:T(8,128)(2,1)} %collective-permute-done.6, bf16[800,512]{1,0:T(8,128)(2,1)S(1)} %get-tuple-element.35, bf16[800,512]{1,0:T(8,128)(2,1)S(1)} %get-tuple-element.27), kind=kOutput, calls=%fused_computation.31 | convolution fusion | flops 1313996800 | bytes 5836800 | tf_op jit(solution)/shard_map/dot_general | solution.py:125
  215.1 4.8 %collective-permute-done.17 = bf16[800,512]{1,0:T(8,128)(2,1)S(1)} collective-permute-done((bf16[800,512]{1,0:T(8,128)(2,1)S(1)}, bf16[800,512]{1,0:T(8,128)(2,1)S(1)}, u32[]{:S(2)}, u32[]{:S(2)}) %collective-permute-start.17) | collective-permute-done | bytes 819232 | tf_op jit(solution)/shard_map/ppermute | solution.py:292
  219.8 1.6 fusion.68
  221.4 1.3 slice_bitcast_fusion.1
  222.7 1.4 convert_reduce_fusion
  224.1 0.8 convolution_add_fusion.2
  224.9 0.9 fusion.67
  227.0 0.7 pad_maximum_fusion.17
  227.7 3.4 %all-to-all-start.1 = ((bf16[8,32,512]{2,1,0:T(8,128)(2,1)}), bf16[8,32,512]{2,1,0:T(8,128)(2,1)S(1)}, u32[]{:S(2)}, u32[]{:S(2)}) async-start(bf16[8,32,512]{2,1,0:T(8,128)(2,1)} %pad_maximum_fusion.17), calls=%async_computation.1 | async-start | bytes 524288 | tf_op jit(solution)/shard_map/all_to_all | solution.py:200
  231.1 1.3 pad_maximum_fusion.4
  232.4 0.7 pad_maximum_fusion.18
  233.1 6.2 %all-to-all-done.1 = bf16[8,32,512]{2,1,0:T(8,128)(2,1)S(1)} async-done(((bf16[8,32,512]{2,1,0:T(8,128)(2,1)}), bf16[8,32,512]{2,1,0:T(8,128)(2,1)S(1)}, u32[]{:S(2)}, u32[]{:S(2)}) %all-to-all-start.1) | async-done | bytes 262176 | tf_op jit(solution)/shard_map/all_to_all | solution.py:200
  239.3 1.3 convolution_subtract_fusion.1
  (99 shorter events, 2.9 us)
Async XLA Ops:
  0.6 2.6 %copy-start.4 = (f32[1,512,512]{2,1,0:T(8,128)S(1)}, f32[1,512,512]{2,1,0:T(8,128)}, u32[]{:S(2)}) copy-start(f32[1,512,512]{2,1,0:T(8,128)} %param.10) | copy-start | bytes 3145732
  0.7 2.5 %copy-start.29 = (pred[800,25]{0,1:T(8,128)(4,1)}, pred[800,25]{0,1:T(8,128)(4,1)S(1)}, u32[]{:S(2)}) copy-start(pred[800,25]{0,1:T(8,128)(4,1)S(1)} %iota_compare_fusion) | copy-start | bytes 60004
  3.8 0.7 copy-start.30
  3.8 1.0 copy-start.1
  3.8 1.0 copy-start.28
  5.3 1.0 copy-start.22
  5.3 1.0 copy-start.24
  6.3 3.9 %copy-start = (f32[800,3200]{1,0:T(8,128)S(1)}, f32[800,3200]{1,0:T(8,128)}, u32[]{:S(2)}) copy-start(f32[800,3200]{1,0:T(8,128)} %sigma_ref.1) | copy-start | bytes 30720004
  13.5 61.0 %collective-permute-start.7 = (bf16[800,1600]{1,0:T(8,128)(2,1)}, bf16[800,1600]{1,0:T(8,128)(2,1)}, u32[]{:S(2)}, u32[]{:S(2)}) collective-permute-start(bf16[800,1600]{1,0:T(8,128)(2,1)} %get-tuple-element.15), channel_id=1, source_target_pairs={{0,2},{2,0},{4,6},{6,4},{8,10},{10,8},{12,14},{14,12},{1,3},{3,1},... | collective-permute-start | bytes 7680008 | tf_op jit(solution)/shard_map/ppermute | solution.py:234
  16.4 22.4 %collective-permute-start = (bf16[864,512]{1,0:T(8,128)(2,1)}, bf16[864,512]{1,0:T(8,128)(2,1)}, u32[]{:S(2)}, u32[]{:S(2)}) collective-permute-start(bf16[864,512]{1,0:T(8,128)(2,1)} %maximum_maximum_fusion), channel_id=1, source_target_pairs={{0,4},{2,6},{4,8},{6,10},{8,12},{10,14},{1,5},{3,7},{5,9},{7,11},{... | collective-permute-start | bytes 2654216 | tf_op jit(solution)/shard_map/ppermute | solution.py:176
  20.8 23.0 %collective-permute-start.3 = (bf16[864,512]{1,0:T(8,128)(2,1)}, bf16[864,512]{1,0:T(8,128)(2,1)}, u32[]{:S(2)}, u32[]{:S(2)}) collective-permute-start(bf16[864,512]{1,0:T(8,128)(2,1)} %maximum_maximum_fusion), channel_id=1, source_target_pairs={{4,0},{6,2},{8,4},{10,6},{12,8},{14,10},{5,1},{7,3},{9,5},{11,7},{... | collective-permute-start | bytes 2654216 | tf_op jit(solution)/shard_map/ppermute | solution.py:176
  22.8 24.1 %copy-start.2 = (f32[2,256,256]{2,1,0:T(8,128)S(1)}, f32[2,256,256]{2,1,0:T(8,128)}, u32[]{:S(2)}) copy-start(f32[2,256,256]{2,1,0:T(8,128)} %param.14) | copy-start | bytes 1572868
  22.8 24.1 %copy-start.19 = (bf16[2,800,256]{2,1,0:T(8,128)(2,1)S(1)}, bf16[2,800,256]{2,1,0:T(8,128)(2,1)}, u32[]{:S(2)}) copy-start(bf16[2,800,256]{2,1,0:T(8,128)(2,1)} %param.12) | copy-start | bytes 2457604
  38.8 40.4 %collective-permute-start.1 = (bf16[864,512]{1,0:T(8,128)(2,1)}, bf16[864,512]{1,0:T(8,128)(2,1)}, u32[]{:S(2)}, u32[]{:S(2)}) collective-permute-start(bf16[864,512]{1,0:T(8,128)(2,1)} %collective-permute-done), channel_id=1, source_target_pairs={{4,8},{6,10},{8,12},{10,14},{5,9},{7,11},{9,13},{11,15},{20,24},{2... | collective-permute-start | bytes 2654216 | tf_op jit(solution)/shard_map/ppermute | solution.py:176
  43.9 37.0 %collective-permute-start.4 = (bf16[864,512]{1,0:T(8,128)(2,1)}, bf16[864,512]{1,0:T(8,128)(2,1)}, u32[]{:S(2)}, u32[]{:S(2)}) collective-permute-start(bf16[864,512]{1,0:T(8,128)(2,1)} %collective-permute-done.3), channel_id=1, source_target_pairs={{4,0},{6,2},{8,4},{10,6},{5,1},{7,3},{9,5},{11,7},{20,16},{22,18},... | collective-permute-start | bytes 2654216 | tf_op jit(solution)/shard_map/ppermute | solution.py:176
  47.3 28.1 %copy-start.15 = (bf16[2,800,256]{2,1,0:T(8,128)(2,1)}, bf16[2,800,256]{2,1,0:T(8,128)(2,1)S(1)}, u32[]{:S(2)}) copy-start(bf16[2,800,256]{2,1,0:T(8,128)(2,1)S(1)} %add_convert_fusion.1) | copy-start | bytes 2457604
  47.4 50.2 %copy-start.8 = (bf16[800,256]{1,0:T(8,128)(2,1)}, bf16[800,256]{1,0:T(8,128)(2,1)S(1)}, u32[]{:S(2)}) copy-start(bf16[800,256]{1,0:T(8,128)(2,1)S(1)} %get-tuple-element.43) | copy-start | bytes 1228804
  47.4 50.2 %copy-start.11 = (bf16[800,256]{1,0:T(8,128)(2,1)}, bf16[800,256]{1,0:T(8,128)(2,1)S(1)}, u32[]{:S(2)}) copy-start(bf16[800,256]{1,0:T(8,128)(2,1)S(1)} %get-tuple-element.44) | copy-start | bytes 1228804
  74.5 58.4 %collective-permute-start.8 = (bf16[800,1600]{1,0:T(8,128)(2,1)}, bf16[800,1600]{1,0:T(8,128)(2,1)}, u32[]{:S(2)}, u32[]{:S(2)}) collective-permute-start(bf16[800,1600]{1,0:T(8,128)(2,1)} %collective-permute-done.7), channel_id=1, source_target_pairs={{0,1},{1,0},{2,3},{3,2},{4,5},{5,4},{6,7},{7,6},{8,9},{9,8},{10,11... | collective-permute-start | bytes 7680008 | tf_op jit(solution)/shard_map/ppermute | solution.py:236
  75.4 22.2 %collective-permute-start.11 = (bf16[800,512]{1,0:T(8,128)(2,1)}, bf16[800,512]{1,0:T(8,128)(2,1)S(1)}, u32[]{:S(2)}, u32[]{:S(2)}) collective-permute-start(bf16[800,512]{1,0:T(8,128)(2,1)} %pad_maximum_fusion.15), channel_id=1, source_target_pairs={{0,4},{2,6},{4,8},{6,10},{8,12},{10,14},{1,5},{3,7},{5,9},{7,11},{... | collective-permute-start | bytes 2457608 | tf_op jit(solution)/shard_map/ppermute | solution.py:176
  79.3 44.7 %collective-permute-start.2 = (bf16[864,512]{1,0:T(8,128)(2,1)}, bf16[864,512]{1,0:T(8,128)(2,1)}, u32[]{:S(2)}, u32[]{:S(2)}) collective-permute-start(bf16[864,512]{1,0:T(8,128)(2,1)} %collective-permute-done.1), channel_id=1, source_target_pairs={{8,12},{10,14},{9,13},{11,15},{24,28},{26,30},{25,29},{27,31}} | collective-permute-start | bytes 2654216 | tf_op jit(solution)/shard_map/ppermute | solution.py:176
  80.8 44.4 %collective-permute-start.5 = (bf16[864,512]{1,0:T(8,128)(2,1)}, bf16[864,512]{1,0:T(8,128)(2,1)}, u32[]{:S(2)}, u32[]{:S(2)}) collective-permute-start(bf16[864,512]{1,0:T(8,128)(2,1)} %collective-permute-done.4), channel_id=1, source_target_pairs={{4,0},{6,2},{5,1},{7,3},{20,16},{22,18},{21,17},{23,19}} | collective-permute-start | bytes 2654216 | tf_op jit(solution)/shard_map/ppermute | solution.py:176
  82.1 40.2 %collective-permute-start.13 = (bf16[800,512]{1,0:T(8,128)(2,1)}, bf16[800,512]{1,0:T(8,128)(2,1)}, u32[]{:S(2)}, u32[]{:S(2)}) collective-permute-start(bf16[800,512]{1,0:T(8,128)(2,1)} %pad_maximum_fusion.15), channel_id=1, source_target_pairs={{4,0},{6,2},{8,4},{10,6},{12,8},{14,10},{5,1},{7,3},{9,5},{11,7},{... | collective-permute-start | bytes 2457608 | tf_op jit(solution)/shard_map/ppermute | solution.py:176
  97.7 0.9 copy-start.21
  98.6 40.0 %collective-permute-start.6 = (bf16[800,1600]{1,0:T(8,128)(2,1)S(1)}, bf16[800,1600]{1,0:T(8,128)(2,1)}, u32[]{:S(2)}, u32[]{:S(2)}) collective-permute-start(bf16[800,1600]{1,0:T(8,128)(2,1)S(1)} %get-tuple-element.14), channel_id=1, source_target_pairs={{0,1},{1,0},{2,3},{3,2},{4,5},{5,4},{6,7},{7,6},{8,9},{9,8},{10,11... | collective-permute-start | bytes 7680008 | tf_op jit(solution)/shard_map/ppermute | solution.py:235
  122.4 40.1 %collective-permute-start.12 = (bf16[800,512]{1,0:T(8,128)(2,1)}, bf16[800,512]{1,0:T(8,128)(2,1)}, u32[]{:S(2)}, u32[]{:S(2)}) collective-permute-start(bf16[800,512]{1,0:T(8,128)(2,1)} %copy-done.21), channel_id=1, source_target_pairs={{4,8},{6,10},{8,12},{10,14},{5,9},{7,11},{9,13},{11,15},{20,24},{2... | collective-permute-start | bytes 2457608 | tf_op jit(solution)/shard_map/ppermute | solution.py:176
  123.9 38.5 %collective-permute-start.14 = (bf16[800,512]{1,0:T(8,128)(2,1)}, bf16[800,512]{1,0:T(8,128)(2,1)}, u32[]{:S(2)}, u32[]{:S(2)}) collective-permute-start(bf16[800,512]{1,0:T(8,128)(2,1)} %collective-permute-done.13), channel_id=1, source_target_pairs={{4,0},{6,2},{8,4},{10,6},{5,1},{7,3},{9,5},{11,7},{20,16},{22,18},... | collective-permute-start | bytes 2457608 | tf_op jit(solution)/shard_map/ppermute | solution.py:176
  132.8 5.0 %copy-start.23 = (bf16[64,256]{1,0:T(8,128)(2,1)S(1)}, bf16[64,256]{1,0:T(8,128)(2,1)}, u32[]{:S(2)}) copy-start(bf16[64,256]{1,0:T(8,128)(2,1)} %copy-done.22) | copy-start | bytes 98308
  132.9 5.0 %copy-start.25 = (bf16[64,256]{1,0:T(8,128)(2,1)S(1)}, bf16[64,256]{1,0:T(8,128)(2,1)}, u32[]{:S(2)}) copy-start(bf16[64,256]{1,0:T(8,128)(2,1)} %copy-done.24) | copy-start | bytes 98308
  136.3 29.2 %collective-permute-start.9 = (bf16[800,512]{1,0:T(8,128)(2,1)S(1)}, bf16[800,512]{1,0:T(8,128)(2,1)S(1)}, u32[]{:S(2)}, u32[]{:S(2)}) collective-permute-start(bf16[800,512]{1,0:T(8,128)(2,1)S(1)} %add_convert_fusion.2), channel_id=1, source_target_pairs={{0,2},{2,0},{4,6},{6,4},{8,10},{10,8},{12,14},{14,12},{1,3},{3,1},... | collective-permute-start | bytes 2457608 | tf_op jit(solution)/shard_map/ppermute | solution.py:261
  138.0 23.6 %collective-permute-start.10 = (bf16[4,64,512]{2,1,0:T(8,128)(2,1)S(1)}, bf16[4,64,512]{2,1,0:T(8,128)(2,1)S(1)}, u32[]{:S(2)}, u32[]{:S(2)}) collective-permute-start(bf16[4,64,512]{2,1,0:T(8,128)(2,1)S(1)} %get-tuple-element.48), channel_id=1, source_target_pairs={{0,2},{2,0},{4,6},{6,4},{8,10},{10,8},{12,14},{14,12},{1,3},{3,1},... | collective-permute-start | bytes 786440 | tf_op jit(solution)/shard_map/ppermute | solution.py:267
  162.5 4.7 %copy-start.9 = (bf16[800,256]{1,0:T(8,128)(2,1)S(1)}, bf16[800,256]{1,0:T(8,128)(2,1)}, u32[]{:S(2)}) copy-start(bf16[800,256]{1,0:T(8,128)(2,1)} %copy-done.8) | copy-start | bytes 1228804
  162.5 4.7 %copy-start.12 = (bf16[800,256]{1,0:T(8,128)(2,1)S(1)}, bf16[800,256]{1,0:T(8,128)(2,1)}, u32[]{:S(2)}) copy-start(bf16[800,256]{1,0:T(8,128)(2,1)} %copy-done.11) | copy-start | bytes 1228804
  162.5 13.1 %collective-permute-start.15 = (bf16[800,512]{1,0:T(8,128)(2,1)}, bf16[800,512]{1,0:T(8,128)(2,1)}, u32[]{:S(2)}, u32[]{:S(2)}) collective-permute-start(bf16[800,512]{1,0:T(8,128)(2,1)} %collective-permute-done.12), channel_id=1, source_target_pairs={{8,12},{10,14},{9,13},{11,15},{24,28},{26,30},{25,29},{27,31}} | collective-permute-start | bytes 2457608 | tf_op jit(solution)/shard_map/ppermute | solution.py:176
  164.2 30.6 %collective-permute-start.16 = (bf16[800,512]{1,0:T(8,128)(2,1)}, bf16[800,512]{1,0:T(8,128)(2,1)}, u32[]{:S(2)}, u32[]{:S(2)}) collective-permute-start(bf16[800,512]{1,0:T(8,128)(2,1)} %collective-permute-done.14), channel_id=1, source_target_pairs={{4,0},{6,2},{5,1},{7,3},{20,16},{22,18},{21,17},{23,19}} | collective-permute-start | bytes 2457608 | tf_op jit(solution)/shard_map/ppermute | solution.py:176
  167.2 2.3 copy-start.6
  169.4 25.3 %copy-start.10 = (bf16[800,256]{1,0:T(8,128)(2,1)S(1)}, bf16[800,256]{1,0:T(8,128)(2,1)}, u32[]{:S(2)}) copy-start(bf16[800,256]{1,0:T(8,128)(2,1)} %copy-done.8) | copy-start | bytes 1228804
  169.4 25.3 %copy-start.13 = (bf16[800,256]{1,0:T(8,128)(2,1)S(1)}, bf16[800,256]{1,0:T(8,128)(2,1)}, u32[]{:S(2)}) copy-start(bf16[800,256]{1,0:T(8,128)(2,1)} %copy-done.11) | copy-start | bytes 1228804
  169.4 53.2 %all-to-all-start = ((bf16[8,64,1024]{2,1,0:T(8,128)(2,1)}), bf16[8,64,1024]{2,1,0:T(8,128)(2,1)}, u32[]{:S(2)}, u32[]{:S(2)}) async-start(bf16[8,64,1024]{2,1,0:T(8,128)(2,1)} %bitcast.78), calls=%async_computation | async-start | bytes 2097152 | tf_op jit(solution)/shard_map/all_to_all | solution.py:200
  201.6 7.1 %copy-start.7 = (f32[800,512]{1,0:T(8,128)S(1)}, f32[800,512]{1,0:T(8,128)}, u32[]{:S(2)}) copy-start(f32[800,512]{1,0:T(8,128)} %copy-done.6) | copy-start | bytes 4915204
  205.1 14.7 %collective-permute-start.17 = (bf16[800,512]{1,0:T(8,128)(2,1)S(1)}, bf16[800,512]{1,0:T(8,128)(2,1)S(1)}, u32[]{:S(2)}, u32[]{:S(2)}) collective-permute-start(bf16[800,512]{1,0:T(8,128)(2,1)S(1)} %add_convert_fusion), channel_id=1, source_target_pairs={{0,2},{2,0},{4,6},{6,4},{8,10},{10,8},{12,14},{14,12},{1,3},{3,1},... | collective-permute-start | bytes 2457608 | tf_op jit(solution)/shard_map/ppermute | solution.py:292
  211.6 8.2 %copy-start.14 = (bf16[4,2,64,512]{3,2,1,0:T(8,128)(2,1)S(1)}, bf16[4,2,64,512]{3,2,1,0:T(8,128)(2,1)}, u32[]{:S(2)}) copy-start(bf16[4,2,64,512]{3,2,1,0:T(8,128)(2,1)} %copy.20) | copy-start | bytes 1572868
  221.4 2.7 %copy-start.5 = (f32[1,512,512]{2,1,0:T(8,128)S(1)}, f32[1,512,512]{2,1,0:T(8,128)}, u32[]{:S(2)}) copy-start(f32[1,512,512]{2,1,0:T(8,128)} %param.10) | copy-start | bytes 3145732
  224.1 2.1 copy-start.16
  224.1 2.1 copy-start.20
  224.9 2.0 copy-start.26
  226.6 4.5 %copy-start.17 = (f32[1,800,256]{2,1,0:T(8,128)S(1)}, f32[1,800,256]{2,1,0:T(8,128)}, u32[]{:S(2)}) copy-start(f32[1,800,256]{2,1,0:T(8,128)} %get-tuple-element.41) | copy-start | bytes 2457604
  226.6 4.5 %copy-start.18 = (f32[1,800,256]{2,1,0:T(8,128)S(1)}, f32[1,800,256]{2,1,0:T(8,128)}, u32[]{:S(2)}) copy-start(f32[1,800,256]{2,1,0:T(8,128)} %get-tuple-element.42) | copy-start | bytes 2457604
  227.7 11.6 %all-to-all-start.1 = ((bf16[8,32,512]{2,1,0:T(8,128)(2,1)}), bf16[8,32,512]{2,1,0:T(8,128)(2,1)S(1)}, u32[]{:S(2)}, u32[]{:S(2)}) async-start(bf16[8,32,512]{2,1,0:T(8,128)(2,1)} %pad_maximum_fusion.17), calls=%async_computation.1 | async-start | bytes 524288 | tf_op jit(solution)/shard_map/all_to_all | solution.py:200
  231.1 1.3 copy-start.27
  231.1 8.2 %copy-start.3 = (f32[2,256,256]{2,1,0:T(8,128)S(1)}, f32[2,256,256]{2,1,0:T(8,128)}, u32[]{:S(2)}) copy-start(f32[2,256,256]{2,1,0:T(8,128)} %param.14) | copy-start | bytes 1572868

commit v5 on v3

--- a/solution.py
+++ b/solution.py
@@ -104,8 +104,16 @@
 
 
 def masked_product(lower_part, pattern, weights, first_row):
-    mask = expand_pattern(pattern, first_row, lower_part.shape[1], B).astype(jnp.bfloat16)
-    masked = lower_part * mask
+    block_ids = (first_row + lax.iota(jnp.int32, lower_part.shape[1])) // B
+    picked = (block_ids[:, None] == lax.iota(jnp.int32, pattern.shape[1])[None, :])[None, :, :, None]
+    spread = jnp.sum(jnp.where(picked, pattern[:, None], 0), axis=2).astype(jnp.bfloat16)
+    masked = jnp.concatenate(
+        [
+            lower_part[:, :, k * B : (k + 1) * B] * spread[:, :, k : k + 1]
+            for k in range(pattern.shape[2])
+        ],
+        axis=2,
+    )
     high, low = split_high_low(weights)
     both = jnp.einsum(
         "nrk,nkc->nrc", masked, high, preferred_element_type=jnp.float32
@@ -176,6 +184,22 @@
         at = lax.rem(layer - back + layers, layers)
         gathered = lax.dynamic_update_slice(gathered, piece[None], (at, 0, 0))
     return gathered
+
+
+def line_pick(block, hops, layers, layer, first):
+    by_distance = [block] + [
+        jnp.where(layer >= back, hops[back - 1][0], hops[layers - back - 1][1])
+        for back in range(1, layers)
+    ]
+
+    def at(place):
+        back = lax.rem(layer - place + 2 * layers, layers)
+        found = by_distance[0]
+        for distance in range(1, layers):
+            found = jnp.where(back == distance, by_distance[distance], found)
+        return found
+
+    return [at(first + place) for place in range(layers)]
 
 
 def tie(values, after):
@@ -267,7 +291,9 @@
     sep_two = sums[:, sep_width:] - dot(diag_rows.astype(jnp.bfloat16), all_sep)
     short_sep = sep_two.astype(jnp.bfloat16)
 
-    near_two, far_two, away_two = root_parts(line_order(own_two, hops_two, layers, layer))
+    picked = line_pick(own_two, hops_two, layers, layer, core * half)
+    near_two, far_two = jnp.concatenate(picked[:half]), jnp.concatenate(picked[half:])
+    away_two = (dot(taken, near_two) + dot(taken_sibling, far_two)).astype(jnp.bfloat16)
     arrived_two = lax.ppermute(away_two, "prow", swap_side)
     product_two = root_total(near_two, far_two, arrived_two)
     two_root = dot(short_one, all_sep) - product_two

time: 202 us -> 195 us (0.965)
  local copies, waits for them, and re-layouts: 16.3 us -> 8.16 us
  waiting for transfers between devices: 84.6 us -> 87.5 us
    ppermute x1, waiting for transfers between devices: 7 us -> 13.8 us  [on_pairs(): arrived_two = lax.ppermute(away_two, 'prow', swap_side)]
    ppermute x6, waiting for transfers between devices: 56.8 us -> 50.1 us  [line_hop(): lax.ppermute(held[1], 'prow', down)]
    dynamic_update_slice x6 -> x3, other arithmetic: 10.1 us -> 4.37 us  [line_order(): gathered = lax.dynamic_update_slice(gathered, piece[None], (at, 0, 0))]
    select_n x2 -> x4, other arithmetic: 0.02 us -> 3.64 us  [the longest x2 3.62 us: at(): found = jnp.where(back == distance, by_distance[distance], found)]
    convert_element_type x2 -> x0, local copies, waits for them, and re-layouts: 3.41 us -> none  [masked_product(): expand_pattern(pattern, first_row, lower_part.shape[1], B)]
    dynamic_slice x2 -> x1, local copies, waits for them, and re-layouts: 2.44 us -> 0.21 us  [root_parts(): lax.dynamic_slice_in_dim(gathered, (1 - core) * half, half, 0)]
    unnamed x62 -> x52, local copies, waits for them, and re-layouts: 6.55 us -> 5.76 us
  transfers between devices with their start and end apart: 20 -> 20, of which waited for: 9 -> 8; matrix products, arithmetic and copies ran while one was open for 28% -> 25% of each run, Pallas kernels for 0% -> 0%
where the time goes in v5:
time: 195 us; the launch traced here: 194 us
  waiting for transfers between devices  87.5 us (45%)
  starting transfers between devices  42.6 us (22%)
  matrix products  30.9 us (16%)
  other arithmetic  19.7 us (10%)
  local copies, waits for them, and re-layouts  8.16 us (4%)
  Pallas kernels  3.34 us (2%)
    ppermute x6, waiting for transfers between devices, line_hop(): lax.ppermute(held[1], 'prow', down)  50.1 us
    dot_general x10, matrix products, dot(): return jnp.dot(left, right, preferred_element_type=jnp.float32)  21.9 us
    ppermute x6, starting transfers between devices, line_hop(): lax.ppermute(held[0], 'prow', up)  18.3 us
    ppermute x1, waiting for transfers between devices, on_pairs(): arrived_two = lax.ppermute(away_two, 'prow', swap_side)  13.8 us
    ppermute x6, waiting for transfers between devices, line_hop(): lax.ppermute(held[0], 'prow', up)  10.2 us
    all_to_all x2, starting transfers between devices, scatter_sum(): moved = lax.all_to_all(parts.astype(jnp.bfloat16), 'prow', 0, 0, tiled=True)  8.46 us
    ppermute x1, waiting for transfers between devices, on_pairs(): arrived_one = lax.ppermute(away_one, 'prow', swap_side)  8.27 us
    ppermute x6, starting transfers between devices, line_hop(): lax.ppermute(held[1], 'prow', down)  7.68 us
  transfers between devices with their start and end apart: 20, of which 8 were waited for; matrix products, arithmetic and copies ran while one was open for 25% of the time, Pallas kernels for 0%

profile of v5, /device:TPU:0, one launch (start us, length us, event | category | flops | bytes accessed | tf_op | source)
XLA Modules:
  0.0 193.6 jit_solution(12999209782478708582)
XLA Ops:
  0.6 3.9 %copy-done = f32[800,3200]{1,0:T(8,128)S(1)} copy-done((f32[800,3200]{1,0:T(8,128)S(1)}, f32[800,3200]{1,0:T(8,128)}, u32[]{:S(2)}) %copy-start) | copy-done | bytes 10240024
  4.6 3.3 %shard_map.119 = (bf16[800,1600]{1,0:T(8,128)(2,1)S(1)}, bf16[800,1600]{1,0:T(8,128)(2,1)}) custom-call(s32[1]{0:T(128)} %bitcast.side_ref, f32[800,3200]{1,0:T(8,128)S(1)} %copy-done), custom_call_target="tpu_custom_call" | custom-call | bytes 15360000 | tf_op jit(solution)/shard_map/pallas_call | solution.py:157
  7.9 2.9 %collective-permute-start.7 = (bf16[800,1600]{1,0:T(8,128)(2,1)}, bf16[800,1600]{1,0:T(8,128)(2,1)}, u32[]{:S(2)}, u32[]{:S(2)}) collective-permute-start(bf16[800,1600]{1,0:T(8,128)(2,1)} %get-tuple-element.13), channel_id=1, source_target_pairs={{0,2},{2,0},{4,6},{6,4},{8,10},{10,8},{12,14},{14,12},{1,3},{3,1},... | collective-permute-start | bytes 7680008 | tf_op jit(solution)/shard_map/ppermute | solution.py:243
  11.9 1.4 slice_multiply_fusion.1
  13.3 0.6 fusion.20
  13.9 0.6 add_convert_fusion.3
  14.5 0.9 copy-done.4
  15.4 1.0 maximum_maximum_fusion
  16.4 1.3 collective-permute-start.1
  17.7 5.5 %collective-permute-start = (bf16[864,512]{1,0:T(8,128)(2,1)}, bf16[864,512]{1,0:T(8,128)(2,1)}, u32[]{:S(2)}, u32[]{:S(2)}) collective-permute-start(bf16[864,512]{1,0:T(8,128)(2,1)} %maximum_maximum_fusion), channel_id=1, source_target_pairs={{0,4},{2,6},{4,8},{6,10},{8,12},{10,14},{1,5},{3,7},{5,9},{7,11},{... | collective-permute-start | bytes 2654216 | tf_op jit(solution)/shard_map/ppermute | solution.py:176
  23.3 16.4 %collective-permute-done.1 = bf16[864,512]{1,0:T(8,128)(2,1)} collective-permute-done((bf16[864,512]{1,0:T(8,128)(2,1)}, bf16[864,512]{1,0:T(8,128)(2,1)}, u32[]{:S(2)}, u32[]{:S(2)}) %collective-permute-start.1) | collective-permute-done | bytes 884768 | tf_op jit(solution)/shard_map/ppermute | solution.py:176
  39.7 1.3 collective-permute-start.2
  41.2 1.6 fusion.18
  42.8 0.4 add_convert_fusion.1
  43.2 1.6 collective-permute-start.4
  44.9 17.2 %collective-permute-done.2 = bf16[864,512]{1,0:T(8,128)(2,1)} collective-permute-done((bf16[864,512]{1,0:T(8,128)(2,1)}, bf16[864,512]{1,0:T(8,128)(2,1)}, u32[]{:S(2)}, u32[]{:S(2)}) %collective-permute-start.2) | collective-permute-done | bytes 884768 | tf_op jit(solution)/shard_map/ppermute | solution.py:176
  62.1 1.3 collective-permute-start.3
  63.4 1.0 pad_maximum_fusion.7
  64.3 6.5 %collective-permute-start.11 = (bf16[800,512]{1,0:T(8,128)(2,1)}, bf16[800,512]{1,0:T(8,128)(2,1)}, u32[]{:S(2)}, u32[]{:S(2)}) collective-permute-start(bf16[800,512]{1,0:T(8,128)(2,1)} %pad_maximum_fusion.7), channel_id=1, source_target_pairs={{0,4},{2,6},{4,8},{6,10},{8,12},{10,14},{1,5},{3,7},{5,9},{7,11},{... | collective-permute-start | bytes 2457608 | tf_op jit(solution)/shard_map/ppermute | solution.py:176
  70.8 1.3 collective-permute-start.13
  72.2 1.6 collective-permute-start.5
  73.8 0.3 broadcast_in_dim.97
  74.1 0.9 copy-done.5
  75.1 10.2 %collective-permute-done.11 = bf16[800,512]{1,0:T(8,128)(2,1)} collective-permute-done((bf16[800,512]{1,0:T(8,128)(2,1)}, bf16[800,512]{1,0:T(8,128)(2,1)}, u32[]{:S(2)}, u32[]{:S(2)}) %collective-permute-start.11) | collective-permute-done | bytes 819232 | tf_op jit(solution)/shard_map/ppermute | solution.py:176
  85.3 15.8 %collective-permute-done.13 = bf16[800,512]{1,0:T(8,128)(2,1)} collective-permute-done((bf16[800,512]{1,0:T(8,128)(2,1)}, bf16[800,512]{1,0:T(8,128)(2,1)}, u32[]{:S(2)}, u32[]{:S(2)}) %collective-permute-start.13) | collective-permute-done | bytes 819232 | tf_op jit(solution)/shard_map/ppermute | solution.py:176
  101.1 1.6 collective-permute-start.12
  102.7 1.3 collective-permute-start.14
  104.0 1.5 bitcast_dynamic-update-slice_fusion.2
  105.4 1.5 bitcast_dynamic-update-slice_fusion.1
  106.9 1.5 bitcast_dynamic-update-slice_fusion
  108.6 1.1 collective-permute-start.10
  109.9 3.4 %fusion.63 = f32[800,512]{1,0:T(8,128)S(1)} fusion(bf16[800,1600]{1,0:T(8,128)(2,1)} %collective-permute-done.7, bf16[1600,512]{1,0:T(8,128)(2,1)S(1)} %bitcast.88), kind=kOutput, calls=%fused_computation.129 | convolution fusion | flops 1310720000 | bytes 5836800 | tf_op jit(solution)/shard_map/dot_general | solution.py:125
  113.4 3.4 %add_convert_fusion.2 = bf16[800,512]{1,0:T(8,128)(2,1)S(1)} fusion(f32[800,512]{1,0:T(8,128)S(1)} %fusion.63, bf16[800,1600]{1,0:T(8,128)(2,1)} %collective-permute-done.8, bf16[1600,512]{1,0:T(8,128)(2,1)S(1)} %bitcast.86), kind=kOutput, calls=%fused_computation.15 | convolution fusion | flops 1311539200 | bytes 6656000 | tf_op jit(solution)/shard_map/dot_general | solution.py:125
  116.8 1.1 collective-permute-start.9
  117.8 1.6 fusion.61
  119.5 1.6 fusion.62
  121.2 0.7 collective-permute-done.14
  121.8 1.5 collective-permute-start.15
  123.4 1.3 collective-permute-start.16
  124.7 0.9 maximum_select_fusion
  125.5 8.3 %collective-permute-done.9 = bf16[800,512]{1,0:T(8,128)(2,1)S(1)} collective-permute-done((bf16[800,512]{1,0:T(8,128)(2,1)S(1)}, bf16[800,512]{1,0:T(8,128)(2,1)S(1)}, u32[]{:S(2)}, u32[]{:S(2)}) %collective-permute-start.9) | collective-permute-done | bytes 819232 | tf_op jit(solution)/shard_map/ppermute | solution.py:268
  133.8 1.7 negate_bitcast_fusion
  135.5 2.2 %fusion.6 = bf16[512,1024]{1,0:T(8,128)(2,1)} fusion(bf16[800,256]{1,0:T(8,128)(2,1)S(1)} %copy-done.10, bf16[800,256]{1,0:T(8,128)(2,1)S(1)} %copy-done.7, bf16[800,512]{1,0:T(8,128)(2,1)S(1)} %copy-done.5, bf16[800,512]{1,0:T(8,128)(2,1)S(1)} %get-tuple-element.26), kind=kOutput, calls=%fused_computation.19 | convolution fusion | flops 844300288 | bytes 3506176 | tf_op jit(solution)/shard_map/dot_general | solution.py:129
  137.7 4.4 %all-to-all-start = ((bf16[8,64,1024]{2,1,0:T(8,128)(2,1)}), bf16[8,64,1024]{2,1,0:T(8,128)(2,1)}, u32[]{:S(2)}, u32[]{:S(2)}) async-start(bf16[8,64,1024]{2,1,0:T(8,128)(2,1)} %bitcast.90), calls=%async_computation | async-start | bytes 2097152 | tf_op jit(solution)/shard_map/all_to_all | solution.py:210
  142.2 2.8 %select_select_fusion.1 = (bf16[800,512]{1,0:T(8,128)(2,1)S(1)}, bf16[800,512]{1,0:T(8,128)(2,1)S(1)}, bf16[800,512]{1,0:T(8,128)(2,1)S(1)}, bf16[800,512]{1,0:T(8,128)(2,1)S(1)}) fusion(pred[]{:T(512)S(6)} %eq.94, pred[]{:T(512)S(6)} %eq.93, pred[]{:T(512)S(6)} %eq.92, bf16[800,256]{1,0:T(8,128)(2,1)} %copy-done.9, bf16[800,256]{1,0:T(8,128)(2,1)} %copy-done.6, ...), kind=kLoop, calls=%fused_computation.44 | loop fusion | flops 4096000 | bytes 9011206 | tf_op jit(solution)/shard_map/jit(_where)/select_n | solution.py:199
  145.0 0.8 select_select_fusion
  145.9 3.4 %fusion.13 = f32[800,512]{1,0:T(8,128)S(1)} fusion(bf16[800,1600]{1,0:T(8,128)(2,1)} %collective-permute-done.7, bf16[800,512]{1,0:T(8,128)(2,1)S(1)} %get-tuple-element.30, bf16[800,512]{1,0:T(8,128)(2,1)S(1)} %get-tuple-element.31), kind=kOutput, calls=%fused_computation.30 | convolution fusion | flops 1313996800 | bytes 5836800 | tf_op jit(solution)/shard_map/dot_general | solution.py:125
  149.3 3.4 %add_convert_fusion = bf16[800,512]{1,0:T(8,128)(2,1)S(1)} fusion(f32[800,512]{1,0:T(8,128)S(1)} %fusion.13, bf16[800,1600]{1,0:T(8,128)(2,1)} %collective-permute-done.8, bf16[800,512]{1,0:T(8,128)(2,1)S(1)} %get-tuple-element.29, bf16[800,512]{1,0:T(8,128)(2,1)S(1)} %get-tuple-element.21), kind=kOutput, calls=%fused_computation.11 | convolution fusion | flops 1314816000 | bytes 6656000 | tf_op jit(solution)/shard_map/dot_general | solution.py:125
  152.7 3.0 %collective-permute-start.17 = (bf16[800,512]{1,0:T(8,128)(2,1)S(1)}, bf16[800,512]{1,0:T(8,128)(2,1)S(1)}, u32[]{:S(2)}, u32[]{:S(2)}) collective-permute-start(bf16[800,512]{1,0:T(8,128)(2,1)S(1)} %add_convert_fusion), channel_id=1, source_target_pairs={{0,2},{2,0},{4,6},{6,4},{8,10},{10,8},{12,14},{14,12},{1,3},{3,1},... | collective-permute-start | bytes 2457608 | tf_op jit(solution)/shard_map/ppermute | solution.py:297
  155.7 1.6 fusion.14
  157.4 1.6 fusion.12
  159.0 13.8 %collective-permute-done.17 = bf16[800,512]{1,0:T(8,128)(2,1)S(1)} collective-permute-done((bf16[800,512]{1,0:T(8,128)(2,1)S(1)}, bf16[800,512]{1,0:T(8,128)(2,1)S(1)}, u32[]{:S(2)}, u32[]{:S(2)}) %collective-permute-start.17) | collective-permute-done | bytes 819232 | tf_op jit(solution)/shard_map/ppermute | solution.py:297
  172.8 1.5 fusion.60
  174.3 1.3 slice_bitcast_fusion.1
  175.6 1.4 convert_reduce_fusion
  177.1 0.8 convolution_add_fusion.2
  178.5 0.3 fusion.9
  178.9 0.3 fusion.10
  179.2 0.7 pad_maximum_fusion.8
  179.9 4.0 %all-to-all-start.1 = ((bf16[8,32,512]{2,1,0:T(8,128)(2,1)}), bf16[8,32,512]{2,1,0:T(8,128)(2,1)S(1)}, u32[]{:S(2)}, u32[]{:S(2)}) async-start(bf16[8,32,512]{2,1,0:T(8,128)(2,1)} %pad_maximum_fusion.8), calls=%async_computation.1 | async-start | bytes 524288 | tf_op jit(solution)/shard_map/all_to_all | solution.py:210
  184.0 2.4 %pad_maximum_fusion.2 = f32[2,800,256]{2,1,0:T(8,128)} fusion(f32[1,800,256]{2,1,0:T(8,128)} %get-tuple-element.35, f32[1,800,256]{2,1,0:T(8,128)S(1)} %copy-done.15), kind=kLoop, calls=%fused_computation.9 | loop fusion | flops 409600 | bytes 3276800 | tf_op jit(solution)/shard_map/stack | solution.py:313
  186.4 0.7 pad_maximum_fusion.9
  187.1 5.1 %all-to-all-done.1 = bf16[8,32,512]{2,1,0:T(8,128)(2,1)S(1)} async-done(((bf16[8,32,512]{2,1,0:T(8,128)(2,1)}), bf16[8,32,512]{2,1,0:T(8,128)(2,1)S(1)}, u32[]{:S(2)}, u32[]{:S(2)}) %all-to-all-start.1) | async-done | bytes 262176 | tf_op jit(solution)/shard_map/all_to_all | solution.py:210
  192.3 1.3 convolution_subtract_fusion.1
  (91 shorter events, 2.7 us)
Async XLA Ops:
  0.6 3.9 %copy-start = (f32[800,3200]{1,0:T(8,128)S(1)}, f32[800,3200]{1,0:T(8,128)}, u32[]{:S(2)}) copy-start(f32[800,3200]{1,0:T(8,128)} %sigma_ref.1) | copy-start | bytes 30720004
  4.6 6.3 %copy-start.23 = (s32[1,25,2]{1,2,0:T(2,128)S(1)}, s32[1,25,2]{1,2,0:T(2,128)}, u32[]{:S(2)}) copy-start(s32[1,25,2]{1,2,0:T(2,128)} %param.11) | copy-start | bytes 604
  4.6 6.7 %copy-start.22 = (s32[2,27,1]{1,2,0:T(1,128)S(1)}, s32[2,27,1]{1,2,0:T(1,128)}, u32[]{:S(2)}) copy-start(s32[2,27,1]{1,2,0:T(1,128)} %param.15) | copy-start | bytes 652
  4.6 6.9 %copy-start.1 = (f32[2,256,256]{2,1,0:T(8,128)S(1)}, f32[2,256,256]{2,1,0:T(8,128)}, u32[]{:S(2)}) copy-start(f32[2,256,256]{2,1,0:T(8,128)} %param.14) | copy-start | bytes 1572868
  4.6 6.9 %copy-start.21 = (bf16[2,64,256]{2,1,0:T(8,128)(2,1)S(1)}, bf16[2,64,256]{2,1,0:T(8,128)(2,1)}, u32[]{:S(2)}) copy-start(bf16[2,64,256]{2,1,0:T(8,128)(2,1)} %param.13) | copy-start | bytes 196612
  7.9 64.2 %collective-permute-start.7 = (bf16[800,1600]{1,0:T(8,128)(2,1)}, bf16[800,1600]{1,0:T(8,128)(2,1)}, u32[]{:S(2)}, u32[]{:S(2)}) collective-permute-start(bf16[800,1600]{1,0:T(8,128)(2,1)} %get-tuple-element.13), channel_id=1, source_target_pairs={{0,2},{2,0},{4,6},{6,4},{8,10},{10,8},{12,14},{14,12},{1,3},{3,1},... | collective-permute-start | bytes 7680008 | tf_op jit(solution)/shard_map/ppermute | solution.py:243
  11.2 2.1 %copy-start.2 = (f32[1,512,512]{2,1,0:T(8,128)S(1)}, f32[1,512,512]{2,1,0:T(8,128)}, u32[]{:S(2)}) copy-start(f32[1,512,512]{2,1,0:T(8,128)} %param.10) | copy-start | bytes 3145732
  14.5 0.9 copy-start.4
  16.4 23.3 %collective-permute-start.1 = (bf16[864,512]{1,0:T(8,128)(2,1)}, bf16[864,512]{1,0:T(8,128)(2,1)}, u32[]{:S(2)}, u32[]{:S(2)}) collective-permute-start(bf16[864,512]{1,0:T(8,128)(2,1)} %maximum_maximum_fusion), channel_id=1, source_target_pairs={{4,0},{6,2},{8,4},{10,6},{12,8},{14,10},{5,1},{7,3},{9,5},{11,7},{... | collective-permute-start | bytes 2654216 | tf_op jit(solution)/shard_map/ppermute | solution.py:176
  17.7 25.5 %collective-permute-start = (bf16[864,512]{1,0:T(8,128)(2,1)}, bf16[864,512]{1,0:T(8,128)(2,1)}, u32[]{:S(2)}, u32[]{:S(2)}) collective-permute-start(bf16[864,512]{1,0:T(8,128)(2,1)} %maximum_maximum_fusion), channel_id=1, source_target_pairs={{0,4},{2,6},{4,8},{6,10},{8,12},{10,14},{1,5},{3,7},{5,9},{7,11},{... | collective-permute-start | bytes 2654216 | tf_op jit(solution)/shard_map/ppermute | solution.py:176
  23.3 19.5 %copy-start.16 = (bf16[2,800,256]{2,1,0:T(8,128)(2,1)S(1)}, bf16[2,800,256]{2,1,0:T(8,128)(2,1)}, u32[]{:S(2)}) copy-start(bf16[2,800,256]{2,1,0:T(8,128)(2,1)} %param.12) | copy-start | bytes 2457604
  39.7 22.4 %collective-permute-start.2 = (bf16[864,512]{1,0:T(8,128)(2,1)}, bf16[864,512]{1,0:T(8,128)(2,1)}, u32[]{:S(2)}, u32[]{:S(2)}) collective-permute-start(bf16[864,512]{1,0:T(8,128)(2,1)} %collective-permute-done.1), channel_id=1, source_target_pairs={{4,0},{6,2},{8,4},{10,6},{5,1},{7,3},{9,5},{11,7},{20,16},{22,18},... | collective-permute-start | bytes 2654216 | tf_op jit(solution)/shard_map/ppermute | solution.py:176
  43.2 21.1 %copy-start.13 = (bf16[2,800,256]{2,1,0:T(8,128)(2,1)}, bf16[2,800,256]{2,1,0:T(8,128)(2,1)S(1)}, u32[]{:S(2)}) copy-start(bf16[2,800,256]{2,1,0:T(8,128)(2,1)S(1)} %add_convert_fusion.1) | copy-start | bytes 2457604
  43.2 29.0 %collective-permute-start.4 = (bf16[864,512]{1,0:T(8,128)(2,1)}, bf16[864,512]{1,0:T(8,128)(2,1)}, u32[]{:S(2)}, u32[]{:S(2)}) collective-permute-start(bf16[864,512]{1,0:T(8,128)(2,1)} %collective-permute-done), channel_id=1, source_target_pairs={{4,8},{6,10},{8,12},{10,14},{5,9},{7,11},{9,13},{11,15},{20,24},{2... | collective-permute-start | bytes 2654216 | tf_op jit(solution)/shard_map/ppermute | solution.py:176
  44.9 18.5 %copy-start.6 = (bf16[800,256]{1,0:T(8,128)(2,1)}, bf16[800,256]{1,0:T(8,128)(2,1)S(1)}, u32[]{:S(2)}) copy-start(bf16[800,256]{1,0:T(8,128)(2,1)S(1)} %get-tuple-element.36) | copy-start | bytes 1228804
  44.9 19.4 %copy-start.9 = (bf16[800,256]{1,0:T(8,128)(2,1)}, bf16[800,256]{1,0:T(8,128)(2,1)S(1)}, u32[]{:S(2)}) copy-start(bf16[800,256]{1,0:T(8,128)(2,1)S(1)} %get-tuple-element.37) | copy-start | bytes 1228804
  62.1 40.6 %collective-permute-start.3 = (bf16[864,512]{1,0:T(8,128)(2,1)}, bf16[864,512]{1,0:T(8,128)(2,1)}, u32[]{:S(2)}, u32[]{:S(2)}) collective-permute-start(bf16[864,512]{1,0:T(8,128)(2,1)} %collective-permute-done.2), channel_id=1, source_target_pairs={{4,0},{6,2},{5,1},{7,3},{20,16},{22,18},{21,17},{23,19}} | collective-permute-start | bytes 2654216 | tf_op jit(solution)/shard_map/ppermute | solution.py:176
  64.3 20.9 %collective-permute-start.11 = (bf16[800,512]{1,0:T(8,128)(2,1)}, bf16[800,512]{1,0:T(8,128)(2,1)}, u32[]{:S(2)}, u32[]{:S(2)}) collective-permute-start(bf16[800,512]{1,0:T(8,128)(2,1)} %pad_maximum_fusion.7), channel_id=1, source_target_pairs={{0,4},{2,6},{4,8},{6,10},{8,12},{10,14},{1,5},{3,7},{5,9},{7,11},{... | collective-permute-start | bytes 2457608 | tf_op jit(solution)/shard_map/ppermute | solution.py:176
  70.8 30.3 %collective-permute-start.13 = (bf16[800,512]{1,0:T(8,128)(2,1)}, bf16[800,512]{1,0:T(8,128)(2,1)}, u32[]{:S(2)}, u32[]{:S(2)}) collective-permute-start(bf16[800,512]{1,0:T(8,128)(2,1)} %pad_maximum_fusion.7), channel_id=1, source_target_pairs={{4,0},{6,2},{8,4},{10,6},{12,8},{14,10},{5,1},{7,3},{9,5},{11,7},{... | collective-permute-start | bytes 2457608 | tf_op jit(solution)/shard_map/ppermute | solution.py:176
  72.1 41.2 %collective-permute-start.8 = (bf16[800,1600]{1,0:T(8,128)(2,1)}, bf16[800,1600]{1,0:T(8,128)(2,1)}, u32[]{:S(2)}, u32[]{:S(2)}) collective-permute-start(bf16[800,1600]{1,0:T(8,128)(2,1)} %collective-permute-done.7), channel_id=1, source_target_pairs={{0,1},{1,0},{2,3},{3,2},{4,5},{5,4},{6,7},{7,6},{8,9},{9,8},{10,11... | collective-permute-start | bytes 7680008 | tf_op jit(solution)/shard_map/ppermute | solution.py:245
  72.2 34.7 %collective-permute-start.5 = (bf16[864,512]{1,0:T(8,128)(2,1)}, bf16[864,512]{1,0:T(8,128)(2,1)}, u32[]{:S(2)}, u32[]{:S(2)}) collective-permute-start(bf16[864,512]{1,0:T(8,128)(2,1)} %collective-permute-done.4), channel_id=1, source_target_pairs={{8,12},{10,14},{9,13},{11,15},{24,28},{26,30},{25,29},{27,31}} | collective-permute-start | bytes 2654216 | tf_op jit(solution)/shard_map/ppermute | solution.py:176
  73.8 1.1 copy-start.5
  85.3 34.2 %collective-permute-start.6 = (bf16[800,1600]{1,0:T(8,128)(2,1)S(1)}, bf16[800,1600]{1,0:T(8,128)(2,1)S(1)}, u32[]{:S(2)}, u32[]{:S(2)}) collective-permute-start(bf16[800,1600]{1,0:T(8,128)(2,1)S(1)} %get-tuple-element.12), channel_id=1, source_target_pairs={{0,1},{1,0},{2,3},{3,2},{4,5},{5,4},{6,7},{7,6},{8,9},{9,8},{10,11... | collective-permute-start | bytes 7680008 | tf_op jit(solution)/shard_map/ppermute | solution.py:244
  101.1 20.0 %collective-permute-start.12 = (bf16[800,512]{1,0:T(8,128)(2,1)}, bf16[800,512]{1,0:T(8,128)(2,1)}, u32[]{:S(2)}, u32[]{:S(2)}) collective-permute-start(bf16[800,512]{1,0:T(8,128)(2,1)} %collective-permute-done.11), channel_id=1, source_target_pairs={{4,8},{6,10},{8,12},{10,14},{5,9},{7,11},{9,13},{11,15},{20,24},{2... | collective-permute-start | bytes 2457608 | tf_op jit(solution)/shard_map/ppermute | solution.py:176
  102.7 19.1 %collective-permute-start.14 = (bf16[800,512]{1,0:T(8,128)(2,1)}, bf16[800,512]{1,0:T(8,128)(2,1)}, u32[]{:S(2)}, u32[]{:S(2)}) collective-permute-start(bf16[800,512]{1,0:T(8,128)(2,1)} %collective-permute-done.13), channel_id=1, source_target_pairs={{4,0},{6,2},{8,4},{10,6},{5,1},{7,3},{9,5},{11,7},{20,16},{22,18},... | collective-permute-start | bytes 2457608 | tf_op jit(solution)/shard_map/ppermute | solution.py:176
  108.6 16.0 %collective-permute-start.10 = (bf16[4,64,512]{2,1,0:T(8,128)(2,1)S(1)}, bf16[4,64,512]{2,1,0:T(8,128)(2,1)S(1)}, u32[]{:S(2)}, u32[]{:S(2)}) collective-permute-start(bf16[4,64,512]{2,1,0:T(8,128)(2,1)S(1)} %get-tuple-element.28), channel_id=1, source_target_pairs={{0,2},{2,0},{4,6},{6,4},{8,10},{10,8},{12,14},{14,12},{1,3},{3,1},... | collective-permute-start | bytes 786440 | tf_op jit(solution)/shard_map/ppermute | solution.py:270
  116.8 17.1 %collective-permute-start.9 = (bf16[800,512]{1,0:T(8,128)(2,1)S(1)}, bf16[800,512]{1,0:T(8,128)(2,1)S(1)}, u32[]{:S(2)}, u32[]{:S(2)}) collective-permute-start(bf16[800,512]{1,0:T(8,128)(2,1)S(1)} %add_convert_fusion.2), channel_id=1, source_target_pairs={{0,2},{2,0},{4,6},{6,4},{8,10},{10,8},{12,14},{14,12},{1,3},{3,1},... | collective-permute-start | bytes 2457608 | tf_op jit(solution)/shard_map/ppermute | solution.py:268
  119.5 1.7 copy-start.24
  121.8 20.4 %collective-permute-start.15 = (bf16[800,512]{1,0:T(8,128)(2,1)}, bf16[800,512]{1,0:T(8,128)(2,1)}, u32[]{:S(2)}, u32[]{:S(2)}) collective-permute-start(bf16[800,512]{1,0:T(8,128)(2,1)} %collective-permute-done.12), channel_id=1, source_target_pairs={{8,12},{10,14},{9,13},{11,15},{24,28},{26,30},{25,29},{27,31}} | collective-permute-start | bytes 2457608 | tf_op jit(solution)/shard_map/ppermute | solution.py:176
  123.4 18.8 %collective-permute-start.16 = (bf16[800,512]{1,0:T(8,128)(2,1)}, bf16[800,512]{1,0:T(8,128)(2,1)}, u32[]{:S(2)}, u32[]{:S(2)}) collective-permute-start(bf16[800,512]{1,0:T(8,128)(2,1)} %collective-permute-done.14), channel_id=1, source_target_pairs={{4,0},{6,2},{5,1},{7,3},{20,16},{22,18},{21,17},{23,19}} | collective-permute-start | bytes 2457608 | tf_op jit(solution)/shard_map/ppermute | solution.py:176
  125.5 9.9 %copy-start.7 = (bf16[800,256]{1,0:T(8,128)(2,1)S(1)}, bf16[800,256]{1,0:T(8,128)(2,1)}, u32[]{:S(2)}) copy-start(bf16[800,256]{1,0:T(8,128)(2,1)} %copy-done.6) | copy-start | bytes 1228804
  125.5 9.9 %copy-start.10 = (bf16[800,256]{1,0:T(8,128)(2,1)S(1)}, bf16[800,256]{1,0:T(8,128)(2,1)}, u32[]{:S(2)}) copy-start(bf16[800,256]{1,0:T(8,128)(2,1)} %copy-done.9) | copy-start | bytes 1228804
  135.5 2.3 %copy-start.17 = (bf16[800,512]{1,0:T(8,128)(2,1)}, bf16[800,512]{1,0:T(8,128)(2,1)S(1)}, u32[]{:S(2)}) copy-start(bf16[800,512]{1,0:T(8,128)(2,1)S(1)} %get-tuple-element.26) | copy-start | bytes 2457604
  137.7 37.9 %all-to-all-start = ((bf16[8,64,1024]{2,1,0:T(8,128)(2,1)}), bf16[8,64,1024]{2,1,0:T(8,128)(2,1)}, u32[]{:S(2)}, u32[]{:S(2)}) async-start(bf16[8,64,1024]{2,1,0:T(8,128)(2,1)} %bitcast.90), calls=%async_computation | async-start | bytes 2097152 | tf_op jit(solution)/shard_map/all_to_all | solution.py:210
  142.2 2.9 %copy-start.8 = (bf16[800,256]{1,0:T(8,128)(2,1)S(1)}, bf16[800,256]{1,0:T(8,128)(2,1)}, u32[]{:S(2)}) copy-start(bf16[800,256]{1,0:T(8,128)(2,1)} %copy-done.6) | copy-start | bytes 1228804
  142.2 2.9 %copy-start.11 = (bf16[800,256]{1,0:T(8,128)(2,1)S(1)}, bf16[800,256]{1,0:T(8,128)(2,1)}, u32[]{:S(2)}) copy-start(bf16[800,256]{1,0:T(8,128)(2,1)} %copy-done.9) | copy-start | bytes 1228804
  152.7 4.7 %copy-start.25 = (bf16[800,1600]{1,0:T(8,128)(2,1)S(1)}, bf16[800,1600]{1,0:T(8,128)(2,1)}, u32[]{:S(2)}) copy-start(bf16[800,1600]{1,0:T(8,128)(2,1)} %copy-done.24) | copy-start | bytes 7680004
  152.7 20.1 %collective-permute-start.17 = (bf16[800,512]{1,0:T(8,128)(2,1)S(1)}, bf16[800,512]{1,0:T(8,128)(2,1)S(1)}, u32[]{:S(2)}, u32[]{:S(2)}) collective-permute-start(bf16[800,512]{1,0:T(8,128)(2,1)S(1)} %add_convert_fusion), channel_id=1, source_target_pairs={{0,2},{2,0},{4,6},{6,4},{8,10},{10,8},{12,14},{14,12},{1,3},{3,1},... | collective-permute-start | bytes 2457608 | tf_op jit(solution)/shard_map/ppermute | solution.py:297
  157.4 15.4 %copy-start.12 = (bf16[4,2,64,512]{3,2,1,0:T(8,128)(2,1)S(1)}, bf16[4,2,64,512]{3,2,1,0:T(8,128)(2,1)}, u32[]{:S(2)}) copy-start(bf16[4,2,64,512]{3,2,1,0:T(8,128)(2,1)} %maximum_select_fusion) | copy-start | bytes 1572868
  157.4 15.4 %copy-start.18 = (bf16[800,512]{1,0:T(8,128)(2,1)S(1)}, bf16[800,512]{1,0:T(8,128)(2,1)}, u32[]{:S(2)}) copy-start(bf16[800,512]{1,0:T(8,128)(2,1)} %copy-done.17) | copy-start | bytes 2457604
  174.3 2.7 %copy-start.3 = (f32[1,512,512]{2,1,0:T(8,128)S(1)}, f32[1,512,512]{2,1,0:T(8,128)}, u32[]{:S(2)}) copy-start(f32[1,512,512]{2,1,0:T(8,128)} %param.10) | copy-start | bytes 3145732
  177.1 1.4 copy-start.14
  177.1 1.4 copy-start.19
  177.8 1.4 copy-start.20
  178.9 5.1 %copy-start.15 = (f32[1,800,256]{2,1,0:T(8,128)S(1)}, f32[1,800,256]{2,1,0:T(8,128)}, u32[]{:S(2)}) copy-start(f32[1,800,256]{2,1,0:T(8,128)} %get-tuple-element.34) | copy-start | bytes 2457604
  179.9 12.3 %all-to-all-start.1 = ((bf16[8,32,512]{2,1,0:T(8,128)(2,1)}), bf16[8,32,512]{2,1,0:T(8,128)(2,1)S(1)}, u32[]{:S(2)}, u32[]{:S(2)}) async-start(bf16[8,32,512]{2,1,0:T(8,128)(2,1)} %pad_maximum_fusion.8), calls=%async_computation.1 | async-start | bytes 524288 | tf_op jit(solution)/shard_map/all_to_all | solution.py:210
